TPU v7x, 32 devices: a whole 2x2x4 slice. The times are simulated.
32 devices in a mesh: dp: 8 (over y, x, core), mp: 4 (over z).
Axes of the slice: x: 2, y: 2, z: 4, core: 2. Of those that a mesh axis runs over, the one named last changes fastest.
Arguments:
- queries: bfloat16 [128, 2048], P('dp', 'mp'), may hold values from -160 to 160
- prefix_pool: bfloat16 [48, 2, 2, 128, 128], P('dp'), may hold values from -6 to 6
- slot_offset: int32 [48], P('dp'), may hold values from 0 to 5, as said below
- suffix_kv: bfloat16 [128, 2, 2, 48, 128], P('dp'), may hold values from -7.1875 to 7.1875
- out_weight: bfloat16 [2048, 8192], P('mp'), may hold values from -0.125 to 0.125
Outputs:
- block_out: bfloat16 [128, 8192], P('dp')
Inputs may be any that keep to these rules, and one draw needn't show every extreme that they name: `slot_offset`: on every index of dp, among its 6 blocks no value occurs more than 2 times and some value occurs exactly 2 times. One document gets at most 12 blocks, and in every draw some document gets that many.
All inputs are finite; a program needn't handle non-finite values.
Results may differ from a plain program's by a relative error of at most 0.023.
Values may be sent and summed in bfloat16 or wider, within the bound.
No kernel may reach another device: no remote copies, remote signals or barrier semaphores. Data moves between devices by JAX's collectives and lax.ppermute only.
A program may use at most 64 MiB of HBM per device.

v0:
```python
import jax
import jax.numpy as jnp
from jax import lax
from jax.sharding import PartitionSpec as P

GQA = 8
BLK = 128
SPREAD = 6
CAPACITY = 2


NEG = -1e30


def passed_along(block, axis, distance):
    devices = range(lax.axis_size(axis))
    route = [((i - distance) % len(devices), i) for i in devices]
    return lax.ppermute(block, axis, route)


def packed_slots(slot_offset, lagged, capacity):
    chosen = slot_offset == lagged
    order_in_lag = jnp.cumsum(chosen.astype(jnp.int32)) - 1
    positions = jnp.arange(slot_offset.shape[0], dtype=jnp.int32)
    index_list = []
    live_list = []
    for position in range(capacity):
        matched = chosen & (order_in_lag == position)
        index_list.append(jnp.sum(jnp.where(matched, positions, 0)))
        live_list.append(jnp.any(matched))
    return (jnp.stack(index_list), jnp.stack(live_list).astype(jnp.int32))


def row_scores(query_rows, key_rows, score_scale):
    product = lax.dot_general(
        query_rows, key_rows, (((1,), (1,)), ((), ())), preferred_element_type=jnp.float32
    )
    return product * score_scale


def local(queries, prefix_pool, slot_offset, suffix_kv, out_weight):
    head_dim = prefix_pool.shape[-1]
    samples = queries.shape[0]
    local_heads = queries.shape[1] // head_dim
    kv_index = lax.axis_index("mp") * local_heads // GQA
    pool_head = lax.dynamic_index_in_dim(prefix_pool, kv_index, 1, keepdims=False)
    suffix_head = lax.dynamic_index_in_dim(suffix_kv, kv_index, 1, keepdims=False)
    score_scale = head_dim ** (-0.5)
    query_heads = queries.reshape(samples, local_heads, head_dim)
    flat_query = queries.reshape(samples * local_heads, head_dim)
    suffix_scores = (
        jnp.einsum(
            "shd,std->sht", query_heads, suffix_head[:, 0], preferred_element_type=jnp.float32
        )
        * score_scale
    )
    block_list = []
    flag_list = []
    for lagged in range(SPREAD):
        slot_index, slot_live = packed_slots(slot_offset, lagged, CAPACITY)
        outgoing = jnp.take(pool_head, slot_index, axis=0)
        if lagged > 0:
            outgoing, slot_live = passed_along((outgoing, slot_live), "dp", lagged)
        block_list.append(outgoing)
        flag_list.append(slot_live)
    gathered = jnp.stack(block_list)
    key_rows = gathered[:, :, 0].reshape(-1, head_dim)
    value_rows = gathered[:, :, 1].reshape(-1, head_dim)
    live_rows = jnp.repeat(jnp.stack(flag_list).reshape(-1), BLK) > 0
    prefix_scores = row_scores(flat_query, key_rows, score_scale)
    prefix_scores = jnp.where(live_rows[None, :], prefix_scores, NEG).reshape(
        samples, local_heads, -1
    )
    row_peak = jnp.maximum(prefix_scores.max(-1), suffix_scores.max(-1))
    prefix_weight = jnp.exp(prefix_scores - row_peak[..., None])
    suffix_weight = jnp.exp(suffix_scores - row_peak[..., None])
    denominator = prefix_weight.sum(-1) + suffix_weight.sum(-1)
    weight_rows = prefix_weight.astype(jnp.bfloat16).reshape(samples * local_heads, -1)
    accumulated = jnp.dot(weight_rows, value_rows, preferred_element_type=jnp.float32).reshape(
        samples, local_heads, head_dim
    )
    accumulated = accumulated + jnp.einsum(
        "sht,std->shd",
        suffix_weight.astype(jnp.bfloat16),
        suffix_head[:, 1],
        preferred_element_type=jnp.float32,
    )
    attended = (
        (accumulated / denominator[..., None])
        .astype(jnp.bfloat16)
        .reshape(samples, local_heads * head_dim)
    )
    partial_out = jnp.dot(attended, out_weight, preferred_element_type=jnp.float32)
    return lax.psum(partial_out.astype(jnp.bfloat16), "mp")


def solution(mesh):
    placed = (
        P("dp", "mp"),
        P("dp", None, None, None, None),
        P("dp"),
        P("dp", None, None, None, None),
        P("mp", None),
    )
    return jax.shard_map(
        local, mesh=mesh, in_specs=placed, out_specs=P("dp", None), check_vma=False
    )
```

profile of v0, /device:TPU:0, one launch (start us, length us, event | category | flops | bytes accessed | tf_op | source)
XLA Modules:
  0.0 117.6 jit_solution(5643050547206987988)
XLA Ops:
  6.5 0.7 convert_bitcast_fusion
  8.4 1.6 %fusion.16 = (pred[]{:T(512)}, pred[6]{0:T(512)(128)(4,1)S(1)}, pred[]{:T(512)}, pred[6]{0:T(512)(128)(4,1)S(1)}, pred[]{:T(512)}, /*index=5*/pred[6]{0:T(512)(1...) fusion(s32[6,1]{0,1:T(1,128)S(1)} %reduce-window.59, ...), kind=kLoop, calls=%fused_computation.105 | loop fusion | flops 276 | bytes 252 | tf_op jit(solution)/shard_map/reduce_or | solution.py:30
  9.9 0.6 select_reduce_fusion.11
  10.5 0.7 select_reduce_fusion.10
  11.2 0.7 select_reduce_fusion.9
  11.9 0.7 select_reduce_fusion.8
  12.5 2.5 %compare_and_fusion.4 = (pred[2]{0:T(512)(128)(4,1)S(1)}, s32[2]{0:T(128)S(1)}, pred[2]{0:T(512)(128)(4,1)S(1)}, s32[2]{0:T(128)S(1)}) fusion(s32[1]{0:T(128)} %bitcast.41, s32[1]{0:T(128)} %bitcast.40, s32[1]{0:T(128)} %bitcast.37, s32[1]{0:T(128)} %bitcast.36), kind=kLoop, calls=%fused_computation.77 | loop fusion | flops 28 | bytes 36 | tf_op jit(solution)/shard_map/jit(_take)/and | solution.py:61
  15.1 0.6 gather_fusion.1
  15.8 0.5 collective-permute-start.5
  16.3 0.6 select_reduce_fusion.7
  16.9 0.7 select_reduce_fusion.6
  17.6 0.7 select_reduce_fusion.5
  18.3 0.7 select_reduce_fusion.4
  19.0 2.5 %compare_and_fusion.2 = (pred[2]{0:T(512)(128)(4,1)S(1)}, s32[2]{0:T(128)S(1)}, pred[2]{0:T(512)(128)(4,1)S(1)}, s32[2]{0:T(128)S(1)}) fusion(s32[1]{0:T(128)} %bitcast.47, s32[1]{0:T(128)} %bitcast.46, s32[1]{0:T(128)} %bitcast.44, s32[1]{0:T(128)} %bitcast.43), kind=kLoop, calls=%fused_computation.75 | loop fusion | flops 28 | bytes 36 | tf_op jit(solution)/shard_map/jit(_take)/and | solution.py:61
  21.5 0.6 gather_fusion.2
  22.2 2.6 %collective-permute-start.6 = (bf16[2,2,128,128]{3,2,1,0:T(8,128)(2,1)S(1)}, bf16[2,2,128,128]{3,2,1,0:T(8,128)(2,1)S(1)}, u32[]{:S(2)}, u32[]{:S(2)}) collective-permute-start(bf16[2,2,128,128]{3,2,1,0:T(8,128)(2,1)S(1)} %broadcast_select_fusion.3), channel_id=1, source_target_pairs={{24,0},{28,4},{0,8},{4,12},{8,16},{12,20},{16,24},{20,28},{25,1},{... | collective-permute-start | bytes 393224 | tf_op jit(solution)/shard_map/ppermute | solution.py:18
  24.7 0.6 gather_fusion.3
  25.4 2.5 %collective-permute-start.7 = (bf16[2,2,128,128]{3,2,1,0:T(8,128)(2,1)S(1)}, bf16[2,2,128,128]{3,2,1,0:T(8,128)(2,1)S(1)}, u32[]{:S(2)}, u32[]{:S(2)}) collective-permute-start(bf16[2,2,128,128]{3,2,1,0:T(8,128)(2,1)S(1)} %broadcast_select_fusion.2), channel_id=1, source_target_pairs={{20,0},{24,4},{28,8},{0,12},{4,16},{8,20},{12,24},{16,28},{21,1},{... | collective-permute-start | bytes 393224 | tf_op jit(solution)/shard_map/ppermute | solution.py:18
  27.8 0.6 select_reduce_fusion.3
  28.5 0.7 select_reduce_fusion.2
  29.1 0.7 select_reduce_fusion.1
  29.8 0.7 select_reduce_fusion
  30.5 2.5 %compare_and_fusion = (pred[2]{0:T(512)(128)(4,1)S(1)}, s32[2]{0:T(128)S(1)}, pred[2]{0:T(512)(128)(4,1)S(1)}, s32[2]{0:T(128)S(1)}) fusion(s32[1]{0:T(128)} %bitcast.53, s32[1]{0:T(128)} %bitcast.52, s32[1]{0:T(128)} %bitcast.50, s32[1]{0:T(128)} %bitcast.49), kind=kLoop, calls=%fused_computation.73 | loop fusion | flops 28 | bytes 36 | tf_op jit(solution)/shard_map/jit(_take)/and | solution.py:61
  33.0 0.6 gather_fusion.4
  33.7 0.6 collective-permute-start.8
  34.3 1.3 %add_convert_fusion.1 = s32[2]{0:T(128)S(1)} fusion(pred[1]{0:T(512)(128)(4,1)} %bitcast.9, pred[1]{0:T(512)(128)(4,1)} %bitcast.7), kind=kLoop, calls=%fused_computation.56 | loop fusion | flops 4 | bytes 10 | tf_op jit(solution)/shard_map/convert_element_type | solution.py:31
  35.6 0.7 reshape.275
  36.3 0.7 reshape.276
  37.1 0.6 gather_fusion
  37.7 0.6 gather_fusion.5
  38.2 1.0 copy_bitcast_fusion
  39.8 1.2 %add_convert_fusion.2 = s32[2]{0:T(128)S(1)} fusion(pred[1]{0:T(512)(128)(4,1)} %bitcast.15, pred[1]{0:T(512)(128)(4,1)} %bitcast.13), kind=kLoop, calls=%fused_computation.57 | loop fusion | flops 4 | bytes 10 | tf_op jit(solution)/shard_map/convert_element_type | solution.py:31
  41.1 1.3 %add_convert_fusion.3 = s32[2]{0:T(128)S(1)} fusion(pred[1]{0:T(512)(128)(4,1)} %bitcast.21, pred[1]{0:T(512)(128)(4,1)} %bitcast.19), kind=kLoop, calls=%fused_computation.58 | loop fusion | flops 4 | bytes 10 | tf_op jit(solution)/shard_map/convert_element_type | solution.py:31
  42.4 1.3 %add_convert_fusion.4 = s32[2]{0:T(128)S(1)} fusion(pred[1]{0:T(512)(128)(4,1)} %bitcast.27, pred[1]{0:T(512)(128)(4,1)} %bitcast.25), kind=kLoop, calls=%fused_computation.59 | loop fusion | flops 4 | bytes 10 | tf_op jit(solution)/shard_map/convert_element_type | solution.py:31
  43.7 1.4 %add_convert_fusion.5 = s32[2]{0:T(128)S(1)} fusion(pred[1]{0:T(512)(128)(4,1)} %bitcast.33, pred[1]{0:T(512)(128)(4,1)} %bitcast.31), kind=kLoop, calls=%fused_computation.60 | loop fusion | flops 4 | bytes 10 | tf_op jit(solution)/shard_map/convert_element_type | solution.py:31
  45.1 1.3 %add_convert_fusion = s32[1,2]{0,1:T(2,128)S(1)} fusion(pred[1,1]{0,1:T(4,128)(4,1)} %bitcast.4, pred[1,1]{0,1:T(4,128)(4,1)} %bitcast.2), kind=kLoop, calls=%fused_computation.55 | loop fusion | flops 4 | bytes 10 | tf_op jit(solution)/shard_map/convert_element_type | solution.py:31
  46.4 1.5 %collective-permute-start.1 = (s32[2]{0:T(128)S(1)}, s32[2]{0:T(128)S(1)}, u32[]{:S(2)}, u32[]{:S(2)}) collective-permute-start(s32[2]{0:T(128)S(1)} %add_convert_fusion.2), channel_id=1, source_target_pairs={{24,0},{28,4},{0,8},{4,12},{8,16},{12,20},{16,24},{20,28},{25,1},{... | collective-permute-start | bytes 32 | tf_op jit(solution)/shard_map/ppermute | solution.py:18
  48.1 2.9 %collective-permute-done.1 = s32[2]{0:T(128)S(1)} collective-permute-done((s32[2]{0:T(128)S(1)}, s32[2]{0:T(128)S(1)}, u32[]{:S(2)}, u32[]{:S(2)}) %collective-permute-start.1) | collective-permute-done | bytes 40 | tf_op jit(solution)/shard_map/ppermute | solution.py:18
  50.9 0.6 collective-permute-start.2
  51.6 2.2 %collective-permute-done.2 = s32[2]{0:T(128)S(1)} collective-permute-done((s32[2]{0:T(128)S(1)}, s32[2]{0:T(128)S(1)}, u32[]{:S(2)}, u32[]{:S(2)}) %collective-permute-start.2) | collective-permute-done | bytes 40 | tf_op jit(solution)/shard_map/ppermute | solution.py:18
  53.9 1.5 %collective-permute-start.3 = (s32[2]{0:T(128)S(1)}, s32[2]{0:T(128)S(1)}, u32[]{:S(2)}, u32[]{:S(2)}) collective-permute-start(s32[2]{0:T(128)S(1)} %add_convert_fusion.4), channel_id=1, source_target_pairs={{16,0},{20,4},{24,8},{28,12},{0,16},{4,20},{8,24},{12,28},{17,1},{... | collective-permute-start | bytes 32 | tf_op jit(solution)/shard_map/ppermute | solution.py:18
  55.5 1.9 %collective-permute-done.3 = s32[2]{0:T(128)S(1)} collective-permute-done((s32[2]{0:T(128)S(1)}, s32[2]{0:T(128)S(1)}, u32[]{:S(2)}, u32[]{:S(2)}) %collective-permute-start.3) | collective-permute-done | bytes 40 | tf_op jit(solution)/shard_map/ppermute | solution.py:18
  57.7 2.7 %collective-permute-done.4 = s32[2]{0:T(128)S(1)} collective-permute-done((s32[2]{0:T(128)S(1)}, s32[2]{0:T(128)S(1)}, u32[]{:S(2)}, u32[]{:S(2)}) %collective-permute-start.4) | collective-permute-done | bytes 40 | tf_op jit(solution)/shard_map/ppermute | solution.py:18
  61.2 3.6 %collective-permute-done.9 = bf16[2,2,128,128]{3,2,1,0:T(8,128)(2,1)S(1)} collective-permute-done((bf16[2,2,128,128]{3,2,1,0:T(8,128)(2,1)S(1)}, bf16[2,2,128,128]{3,2,1,0:T(8,128)(2,1)S(1)}, u32[]{:S(2)}, u32[]{:S(2)}) %collective-permute-start.9) | collective-permute-done | bytes 131104 | tf_op jit(solution)/shard_map/ppermute | solution.py:18
  64.9 0.4 fusion.29
  66.4 5.3 %convolution_convert_fusion = bf16[16,8192]{1,0:T(8,128)(2,1)} fusion(bf16[512,8192]{1,0:T(8,128)(2,1)} %param.11, bf16[4,2,8,128]{3,2,1,0:T(8,128)(2,1)S(1)} %fusion.4), kind=kOutput, calls=%fused_computation.6 | convolution fusion | flops 134348800 | bytes 8667136 | tf_op jit(solution)/shard_map/dot_general | solution.py:93
  71.8 37.3 %all-reduce.2.cloned.1.call-done = bf16[16,8192]{1,0:T(8,128)(2,1)} async-done(((bf16[16,8192]{1,0:T(8,128)(2,1)}), bf16[16,8192]{1,0:T(8,128)(2,1)}) %all-reduce.2.cloned.1.call-update) | async-done | bytes 262160 | tf_op jit(solution)/shard_map/psum | solution.py:94
  109.1 1.7 %copy.41 = bf16[16,8192]{1,0:T(8,128)(2,1)} copy(bf16[16,8192]{1,0:T(8,128)(2,1)} %all-reduce.2.cloned.1.call-done) | data formatting | bytes 524288
  (60 shorter events, 4.5 us)
Async XLA Ops:
  6.5 8.6 %copy-start = (bf16[6,2,2,128,128]{4,3,2,1,0:T(8,128)(2,1)S(1)}, bf16[6,2,2,128,128]{4,3,2,1,0:T(8,128)(2,1)}, u32[]{:S(2)}) copy-start(bf16[6,2,2,128,128]{4,3,2,1,0:T(8,128)(2,1)} %param.8) | copy-start | bytes 2359300
  6.5 102.6 %all-reduce.2.cloned.1.call-start = ((), (), s32[]{:S(2)}) async-start(), calls=%async_computation | async-start | bytes 524288 | tf_op jit(solution)/shard_map/psum | solution.py:94
  15.8 45.2 %collective-permute-start.5 = (bf16[2,2,128,128]{3,2,1,0:T(8,128)(2,1)S(1)}, bf16[2,2,128,128]{3,2,1,0:T(8,128)(2,1)S(1)}, u32[]{:S(2)}, u32[]{:S(2)}) collective-permute-start(bf16[2,2,128,128]{3,2,1,0:T(8,128)(2,1)S(1)} %broadcast_select_fusion.4), channel_id=1, source_target_pairs={{28,0},{0,4},{4,8},{8,12},{12,16},{16,20},{20,24},{24,28},{29,1},{... | collective-permute-start | bytes 393224 | tf_op jit(solution)/shard_map/ppermute | solution.py:18
  22.2 38.9 %collective-permute-start.6 = (bf16[2,2,128,128]{3,2,1,0:T(8,128)(2,1)S(1)}, bf16[2,2,128,128]{3,2,1,0:T(8,128)(2,1)S(1)}, u32[]{:S(2)}, u32[]{:S(2)}) collective-permute-start(bf16[2,2,128,128]{3,2,1,0:T(8,128)(2,1)S(1)} %broadcast_select_fusion.3), channel_id=1, source_target_pairs={{24,0},{28,4},{0,8},{4,12},{8,16},{12,20},{16,24},{20,28},{25,1},{... | collective-permute-start | bytes 393224 | tf_op jit(solution)/shard_map/ppermute | solution.py:18
  25.4 35.7 %collective-permute-start.7 = (bf16[2,2,128,128]{3,2,1,0:T(8,128)(2,1)S(1)}, bf16[2,2,128,128]{3,2,1,0:T(8,128)(2,1)S(1)}, u32[]{:S(2)}, u32[]{:S(2)}) collective-permute-start(bf16[2,2,128,128]{3,2,1,0:T(8,128)(2,1)S(1)} %broadcast_select_fusion.2), channel_id=1, source_target_pairs={{20,0},{24,4},{28,8},{0,12},{4,16},{8,20},{12,24},{16,28},{21,1},{... | collective-permute-start | bytes 393224 | tf_op jit(solution)/shard_map/ppermute | solution.py:18
  33.7 27.4 %collective-permute-start.8 = (bf16[2,2,128,128]{3,2,1,0:T(8,128)(2,1)S(1)}, bf16[2,2,128,128]{3,2,1,0:T(8,128)(2,1)S(1)}, u32[]{:S(2)}, u32[]{:S(2)}) collective-permute-start(bf16[2,2,128,128]{3,2,1,0:T(8,128)(2,1)S(1)} %broadcast_select_fusion.1), channel_id=1, source_target_pairs={{16,0},{20,4},{24,8},{28,12},{0,16},{4,20},{8,24},{12,28},{17,1},{... | collective-permute-start | bytes 393224 | tf_op jit(solution)/shard_map/ppermute | solution.py:18
  35.6 10.8 %collective-permute-start = (s32[2]{0:T(128)S(1)}, s32[2]{0:T(128)S(1)}, u32[]{:S(2)}, u32[]{:S(2)}) collective-permute-start(s32[2]{0:T(128)S(1)} %add_convert_fusion.1), channel_id=1, source_target_pairs={{28,0},{0,4},{4,8},{8,12},{12,16},{16,20},{20,24},{24,28},{29,1},{... | collective-permute-start | bytes 32 | tf_op jit(solution)/shard_map/ppermute | solution.py:18
  46.4 4.5 %collective-permute-start.1 = (s32[2]{0:T(128)S(1)}, s32[2]{0:T(128)S(1)}, u32[]{:S(2)}, u32[]{:S(2)}) collective-permute-start(s32[2]{0:T(128)S(1)} %add_convert_fusion.2), channel_id=1, source_target_pairs={{24,0},{28,4},{0,8},{4,12},{8,16},{12,20},{16,24},{20,28},{25,1},{... | collective-permute-start | bytes 32 | tf_op jit(solution)/shard_map/ppermute | solution.py:18
  50.9 3.0 %collective-permute-start.2 = (s32[2]{0:T(128)S(1)}, s32[2]{0:T(128)S(1)}, u32[]{:S(2)}, u32[]{:S(2)}) collective-permute-start(s32[2]{0:T(128)S(1)} %add_convert_fusion.3), channel_id=1, source_target_pairs={{20,0},{24,4},{28,8},{0,12},{4,16},{8,20},{12,24},{16,28},{21,1},{... | collective-permute-start | bytes 32 | tf_op jit(solution)/shard_map/ppermute | solution.py:18
  53.9 3.5 %collective-permute-start.3 = (s32[2]{0:T(128)S(1)}, s32[2]{0:T(128)S(1)}, u32[]{:S(2)}, u32[]{:S(2)}) collective-permute-start(s32[2]{0:T(128)S(1)} %add_convert_fusion.4), channel_id=1, source_target_pairs={{16,0},{20,4},{24,8},{28,12},{0,16},{4,20},{8,24},{12,28},{17,1},{... | collective-permute-start | bytes 32 | tf_op jit(solution)/shard_map/ppermute | solution.py:18
  57.4 3.0 %collective-permute-start.4 = (s32[2]{0:T(128)S(1)}, s32[2]{0:T(128)S(1)}, u32[]{:S(2)}, u32[]{:S(2)}) collective-permute-start(s32[2]{0:T(128)S(1)} %add_convert_fusion.5), channel_id=1, source_target_pairs={{12,0},{16,4},{20,8},{24,12},{28,16},{0,20},{4,24},{8,28},{13,1},{... | collective-permute-start | bytes 32 | tf_op jit(solution)/shard_map/ppermute | solution.py:18
  60.4 4.4 %collective-permute-start.9 = (bf16[2,2,128,128]{3,2,1,0:T(8,128)(2,1)S(1)}, bf16[2,2,128,128]{3,2,1,0:T(8,128)(2,1)S(1)}, u32[]{:S(2)}, u32[]{:S(2)}) collective-permute-start(bf16[2,2,128,128]{3,2,1,0:T(8,128)(2,1)S(1)} %broadcast_select_fusion), channel_id=1, source_target_pairs={{12,0},{16,4},{20,8},{24,12},{28,16},{0,20},{4,24},{8,28},{13,1},{... | collective-permute-start | bytes 393224 | tf_op jit(solution)/shard_map/ppermute | solution.py:18
Sparse Core Ops, SparseCore 0:
  71.9 37.1 all-reduce.1
where the time goes:
time: 118 us
  waiting for transfers between devices  50.7 us (43%)
  other arithmetic  27.7 us (23%)
  between operations  13.7 us (12%)
  starting transfers between devices  10.1 us (9%)
  local copies, waits for them, and re-layouts  9.05 us (8%)
  matrix products  6.35 us (5%)
    psum x1, waiting for transfers between devices, local(): return lax.psum(partial_out.astype(jnp.bfloat16), 'mp')  37.3 us
    ppermute x10, waiting for transfers between devices, passed_along(): return lax.ppermute(block, axis, route)  13.4 us
    ppermute x10, starting transfers between devices, passed_along(): return lax.ppermute(block, axis, route)  10.1 us
    reduce_sum x12, other arithmetic, packed_slots(): index_list.append(jnp.sum(jnp.where(matched, positions, 0)))  7.92 us
    convert_element_type x6, other arithmetic, packed_slots(): return (jnp.stack(index_list), jnp.stack(live_list).astype(jnp.int32))  7.87 us
    and x3, other arithmetic, local(): outgoing = jnp.take(pool_head, slot_index, axis=0)  7.58 us
    dot_general x1, matrix products, local(): jnp.dot(attended, out_weight, preferred_element_type=jnp.float32)  5.29 us
    gather x6, local copies, waits for them, and re-layouts, local(): outgoing = jnp.take(pool_head, slot_index, axis=0)  3.44 us
  transfers between devices with their start and end apart: 11, of which 6 were waited for; matrix products, arithmetic and copies ran while one was open for 22% of the time, Pallas kernels for 0%

commit v1 on v0

v1 whole, which is shorter than its diff:
```python
import functools

import jax
import jax.numpy as jnp
from jax import lax
from jax.experimental import pallas as pl
from jax.experimental.pallas import tpu as pltpu
from jax.sharding import PartitionSpec as P

GQA = 8
SPREAD = 6
CAPACITY = 2
CHUNKS = 4
NEG = -(2.0**100)

VMEM_SPEC = pl.BlockSpec(memory_space=pltpu.VMEM)
SMEM_SPEC = pl.BlockSpec(memory_space=pltpu.SMEM)
PARAMS = pltpu.CompilerParams(vmem_limit_bytes=16 * 1024 * 1024)


def shifted(block, distance):
    size = lax.axis_size("dp")
    return lax.ppermute(block, "dp", [(i, (i + distance) % size) for i in range(size)])


def head_rows(block, head_dim):
    heads = block.shape[1] // head_dim
    return jnp.concatenate([block[:, h * head_dim : (h + 1) * head_dim] for h in range(heads)], axis=0)


def dot_nt(a, b):
    return lax.dot_general(a, b, (((1,), (1,)), ((), ())), preferred_element_type=jnp.float32)


def slots_of(offset_ref, lag):
    first = jnp.int32(0)
    second = jnp.int32(0)
    count = jnp.int32(0)
    for b in range(offset_ref.shape[0]):
        hit = offset_ref[b] == lag
        second = jnp.where(hit & (count == 1), b, second)
        first = jnp.where(hit & (count == 0), b, first)
        count = count + hit.astype(jnp.int32)
    return first, second, count


def block_pair(pool_ref, offset_ref, kv, lag):
    first, second, count = slots_of(offset_ref, lag)
    keys = jnp.concatenate([pool_ref[first, kv, 0], pool_ref[second, kv, 0]], axis=0)
    values = jnp.concatenate([pool_ref[first, kv, 1], pool_ref[second, kv, 1]], axis=0)
    return keys, values, count


def live_scores(rows, keys, count, scale):
    scores = dot_nt(rows, keys) * scale
    block = keys.shape[0] // CAPACITY
    position = lax.broadcasted_iota(jnp.int32, scores.shape, 1)
    return jnp.where(position < count * block, scores, NEG)


def own_kernel(local_heads, offset_ref, query_ref, pool_ref, suffix_ref, acc_ref, peak_ref, total_ref):
    kv = lax.axis_index("mp") * local_heads // GQA
    samples, _, _, length, head_dim = suffix_ref.shape
    scale = head_dim ** (-0.5)
    rows = head_rows(query_ref[...], head_dim)
    suffix_keys = suffix_ref[:, kv, 0].reshape(samples * length, head_dim)
    suffix_values = suffix_ref[:, kv, 1].reshape(samples * length, head_dim)
    suffix_scores = dot_nt(rows, suffix_keys) * scale
    row_sample = lax.broadcasted_iota(jnp.int32, suffix_scores.shape, 0) % samples
    key_at = lax.broadcasted_iota(jnp.int32, suffix_scores.shape, 1)
    mine = (key_at >= row_sample * length) & (key_at < (row_sample + 1) * length)
    suffix_scores = jnp.where(mine, suffix_scores, NEG)
    keys, values, count = block_pair(pool_ref, offset_ref, kv, 0)
    scores = live_scores(rows, keys, count, scale)
    peak = jnp.maximum(
        jnp.max(suffix_scores, axis=1, keepdims=True), jnp.max(scores, axis=1, keepdims=True)
    )
    suffix_weight = jnp.exp(suffix_scores - peak)
    weight = jnp.exp(scores - peak)
    total = jnp.sum(suffix_weight, axis=1, keepdims=True) + jnp.sum(weight, axis=1, keepdims=True)
    acc_ref[...] = jnp.dot(
        suffix_weight.astype(jnp.bfloat16), suffix_values, preferred_element_type=jnp.float32
    ) + jnp.dot(weight.astype(jnp.bfloat16), values, preferred_element_type=jnp.float32)
    peak_ref[...] = jnp.broadcast_to(peak, peak_ref.shape)
    total_ref[...] = jnp.broadcast_to(total, total_ref.shape)


def lag_kernel(local_heads, offset_ref, pool_ref, *refs):
    kv = lax.axis_index("mp") * local_heads // GQA
    query_refs, out_refs = refs[: SPREAD - 1], refs[SPREAD - 1 :]
    head_dim = pool_ref.shape[-1]
    scale = head_dim ** (-0.5)
    for lag in range(1, SPREAD):
        rows = head_rows(query_refs[lag - 1][...], head_dim)
        keys, values, count = block_pair(pool_ref, offset_ref, kv, lag)
        scores = live_scores(rows, keys, count, scale)
        peak = jnp.max(scores, axis=1, keepdims=True).astype(jnp.bfloat16)
        weight = jnp.exp(scores - peak.astype(jnp.float32))
        total = jnp.sum(weight, axis=1, keepdims=True).astype(jnp.bfloat16)
        acc = jnp.dot(weight.astype(jnp.bfloat16), values, preferred_element_type=jnp.float32)
        half = (rows.shape[0], head_dim // 2)
        out_refs[lag - 1][:, :head_dim] = acc.astype(jnp.bfloat16)
        out_refs[lag - 1][:, head_dim:] = jnp.concatenate(
            [jnp.broadcast_to(peak, half), jnp.broadcast_to(total, half)], axis=1
        )


def merge_kernel(acc_ref, peak_ref, total_ref, *refs):
    parts, out_ref = refs[:-1], refs[-1]
    rows, head_dim = acc_ref.shape
    samples = out_ref.shape[0]
    middle = head_dim + head_dim // 2
    accs = [acc_ref[...]]
    peaks = [peak_ref[...][:, :1]]
    totals = [total_ref[...][:, :1]]
    for part in parts:
        whole = part[...].astype(jnp.float32)
        accs.append(whole[:, :head_dim])
        peaks.append(whole[:, head_dim : head_dim + 1])
        totals.append(whole[:, middle : middle + 1])
    top = functools.reduce(jnp.maximum, peaks)
    shares = [jnp.exp(peak - top) for peak in peaks]
    total = sum(share * t for share, t in zip(shares, totals))
    acc = sum(share * a for share, a in zip(shares, accs))
    attended = (acc / total).astype(jnp.bfloat16)
    out_ref[...] = jnp.concatenate(
        [attended[h * samples : (h + 1) * samples] for h in range(rows // samples)], axis=1
    )


def project_kernel(start, attended_ref, weight_ref, out_ref):
    width = out_ref.shape[1]
    out_ref[...] = jnp.dot(
        attended_ref[...], weight_ref[:, start : start + width], preferred_element_type=jnp.float32
    ).astype(jnp.bfloat16)


def add(a, b):
    return (a.astype(jnp.float32) + b.astype(jnp.float32)).astype(jnp.bfloat16)


def summed_over_mp(attended, weight):
    size = lax.axis_size("mp")
    samples, width = attended.shape[0], weight.shape[1] // CHUNKS
    chunks = []
    for c in range(CHUNKS):
        chunks.append(
            pl.pallas_call(
                functools.partial(project_kernel, c * width),
                out_shape=jax.ShapeDtypeStruct((samples, width), jnp.bfloat16),
                in_specs=[VMEM_SPEC, VMEM_SPEC],
                out_specs=VMEM_SPEC,
                compiler_params=PARAMS,
                cost_estimate=pl.CostEstimate(
                    flops=2 * samples * weight.shape[0] * width,
                    bytes_accessed=2 * weight.shape[0] * width,
                    transcendentals=0,
                ),
            )(attended, weight)
        )
    if size & (size - 1):
        return jnp.concatenate([lax.psum(chunk, "mp") for chunk in chunks], axis=1)
    step = 1
    while step < size:
        route = [(i, i ^ step) for i in range(size)]
        chunks = [add(chunk, lax.ppermute(chunk, "mp", route)) for chunk in chunks]
        step *= 2
    return jnp.concatenate(chunks, axis=1)


def local(queries, prefix_pool, slot_offset, suffix_kv, out_weight):
    samples, _, _, length, head_dim = suffix_kv.shape
    local_heads = queries.shape[1] // head_dim
    rows = samples * local_heads
    f32, bf16 = jnp.float32, jnp.bfloat16
    asked = [shifted(queries, -lag) for lag in range(1, SPREAD)]
    acc, peak, total = pl.pallas_call(
        functools.partial(own_kernel, local_heads),
        out_shape=(jax.ShapeDtypeStruct((rows, head_dim), f32),) * 3,
        in_specs=[SMEM_SPEC] + [VMEM_SPEC] * 3,
        out_specs=(VMEM_SPEC,) * 3,
        compiler_params=PARAMS,
        cost_estimate=pl.CostEstimate(
            flops=4 * rows * samples * length * head_dim,
            bytes_accessed=2 * suffix_kv.size,
            transcendentals=rows * samples * length,
        ),
    )(slot_offset, queries, prefix_pool, suffix_kv)
    answers = pl.pallas_call(
        functools.partial(lag_kernel, local_heads),
        out_shape=(jax.ShapeDtypeStruct((rows, 2 * head_dim), bf16),) * (SPREAD - 1),
        in_specs=[SMEM_SPEC, VMEM_SPEC] + [VMEM_SPEC] * (SPREAD - 1),
        out_specs=(VMEM_SPEC,) * (SPREAD - 1),
        compiler_params=PARAMS,
    )(slot_offset, prefix_pool, *asked)
    parts = [shifted(answers[lag - 1], lag) for lag in range(1, SPREAD)]
    attended = pl.pallas_call(
        merge_kernel,
        out_shape=jax.ShapeDtypeStruct(queries.shape, bf16),
        in_specs=[VMEM_SPEC] * (3 + SPREAD - 1),
        out_specs=VMEM_SPEC,
        compiler_params=PARAMS,
    )(acc, peak, total, *parts)
    return summed_over_mp(attended, out_weight)


def solution(mesh):
    placed = (
        P("dp", "mp"),
        P("dp", None, None, None, None),
        P("dp"),
        P("dp", None, None, None, None),
        P("mp", None),
    )
    return jax.shard_map(
        local, mesh=mesh, in_specs=placed, out_specs=P("dp", None), check_vma=False
    )
```

time: 118 us -> 48.1 us (0.41)
  waiting for transfers between devices: 50.7 us -> 11.4 us
  other arithmetic: 27.7 us -> 0.87 us
  between operations: 13.7 us -> 0.12 us
  starting transfers between devices: 10.1 us -> 22.6 us
  matrix products: 6.35 us -> 0 us
  Pallas kernels: 0 us -> 4.58 us
    psum x1 -> x0, waiting for transfers between devices: 37.3 us -> none  [local(): return lax.psum(partial_out.astype(jnp.bfloat16), 'mp')]
    ppermute x10 -> x18, starting transfers between devices: 10.1 us -> 22.6 us  [the longest x10 11.4 us: shifted(): lax.ppermute(block, 'dp', [(i, (i + distance) % size) for i in range(size)])]
    reduce_sum x14 -> x0, other arithmetic: 8.34 us -> none  [the longest x12 7.92 us: packed_slots(): index_list.append(jnp.sum(jnp.where(matched, positions, 0)))]
    convert_element_type x6 -> x8, other arithmetic: 7.87 us -> 0.15 us  [add(): return (a.astype(jnp.float32) + b.astype(jnp.float32)).astype(jnp.bfloat16)]
    and x3 -> x0, other arithmetic: 7.58 us -> none  [local(): outgoing = jnp.take(pool_head, slot_index, axis=0)]
    unnamed x7 -> x12, local copies, waits for them, and re-layouts: 1.75 us -> 8.15 us
    dot_general x5 -> x0, matrix products: 6.35 us -> none  [the longest x1 5.29 us: local(): jnp.dot(attended, out_weight, preferred_element_type=jnp.float32)]
    pallas_call x0 -> x7, Pallas kernels: none -> 4.58 us  [the longest x1 1.89 us: local(): pl.pallas_call(functools.partial(lag_kernel, local_heads), out_shape=(jax...]
  transfers between devices with their start and end apart: 11 -> 18, of which waited for: 6 -> 7; matrix products, arithmetic and copies ran while one was open for 22% -> 0% of each run, Pallas kernels for 0% -> 4%
where the time goes in v1:
time: 48.1 us; the launch traced here: 47.7 us
  starting transfers between devices  22.6 us (47%)
  waiting for transfers between devices  11.4 us (24%)
  local copies, waits for them, and re-layouts  8.15 us (17%)
  Pallas kernels  4.58 us (10%)
  other arithmetic  0.87 us (2%)
    ppermute x10, starting transfers between devices, shifted(): lax.ppermute(block, 'dp', [(i, (i + distance) % size) for i in range(size)])  11.4 us
    ppermute x8, starting transfers between devices, summed_over_mp(): chunks = [add(chunk, lax.ppermute(chunk, 'mp', route)) for chunk in chunks]  11.2 us
    ppermute x8, waiting for transfers between devices, summed_over_mp(): chunks = [add(chunk, lax.ppermute(chunk, 'mp', route)) for chunk in chunks]  8.95 us
    unnamed x12, local copies, waits for them, and re-layouts  8.15 us
    ppermute x10, waiting for transfers between devices, shifted(): lax.ppermute(block, 'dp', [(i, (i + distance) % size) for i in range(size)])  2.47 us
    pallas_call x1, Pallas kernels, local(): pl.pallas_call(functools.partial(lag_kernel, local_heads), out_shape=(jax...  1.89 us
    pallas_call x4, Pallas kernels, summed_over_mp(): pl.pallas_call(functools.partial(project_kernel, c * width), out_shape=ja...  1.49 us
    pallas_call x1, Pallas kernels, local(): pl.pallas_call(functools.partial(own_kernel, local_heads), out_shape=(jax...  1.03 us
  transfers between devices with their start and end apart: 18, of which 7 were waited for; matrix products, arithmetic and copies ran while one was open for 0% of the time, Pallas kernels for 4%

profile of v1, /device:TPU:0, one launch (start us, length us, event | category | flops | bytes accessed | tf_op | source)
XLA Modules:
  0.0 47.7 jit_solution(10363256902205819172)
XLA Ops:
  0.0 2.4 %collective-permute-start.2 = (bf16[16,512]{1,0:T(8,128)(2,1)}, bf16[16,512]{1,0:T(8,128)(2,1)S(1)}, u32[]{:S(2)}, u32[]{:S(2)}) collective-permute-start(bf16[16,512]{1,0:T(8,128)(2,1)} %query_ref.1), channel_id=1, source_target_pairs={{0,20},{4,24},{8,28},{12,0},{16,4},{20,8},{24,12},{28,16},{1,21},{... | collective-permute-start | bytes 49160 | tf_op jit(solution)/shard_map/ppermute | solution.py:23
  2.4 1.5 %collective-permute-start.1 = (bf16[16,512]{1,0:T(8,128)(2,1)}, bf16[16,512]{1,0:T(8,128)(2,1)S(1)}, u32[]{:S(2)}, u32[]{:S(2)}) collective-permute-start(bf16[16,512]{1,0:T(8,128)(2,1)} %query_ref.1), channel_id=1, source_target_pairs={{0,24},{4,28},{8,0},{12,4},{16,8},{20,12},{24,16},{28,20},{1,25},{... | collective-permute-start | bytes 49160 | tf_op jit(solution)/shard_map/ppermute | solution.py:23
  3.9 1.4 %collective-permute-start = (bf16[16,512]{1,0:T(8,128)(2,1)}, bf16[16,512]{1,0:T(8,128)(2,1)S(1)}, u32[]{:S(2)}, u32[]{:S(2)}) collective-permute-start(bf16[16,512]{1,0:T(8,128)(2,1)} %query_ref.1), channel_id=1, source_target_pairs={{0,28},{4,0},{8,4},{12,8},{16,12},{20,16},{24,20},{28,24},{1,29},{... | collective-permute-start | bytes 49160 | tf_op jit(solution)/shard_map/ppermute | solution.py:23
  5.3 0.1 collective-permute-start.4
  5.4 1.5 %collective-permute-start.3 = (bf16[16,512]{1,0:T(8,128)(2,1)}, bf16[16,512]{1,0:T(8,128)(2,1)S(1)}, u32[]{:S(2)}, u32[]{:S(2)}) collective-permute-start(bf16[16,512]{1,0:T(8,128)(2,1)} %query_ref.1), channel_id=1, source_target_pairs={{0,16},{4,20},{8,24},{12,28},{16,0},{20,4},{24,8},{28,12},{1,17},{... | collective-permute-start | bytes 49160 | tf_op jit(solution)/shard_map/ppermute | solution.py:23
  6.9 0.0 collective-permute-done.2.refs_2_
  6.9 0.0 collective-permute-done.1.refs_1_
  6.9 0.1 collective-permute-done.refs_0_
  7.0 1.7 %collective-permute-done.4.refs_4_ = bf16[16,512]{1,0:T(8,128)(2,1)S(1)} collective-permute-done((bf16[16,512]{1,0:T(8,128)(2,1)}, bf16[16,512]{1,0:T(8,128)(2,1)S(1)}, u32[]{:S(2)}, u32[]{:S(2)}) %collective-permute-start.4) | collective-permute-done | bytes 16416 | tf_op jit(solution)/shard_map/ppermute | solution.py:23
  8.7 0.6 %collective-permute-done.3.refs_3_ = bf16[16,512]{1,0:T(8,128)(2,1)S(1)} collective-permute-done((bf16[16,512]{1,0:T(8,128)(2,1)}, bf16[16,512]{1,0:T(8,128)(2,1)S(1)}, u32[]{:S(2)}, u32[]{:S(2)}) %collective-permute-start.3) | collective-permute-done | bytes 16416 | tf_op jit(solution)/shard_map/ppermute | solution.py:23
  9.3 1.1 %copy-done.1 = bf16[6,2,2,128,128]{4,3,2,1,0:T(8,128)(2,1)S(1)} copy-done((bf16[6,2,2,128,128]{4,3,2,1,0:T(8,128)(2,1)S(1)}, bf16[6,2,2,128,128]{4,3,2,1,0:T(8,128)(2,1)}, u32[]{:S(2)}) %copy-start.1) | copy-done | bytes 786456
  10.5 0.7 %copy-done.5 = s32[6]{0:T(128)S(1)} copy-done((s32[6]{0:T(128)S(1)}, s32[6]{0:T(128)}, u32[]{:S(2)}) %copy-start.5) | copy-done | bytes 48
  11.1 1.9 %shard_map.56 = (bf16[64,256]{1,0:T(8,128)(2,1)S(1)}, bf16[64,256]{1,0:T(8,128)(2,1)S(1)}, bf16[64,256]{1,0:T(8,128)(2,1)S(1)}, bf16[64,256]{1,0:T(8,128)(2,1)S(1)}, bf16[64,256]{1,0:T(8,128)(2,1)S(1)}) custom-call(s32[6]{0:T(128)S(1)} %copy-done.5, bf16[6,2,2,128,128]{4,3,2,1,0:T(8,128)(2,1)S(1)} %copy-done.1, ...), custom_call_target="tpu_custom_call" | custom-call | tf_op jit(solution)/shard_map/pallas_call | solution.py:189
  13.0 0.5 %collective-permute-start.5 = (bf16[64,256]{1,0:T(8,128)(2,1)S(1)}, bf16[64,256]{1,0:T(8,128)(2,1)S(1)}, u32[]{:S(2)}, u32[]{:S(2)}) collective-permute-start(bf16[64,256]{1,0:T(8,128)(2,1)S(1)} %get-tuple-element.16), channel_id=1, source_target_pairs={{0,4},{4,8},{8,12},{12,16},{16,20},{20,24},{24,28},{28,0},{1,5},{5... | collective-permute-start | bytes 98312 | tf_op jit(solution)/shard_map/ppermute | solution.py:23
  13.5 1.2 %collective-permute-start.6 = (bf16[64,256]{1,0:T(8,128)(2,1)S(1)}, bf16[64,256]{1,0:T(8,128)(2,1)S(1)}, u32[]{:S(2)}, u32[]{:S(2)}) collective-permute-start(bf16[64,256]{1,0:T(8,128)(2,1)S(1)} %get-tuple-element.17), channel_id=1, source_target_pairs={{0,8},{4,12},{8,16},{12,20},{16,24},{20,28},{24,0},{28,4},{1,9},{5... | collective-permute-start | bytes 98312 | tf_op jit(solution)/shard_map/ppermute | solution.py:23
  14.7 1.4 %collective-permute-start.7 = (bf16[64,256]{1,0:T(8,128)(2,1)S(1)}, bf16[64,256]{1,0:T(8,128)(2,1)S(1)}, u32[]{:S(2)}, u32[]{:S(2)}) collective-permute-start(bf16[64,256]{1,0:T(8,128)(2,1)S(1)} %get-tuple-element.18), channel_id=1, source_target_pairs={{0,12},{4,16},{8,20},{12,24},{16,28},{20,0},{24,4},{28,8},{1,13},{... | collective-permute-start | bytes 98312 | tf_op jit(solution)/shard_map/ppermute | solution.py:23
  16.1 1.4 %collective-permute-start.8 = (bf16[64,256]{1,0:T(8,128)(2,1)S(1)}, bf16[64,256]{1,0:T(8,128)(2,1)S(1)}, u32[]{:S(2)}, u32[]{:S(2)}) collective-permute-start(bf16[64,256]{1,0:T(8,128)(2,1)S(1)} %get-tuple-element.19), channel_id=1, source_target_pairs={{0,16},{4,20},{8,24},{12,28},{16,0},{20,4},{24,8},{28,12},{1,17},{... | collective-permute-start | bytes 98312 | tf_op jit(solution)/shard_map/ppermute | solution.py:23
  17.6 0.0 collective-permute-start.9
  17.6 1.1 %copy-done.2 = bf16[6,2,2,128,128]{4,3,2,1,0:T(8,128)(2,1)S(1)} copy-done((bf16[6,2,2,128,128]{4,3,2,1,0:T(8,128)(2,1)S(1)}, bf16[6,2,2,128,128]{4,3,2,1,0:T(8,128)(2,1)}, u32[]{:S(2)}) %copy-start.2) | copy-done | bytes 786456
  18.7 1.1 %copy-done.3 = bf16[16,2,2,48,128]{4,3,2,1,0:T(8,128)(2,1)S(1)} copy-done((bf16[16,2,2,48,128]{4,3,2,1,0:T(8,128)(2,1)S(1)}, bf16[16,2,2,48,128]{4,3,2,1,0:T(8,128)(2,1)}, u32[]{:S(2)}) %copy-start.3) | copy-done | bytes 786456
  19.8 0.7 %copy-done.4 = bf16[16,512]{1,0:T(8,128)(2,1)S(1)} copy-done((bf16[16,512]{1,0:T(8,128)(2,1)S(1)}, bf16[16,512]{1,0:T(8,128)(2,1)}, u32[]{:S(2)}) %copy-start.4) | copy-done | bytes 16408
  20.5 1.0 %shard_map.55 = (f32[64,128]{1,0:T(8,128)S(1)}, f32[64,128]{1,0:T(8,128)S(1)}, f32[64,128]{1,0:T(8,128)S(1)}) custom-call(s32[6]{0:T(128)S(1)} %copy-done.5, bf16[16,512]{1,0:T(8,128)(2,1)S(1)} %copy-done.4, bf16[6,2,2,128,128]{4,3,2,1,0:T(8,128)(2,1)S(1)} %copy-done.2, bf16[16,2,2,48,128]{4,3,2,1,0:T(8,128)(2,1)S(1)} %copy-done.3), custom_call_target="tpu_custom_call" | custom-call | flops 25165824 | bytes 786432 | tf_op jit(solution)/shard_map/pallas_call | solution.py:177
  21.6 0.0 collective-permute-done.5.refs_0_
  21.6 0.0 collective-permute-done.6.refs_1_
  21.6 0.0 collective-permute-done.7.refs_2_
  21.6 0.0 collective-permute-done.8.refs_3_
  21.6 0.0 collective-permute-done.9.refs_4_
  21.6 0.2 shard_map.57.attended_ref
  21.8 0.0 copy-start
  21.8 3.4 %copy-done = bf16[512,8192]{1,0:T(8,128)(2,1)S(1)} copy-done((bf16[512,8192]{1,0:T(8,128)(2,1)S(1)}, bf16[512,8192]{1,0:T(8,128)(2,1)}, u32[]{:S(2)}) %copy-start) | copy-done | bytes 8388632
  25.2 0.4 shard_map.58
  25.6 1.6 %collective-permute-start.10 = (bf16[16,2048]{1,0:T(8,128)(2,1)S(1)}, bf16[16,2048]{1,0:T(8,128)(2,1)S(1)}, u32[]{:S(2)}, u32[]{:S(2)}) collective-permute-start(bf16[16,2048]{1,0:T(8,128)(2,1)S(1)} %shard_map.58), channel_id=1, source_target_pairs={{0,1},{1,0},{2,3},{3,2},{4,5},{5,4},{6,7},{7,6},{8,9},{9,8},{10,11... | collective-permute-start | bytes 196616 | tf_op jit(solution)/shard_map/ppermute | solution.py:166
  27.2 0.4 shard_map.59
  27.5 0.5 collective-permute-start.12
  28.0 0.4 shard_map.60
  28.4 1.6 %collective-permute-start.14 = (bf16[16,2048]{1,0:T(8,128)(2,1)S(1)}, bf16[16,2048]{1,0:T(8,128)(2,1)S(1)}, u32[]{:S(2)}, u32[]{:S(2)}) collective-permute-start(bf16[16,2048]{1,0:T(8,128)(2,1)S(1)} %shard_map.60), channel_id=1, source_target_pairs={{0,1},{1,0},{2,3},{3,2},{4,5},{5,4},{6,7},{7,6},{8,9},{9,8},{10,11... | collective-permute-start | bytes 196616 | tf_op jit(solution)/shard_map/ppermute | solution.py:166
  30.0 0.4 shard_map.61
  30.3 0.5 collective-permute-start.16
  30.8 2.7 %collective-permute-start.11 = (bf16[16,2048]{1,0:T(8,128)(2,1)S(1)}, bf16[16,2048]{1,0:T(8,128)(2,1)S(1)}, u32[]{:S(2)}, u32[]{:S(2)}) collective-permute-start(bf16[16,2048]{1,0:T(8,128)(2,1)S(1)} %add_convert_fusion.7), channel_id=1, source_target_pairs={{0,2},{1,3},{2,0},{3,1},{4,6},{5,7},{6,4},{7,5},{8,10},{9,11},{10,... | collective-permute-start | bytes 196616 | tf_op jit(solution)/shard_map/ppermute | solution.py:166
  33.5 1.5 %collective-permute-start.13 = (bf16[16,2048]{1,0:T(8,128)(2,1)S(1)}, bf16[16,2048]{1,0:T(8,128)(2,1)S(1)}, u32[]{:S(2)}, u32[]{:S(2)}) collective-permute-start(bf16[16,2048]{1,0:T(8,128)(2,1)S(1)} %add_convert_fusion.5), channel_id=1, source_target_pairs={{0,2},{1,3},{2,0},{3,1},{4,6},{5,7},{6,4},{7,5},{8,10},{9,11},{10,... | collective-permute-start | bytes 196616 | tf_op jit(solution)/shard_map/ppermute | solution.py:166
  35.0 1.6 %collective-permute-start.15 = (bf16[16,2048]{1,0:T(8,128)(2,1)S(1)}, bf16[16,2048]{1,0:T(8,128)(2,1)S(1)}, u32[]{:S(2)}, u32[]{:S(2)}) collective-permute-start(bf16[16,2048]{1,0:T(8,128)(2,1)S(1)} %add_convert_fusion.3), channel_id=1, source_target_pairs={{0,2},{1,3},{2,0},{3,1},{4,6},{5,7},{6,4},{7,5},{8,10},{9,11},{10,... | collective-permute-start | bytes 196616 | tf_op jit(solution)/shard_map/ppermute | solution.py:166
  36.6 0.1 collective-permute-done.16
  36.8 1.3 %collective-permute-start.17 = (bf16[16,2048]{1,0:T(8,128)(2,1)S(1)}, bf16[16,2048]{1,0:T(8,128)(2,1)S(1)}, u32[]{:S(2)}, u32[]{:S(2)}) collective-permute-start(bf16[16,2048]{1,0:T(8,128)(2,1)S(1)} %add_convert_fusion.1), channel_id=1, source_target_pairs={{0,2},{1,3},{2,0},{3,1},{4,6},{5,7},{6,4},{7,5},{8,10},{9,11},{10,... | collective-permute-start | bytes 196616 | tf_op jit(solution)/shard_map/ppermute | solution.py:166
  38.1 0.0 collective-permute-done.11
  38.1 6.4 %collective-permute-done.13 = bf16[16,2048]{1,0:T(8,128)(2,1)S(1)} collective-permute-done((bf16[16,2048]{1,0:T(8,128)(2,1)S(1)}, bf16[16,2048]{1,0:T(8,128)(2,1)S(1)}, u32[]{:S(2)}, u32[]{:S(2)}) %collective-permute-start.13) | collective-permute-done | bytes 65568 | tf_op jit(solution)/shard_map/ppermute | solution.py:166
  44.5 1.4 %collective-permute-done.15 = bf16[16,2048]{1,0:T(8,128)(2,1)S(1)} collective-permute-done((bf16[16,2048]{1,0:T(8,128)(2,1)S(1)}, bf16[16,2048]{1,0:T(8,128)(2,1)S(1)}, u32[]{:S(2)}, u32[]{:S(2)}) %collective-permute-start.15) | collective-permute-done | bytes 65568 | tf_op jit(solution)/shard_map/ppermute | solution.py:166
  45.9 1.1 %collective-permute-done.17 = bf16[16,2048]{1,0:T(8,128)(2,1)S(1)} collective-permute-done((bf16[16,2048]{1,0:T(8,128)(2,1)S(1)}, bf16[16,2048]{1,0:T(8,128)(2,1)S(1)}, u32[]{:S(2)}, u32[]{:S(2)}) %collective-permute-start.17) | collective-permute-done | bytes 65568 | tf_op jit(solution)/shard_map/ppermute | solution.py:166
  47.0 0.7 %pad_maximum_fusion = bf16[16,8192]{1,0:T(8,128)(2,1)} fusion(bf16[16,2048]{1,0:T(8,128)(2,1)S(1)} %add_convert_fusion, bf16[16,2048]{1,0:T(8,128)(2,1)S(1)} %add_convert_fusion.2, bf16[16,2048]{1,0:T(8,128)(2,1)S(1)} %add_convert_fusion.4, bf16[16,2048]{1,0:T(8,128)(2,1)S(1)} %add_convert_fusion.6), kind=kLoop, calls=%fused_computation | loop fusion | flops 1048576 | bytes 524288 | tf_op jit(solution)/shard_map/concatenate | solution.py:168
  (16 shorter events, 0.2 us)
Async XLA Ops:
  0.0 6.9 %collective-permute-start.2 = (bf16[16,512]{1,0:T(8,128)(2,1)}, bf16[16,512]{1,0:T(8,128)(2,1)S(1)}, u32[]{:S(2)}, u32[]{:S(2)}) collective-permute-start(bf16[16,512]{1,0:T(8,128)(2,1)} %query_ref.1), channel_id=1, source_target_pairs={{0,20},{4,24},{8,28},{12,0},{16,4},{20,8},{24,12},{28,16},{1,21},{... | collective-permute-start | bytes 49160 | tf_op jit(solution)/shard_map/ppermute | solution.py:23
  2.4 4.5 %collective-permute-start.1 = (bf16[16,512]{1,0:T(8,128)(2,1)}, bf16[16,512]{1,0:T(8,128)(2,1)S(1)}, u32[]{:S(2)}, u32[]{:S(2)}) collective-permute-start(bf16[16,512]{1,0:T(8,128)(2,1)} %query_ref.1), channel_id=1, source_target_pairs={{0,24},{4,28},{8,0},{12,4},{16,8},{20,12},{24,16},{28,20},{1,25},{... | collective-permute-start | bytes 49160 | tf_op jit(solution)/shard_map/ppermute | solution.py:23
  3.9 3.0 %collective-permute-start = (bf16[16,512]{1,0:T(8,128)(2,1)}, bf16[16,512]{1,0:T(8,128)(2,1)S(1)}, u32[]{:S(2)}, u32[]{:S(2)}) collective-permute-start(bf16[16,512]{1,0:T(8,128)(2,1)} %query_ref.1), channel_id=1, source_target_pairs={{0,28},{4,0},{8,4},{12,8},{16,12},{20,16},{24,20},{28,24},{1,29},{... | collective-permute-start | bytes 49160 | tf_op jit(solution)/shard_map/ppermute | solution.py:23
  5.3 3.4 %collective-permute-start.4 = (bf16[16,512]{1,0:T(8,128)(2,1)}, bf16[16,512]{1,0:T(8,128)(2,1)S(1)}, u32[]{:S(2)}, u32[]{:S(2)}) collective-permute-start(bf16[16,512]{1,0:T(8,128)(2,1)} %query_ref.1), channel_id=1, source_target_pairs={{0,12},{4,16},{8,20},{12,24},{16,28},{20,0},{24,4},{28,8},{1,13},{... | collective-permute-start | bytes 49160 | tf_op jit(solution)/shard_map/ppermute | solution.py:23
  5.4 3.9 %collective-permute-start.3 = (bf16[16,512]{1,0:T(8,128)(2,1)}, bf16[16,512]{1,0:T(8,128)(2,1)S(1)}, u32[]{:S(2)}, u32[]{:S(2)}) collective-permute-start(bf16[16,512]{1,0:T(8,128)(2,1)} %query_ref.1), channel_id=1, source_target_pairs={{0,16},{4,20},{8,24},{12,28},{16,0},{20,4},{24,8},{28,12},{1,17},{... | collective-permute-start | bytes 49160 | tf_op jit(solution)/shard_map/ppermute | solution.py:23
  9.3 1.1 %copy-start.1 = (bf16[6,2,2,128,128]{4,3,2,1,0:T(8,128)(2,1)S(1)}, bf16[6,2,2,128,128]{4,3,2,1,0:T(8,128)(2,1)}, u32[]{:S(2)}) copy-start(bf16[6,2,2,128,128]{4,3,2,1,0:T(8,128)(2,1)} %pool_ref.3) | copy-start | bytes 2359300
  10.4 0.7 %copy-start.5 = (s32[6]{0:T(128)S(1)}, s32[6]{0:T(128)}, u32[]{:S(2)}) copy-start(s32[6]{0:T(128)} %offset_ref.3) | copy-start | bytes 76
  13.0 8.6 %collective-permute-start.5 = (bf16[64,256]{1,0:T(8,128)(2,1)S(1)}, bf16[64,256]{1,0:T(8,128)(2,1)S(1)}, u32[]{:S(2)}, u32[]{:S(2)}) collective-permute-start(bf16[64,256]{1,0:T(8,128)(2,1)S(1)} %get-tuple-element.16), channel_id=1, source_target_pairs={{0,4},{4,8},{8,12},{12,16},{16,20},{20,24},{24,28},{28,0},{1,5},{5... | collective-permute-start | bytes 98312 | tf_op jit(solution)/shard_map/ppermute | solution.py:23
  13.5 8.1 %collective-permute-start.6 = (bf16[64,256]{1,0:T(8,128)(2,1)S(1)}, bf16[64,256]{1,0:T(8,128)(2,1)S(1)}, u32[]{:S(2)}, u32[]{:S(2)}) collective-permute-start(bf16[64,256]{1,0:T(8,128)(2,1)S(1)} %get-tuple-element.17), channel_id=1, source_target_pairs={{0,8},{4,12},{8,16},{12,20},{16,24},{20,28},{24,0},{28,4},{1,9},{5... | collective-permute-start | bytes 98312 | tf_op jit(solution)/shard_map/ppermute | solution.py:23
  14.7 6.9 %collective-permute-start.7 = (bf16[64,256]{1,0:T(8,128)(2,1)S(1)}, bf16[64,256]{1,0:T(8,128)(2,1)S(1)}, u32[]{:S(2)}, u32[]{:S(2)}) collective-permute-start(bf16[64,256]{1,0:T(8,128)(2,1)S(1)} %get-tuple-element.18), channel_id=1, source_target_pairs={{0,12},{4,16},{8,20},{12,24},{16,28},{20,0},{24,4},{28,8},{1,13},{... | collective-permute-start | bytes 98312 | tf_op jit(solution)/shard_map/ppermute | solution.py:23
  16.1 5.5 %collective-permute-start.8 = (bf16[64,256]{1,0:T(8,128)(2,1)S(1)}, bf16[64,256]{1,0:T(8,128)(2,1)S(1)}, u32[]{:S(2)}, u32[]{:S(2)}) collective-permute-start(bf16[64,256]{1,0:T(8,128)(2,1)S(1)} %get-tuple-element.19), channel_id=1, source_target_pairs={{0,16},{4,20},{8,24},{12,28},{16,0},{20,4},{24,8},{28,12},{1,17},{... | collective-permute-start | bytes 98312 | tf_op jit(solution)/shard_map/ppermute | solution.py:23
  17.6 4.1 %collective-permute-start.9 = (bf16[64,256]{1,0:T(8,128)(2,1)S(1)}, bf16[64,256]{1,0:T(8,128)(2,1)S(1)}, u32[]{:S(2)}, u32[]{:S(2)}) collective-permute-start(bf16[64,256]{1,0:T(8,128)(2,1)S(1)} %get-tuple-element.20), channel_id=1, source_target_pairs={{0,20},{4,24},{8,28},{12,0},{16,4},{20,8},{24,12},{28,16},{1,21},{... | collective-permute-start | bytes 98312 | tf_op jit(solution)/shard_map/ppermute | solution.py:23
  17.6 1.1 %copy-start.2 = (bf16[6,2,2,128,128]{4,3,2,1,0:T(8,128)(2,1)S(1)}, bf16[6,2,2,128,128]{4,3,2,1,0:T(8,128)(2,1)}, u32[]{:S(2)}) copy-start(bf16[6,2,2,128,128]{4,3,2,1,0:T(8,128)(2,1)} %pool_ref.3) | copy-start | bytes 2359300
  18.7 1.1 %copy-start.3 = (bf16[16,2,2,48,128]{4,3,2,1,0:T(8,128)(2,1)S(1)}, bf16[16,2,2,48,128]{4,3,2,1,0:T(8,128)(2,1)}, u32[]{:S(2)}) copy-start(bf16[16,2,2,48,128]{4,3,2,1,0:T(8,128)(2,1)} %suffix_ref.1) | copy-start | bytes 2359300
  19.8 0.7 %copy-start.4 = (bf16[16,512]{1,0:T(8,128)(2,1)S(1)}, bf16[16,512]{1,0:T(8,128)(2,1)}, u32[]{:S(2)}) copy-start(bf16[16,512]{1,0:T(8,128)(2,1)} %query_ref.1) | copy-start | bytes 49156
  21.8 3.4 %copy-start = (bf16[512,8192]{1,0:T(8,128)(2,1)S(1)}, bf16[512,8192]{1,0:T(8,128)(2,1)}, u32[]{:S(2)}) copy-start(bf16[512,8192]{1,0:T(8,128)(2,1)} %weight_ref.7) | copy-start | bytes 25165828
  25.6 5.2 %collective-permute-start.10 = (bf16[16,2048]{1,0:T(8,128)(2,1)S(1)}, bf16[16,2048]{1,0:T(8,128)(2,1)S(1)}, u32[]{:S(2)}, u32[]{:S(2)}) collective-permute-start(bf16[16,2048]{1,0:T(8,128)(2,1)S(1)} %shard_map.58), channel_id=1, source_target_pairs={{0,1},{1,0},{2,3},{3,2},{4,5},{5,4},{6,7},{7,6},{8,9},{9,8},{10,11... | collective-permute-start | bytes 196616 | tf_op jit(solution)/shard_map/ppermute | solution.py:166
  27.5 6.0 %collective-permute-start.12 = (bf16[16,2048]{1,0:T(8,128)(2,1)S(1)}, bf16[16,2048]{1,0:T(8,128)(2,1)S(1)}, u32[]{:S(2)}, u32[]{:S(2)}) collective-permute-start(bf16[16,2048]{1,0:T(8,128)(2,1)S(1)} %shard_map.59), channel_id=1, source_target_pairs={{0,1},{1,0},{2,3},{3,2},{4,5},{5,4},{6,7},{7,6},{8,9},{9,8},{10,11... | collective-permute-start | bytes 196616 | tf_op jit(solution)/shard_map/ppermute | solution.py:166
  28.4 6.6 %collective-permute-start.14 = (bf16[16,2048]{1,0:T(8,128)(2,1)S(1)}, bf16[16,2048]{1,0:T(8,128)(2,1)S(1)}, u32[]{:S(2)}, u32[]{:S(2)}) collective-permute-start(bf16[16,2048]{1,0:T(8,128)(2,1)S(1)} %shard_map.60), channel_id=1, source_target_pairs={{0,1},{1,0},{2,3},{3,2},{4,5},{5,4},{6,7},{7,6},{8,9},{9,8},{10,11... | collective-permute-start | bytes 196616 | tf_op jit(solution)/shard_map/ppermute | solution.py:166
  30.3 6.4 %collective-permute-start.16 = (bf16[16,2048]{1,0:T(8,128)(2,1)S(1)}, bf16[16,2048]{1,0:T(8,128)(2,1)S(1)}, u32[]{:S(2)}, u32[]{:S(2)}) collective-permute-start(bf16[16,2048]{1,0:T(8,128)(2,1)S(1)} %shard_map.61), channel_id=1, source_target_pairs={{0,1},{1,0},{2,3},{3,2},{4,5},{5,4},{6,7},{7,6},{8,9},{9,8},{10,11... | collective-permute-start | bytes 196616 | tf_op jit(solution)/shard_map/ppermute | solution.py:166
  30.8 7.3 %collective-permute-start.11 = (bf16[16,2048]{1,0:T(8,128)(2,1)S(1)}, bf16[16,2048]{1,0:T(8,128)(2,1)S(1)}, u32[]{:S(2)}, u32[]{:S(2)}) collective-permute-start(bf16[16,2048]{1,0:T(8,128)(2,1)S(1)} %add_convert_fusion.7), channel_id=1, source_target_pairs={{0,2},{1,3},{2,0},{3,1},{4,6},{5,7},{6,4},{7,5},{8,10},{9,11},{10,... | collective-permute-start | bytes 196616 | tf_op jit(solution)/shard_map/ppermute | solution.py:166
  33.5 11.0 %collective-permute-start.13 = (bf16[16,2048]{1,0:T(8,128)(2,1)S(1)}, bf16[16,2048]{1,0:T(8,128)(2,1)S(1)}, u32[]{:S(2)}, u32[]{:S(2)}) collective-permute-start(bf16[16,2048]{1,0:T(8,128)(2,1)S(1)} %add_convert_fusion.5), channel_id=1, source_target_pairs={{0,2},{1,3},{2,0},{3,1},{4,6},{5,7},{6,4},{7,5},{8,10},{9,11},{10,... | collective-permute-start | bytes 196616 | tf_op jit(solution)/shard_map/ppermute | solution.py:166
  35.0 10.9 %collective-permute-start.15 = (bf16[16,2048]{1,0:T(8,128)(2,1)S(1)}, bf16[16,2048]{1,0:T(8,128)(2,1)S(1)}, u32[]{:S(2)}, u32[]{:S(2)}) collective-permute-start(bf16[16,2048]{1,0:T(8,128)(2,1)S(1)} %add_convert_fusion.3), channel_id=1, source_target_pairs={{0,2},{1,3},{2,0},{3,1},{4,6},{5,7},{6,4},{7,5},{8,10},{9,11},{10,... | collective-permute-start | bytes 196616 | tf_op jit(solution)/shard_map/ppermute | solution.py:166
  36.8 10.2 %collective-permute-start.17 = (bf16[16,2048]{1,0:T(8,128)(2,1)S(1)}, bf16[16,2048]{1,0:T(8,128)(2,1)S(1)}, u32[]{:S(2)}, u32[]{:S(2)}) collective-permute-start(bf16[16,2048]{1,0:T(8,128)(2,1)S(1)} %add_convert_fusion.1), channel_id=1, source_target_pairs={{0,2},{1,3},{2,0},{3,1},{4,6},{5,7},{6,4},{7,5},{8,10},{9,11},{10,... | collective-permute-start | bytes 196616 | tf_op jit(solution)/shard_map/ppermute | solution.py:166

commit v2 on v1

v2 whole, which is shorter than its diff:
```python
import functools

import jax
import jax.numpy as jnp
from jax import lax
from jax.experimental import pallas as pl
from jax.experimental.pallas import tpu as pltpu
from jax.sharding import PartitionSpec as P

GQA = 8
SPREAD = 6
CAPACITY = 2
CHUNKS = 4
GROUPS = ((3, 2, 1), (5, 4))
NEG = -(2.0**100)

VMEM_SPEC = pl.BlockSpec(memory_space=pltpu.VMEM)
HBM_SPEC = pl.BlockSpec(memory_space=pltpu.HBM)
PARAMS = pltpu.CompilerParams(vmem_limit_bytes=16 * 1024 * 1024)


def shifted(block, distance):
    size = lax.axis_size("dp")
    return lax.ppermute(block, "dp", [(i, (i + distance) % size) for i in range(size)])


def swapped(block, step):
    size = lax.axis_size("mp")
    return lax.ppermute(block, "mp", [(i, i ^ step) for i in range(size)])


def head_rows(block, head_dim):
    heads = block.shape[1] // head_dim
    return jnp.concatenate([block[:, h * head_dim : (h + 1) * head_dim] for h in range(heads)], axis=0)


def dot_nt(a, b):
    return lax.dot_general(a, b, (((1,), (1,)), ((), ())), preferred_element_type=jnp.float32)


def slots_of(offset_ref, lag):
    first = jnp.int32(0)
    second = jnp.int32(0)
    count = jnp.int32(0)
    for b in range(offset_ref.shape[0]):
        hit = offset_ref[b] == lag
        second = jnp.where(hit & (count == 1), b, second)
        first = jnp.where(hit & (count == 0), b, first)
        count = count + hit.astype(jnp.int32)
    return (first, second), count


def chunk_start(chunk, width):
    if chunk > 1:
        return chunk * width
    kept = lax.axis_index("mp") % 2
    return pl.multiple_of((kept if chunk == 1 else 1 - kept) * width, 128)


def weight_copy(weight_hbm, chunk, out_ref, sem):
    width = out_ref.shape[1]
    return pltpu.make_async_copy(
        weight_hbm.at[:, pl.ds(chunk_start(chunk, width), width)], out_ref, sem
    )


def own_kernel(local_heads, chunk, offset_hbm, query_hbm, pool_hbm, suffix_hbm, weight_hbm,
               acc_ref, peak_ref, total_ref, key_ref, value_ref, bias_ref, weight_ref,
               offset_ref, query_ref, suffix_ref, sems, slot_sems):
    kv = lax.axis_index("mp") * local_heads // GQA
    samples, _, length, head_dim = suffix_ref.shape
    block = key_ref.shape[1] // CAPACITY
    scale = head_dim ** (-0.5)
    offset_copy = pltpu.make_async_copy(offset_hbm, offset_ref, sems.at[0])
    query_copy = pltpu.make_async_copy(query_hbm, query_ref, sems.at[1])
    suffix_copy = pltpu.make_async_copy(suffix_hbm.at[:, kv], suffix_ref, sems.at[2])
    weight_load = weight_copy(weight_hbm, chunk, weight_ref, sems.at[3])
    offset_copy.start()
    query_copy.start()
    suffix_copy.start()
    weight_load.start()
    offset_copy.wait()
    slot_copies = []
    for lag in range(SPREAD):
        slots, count = slots_of(offset_ref, lag)
        for position, slot in enumerate(slots):
            place = pl.ds(position * block, block)
            for part, out_ref in enumerate((key_ref, value_ref)):
                copy = pltpu.make_async_copy(
                    pool_hbm.at[slot, kv, part], out_ref.at[lag, place], slot_sems.at[lag, position, part]
                )
                copy.start()
                slot_copies.append(copy)
        at = lax.broadcasted_iota(jnp.int32, bias_ref.shape[1:], 1)
        bias_ref[lag] = jnp.where(at < count * block, 0.0, NEG)
    query_copy.wait()
    rows = head_rows(query_ref[...], head_dim)
    suffix_copy.wait()
    suffix_keys = suffix_ref[:, 0].reshape(samples * length, head_dim)
    suffix_values = suffix_ref[:, 1].reshape(samples * length, head_dim)
    suffix_scores = dot_nt(rows, suffix_keys) * scale
    row_sample = lax.broadcasted_iota(jnp.int32, suffix_scores.shape, 0) % samples
    key_at = lax.broadcasted_iota(jnp.int32, suffix_scores.shape, 1)
    mine = (key_at >= row_sample * length) & (key_at < (row_sample + 1) * length)
    suffix_scores = jnp.where(mine, suffix_scores, NEG)
    for copy in slot_copies:
        copy.wait()
    scores = dot_nt(rows, key_ref[0]) * scale + bias_ref[0][:1]
    peak = jnp.maximum(
        jnp.max(suffix_scores, axis=1, keepdims=True), jnp.max(scores, axis=1, keepdims=True)
    )
    suffix_weight = jnp.exp(suffix_scores - peak)
    weight = jnp.exp(scores - peak)
    total = jnp.sum(suffix_weight, axis=1, keepdims=True) + jnp.sum(weight, axis=1, keepdims=True)
    acc_ref[...] = jnp.dot(
        suffix_weight.astype(jnp.bfloat16), suffix_values, preferred_element_type=jnp.float32
    ) + jnp.dot(weight.astype(jnp.bfloat16), value_ref[0], preferred_element_type=jnp.float32)
    peak_ref[...] = jnp.broadcast_to(peak, peak_ref.shape)
    total_ref[...] = jnp.broadcast_to(total, total_ref.shape)
    weight_load.wait()


def lag_kernel(lags, chunk, key_ref, value_ref, bias_ref, weight_hbm, *refs):
    query_refs = refs[: len(lags)]
    out_refs = refs[len(lags) : 2 * len(lags)]
    weight_ref, sem = refs[2 * len(lags) :]
    load = weight_copy(weight_hbm, chunk, weight_ref, sem)
    load.start()
    head_dim = key_ref.shape[-1]
    scale = head_dim ** (-0.5)
    for lag, query_ref, out_ref in zip(lags, query_refs, out_refs):
        rows = head_rows(query_ref[...], head_dim)
        scores = dot_nt(rows, key_ref[lag]) * scale + bias_ref[lag][:1]
        peak = jnp.max(scores, axis=1, keepdims=True).astype(jnp.bfloat16)
        weight = jnp.exp(scores - peak.astype(jnp.float32))
        total = jnp.sum(weight, axis=1, keepdims=True).astype(jnp.bfloat16)
        acc = jnp.dot(weight.astype(jnp.bfloat16), value_ref[lag], preferred_element_type=jnp.float32)
        half = (rows.shape[0], head_dim // 2)
        out_ref[:, :head_dim] = acc.astype(jnp.bfloat16)
        out_ref[:, head_dim:] = jnp.concatenate(
            [jnp.broadcast_to(peak, half), jnp.broadcast_to(total, half)], axis=1
        )
    load.wait()


def load_kernel(chunk, weight_hbm, after_hbm, weight_ref, sem):
    load = weight_copy(weight_hbm, chunk, weight_ref, sem)
    load.start()
    load.wait()


def merge_kernel(acc_ref, peak_ref, total_ref, *refs):
    parts, out_ref = refs[:-1], refs[-1]
    rows, head_dim = acc_ref.shape
    samples = out_ref.shape[0]
    middle = head_dim + head_dim // 2
    accs = [acc_ref[...]]
    peaks = [peak_ref[...][:, :1]]
    totals = [total_ref[...][:, :1]]
    for part in parts:
        whole = part[...].astype(jnp.float32)
        accs.append(whole[:, :head_dim])
        peaks.append(whole[:, head_dim : head_dim + 1])
        totals.append(whole[:, middle : middle + 1])
    top = functools.reduce(jnp.maximum, peaks)
    shares = [jnp.exp(peak - top) for peak in peaks]
    total = sum(share * t for share, t in zip(shares, totals))
    acc = sum(share * a for share, a in zip(shares, accs))
    attended = (acc / total).astype(jnp.bfloat16)
    out_ref[...] = jnp.concatenate(
        [attended[h * samples : (h + 1) * samples] for h in range(rows // samples)], axis=1
    )


def project_kernel(attended_ref, weight_ref, out_ref):
    out_ref[...] = jnp.dot(
        attended_ref[...], weight_ref[...], preferred_element_type=jnp.float32
    ).astype(jnp.bfloat16)


def project(attended, weight):
    depth, width = weight.shape
    return pl.pallas_call(
        project_kernel,
        out_shape=jax.ShapeDtypeStruct((attended.shape[0], width), jnp.bfloat16),
        in_specs=[VMEM_SPEC, VMEM_SPEC],
        out_specs=VMEM_SPEC,
        compiler_params=PARAMS,
        cost_estimate=pl.CostEstimate(
            flops=2 * attended.shape[0] * depth * width, bytes_accessed=2 * depth * width, transcendentals=0
        ),
    )(attended, weight)


def add(a, b):
    return (a.astype(jnp.float32) + b.astype(jnp.float32)).astype(jnp.bfloat16)


def final_kernel(kept_ref, other_ref, *refs):
    pairs, out_ref = refs[:-1], refs[-1]
    width = kept_ref.shape[1]
    out_ref[:, pl.ds(chunk_start(1, width), width)] = kept_ref[...]
    out_ref[:, pl.ds(chunk_start(0, width), width)] = other_ref[...]
    for i in range(len(pairs) // 2):
        out_ref[:, (2 + i) * width : (3 + i) * width] = add(pairs[2 * i][...], pairs[2 * i + 1][...])


def summed_over_four(attended, weights):
    sent = swapped(project(attended, weights[0]), 1)
    whole = [project(attended, weight) for weight in weights[2:]]
    whole_in = [swapped(chunk, 1) for chunk in whole]
    kept = add(project(attended, weights[1]), sent)
    kept_in = swapped(kept, 2)
    paired = [add(a, b) for a, b in zip(whole, whole_in)]
    paired_in = [swapped(chunk, 2) for chunk in paired]
    kept = add(kept, kept_in)
    other = swapped(kept, 1)
    tail = [x for pair in zip(paired, paired_in) for x in pair]
    samples, width = kept.shape
    return pl.pallas_call(
        final_kernel,
        out_shape=jax.ShapeDtypeStruct((samples, width * CHUNKS), jnp.bfloat16),
        in_specs=[VMEM_SPEC] * (2 + len(tail)),
        out_specs=VMEM_SPEC,
        compiler_params=PARAMS,
    )(kept, other, *tail)


def summed_over_any(attended, weights):
    first = lax.axis_index("mp") % 2 == 0
    chunks = [lax.psum(project(attended, weight), "mp") for weight in weights[2:]]
    ours = [project(attended, weight) for weight in weights[:2]]
    ours = [jnp.where(first, ours[1], ours[0]), jnp.where(first, ours[0], ours[1])]
    return jnp.concatenate([lax.psum(x, "mp") for x in ours] + chunks, axis=1)


def local(queries, prefix_pool, slot_offset, suffix_kv, out_weight):
    blocks, _, _, block, head_dim = prefix_pool.shape
    samples, _, _, length, _ = suffix_kv.shape
    local_heads = queries.shape[1] // head_dim
    rows = samples * local_heads
    depth, columns = out_weight.shape
    width = columns // CHUNKS
    f32, bf16 = jnp.float32, jnp.bfloat16
    in_hbm = [
        pltpu.with_memory_space_constraint(x, pltpu.HBM)
        for x in (slot_offset, queries, prefix_pool, suffix_kv, out_weight)
    ]
    chunk_shape = pltpu.VMEM((depth, width), bf16)
    gathered_shape = pltpu.VMEM((SPREAD, CAPACITY * block, head_dim), bf16)
    asked = {lag: shifted(queries, -lag) for group in GROUPS for lag in group}
    weights = [None] * CHUNKS
    acc, peak, total, keys, values, bias, weights[0] = pl.pallas_call(
        functools.partial(own_kernel, local_heads, 0),
        out_shape=(pltpu.VMEM((rows, head_dim), f32),) * 3
        + (gathered_shape, gathered_shape, pltpu.VMEM((SPREAD, 8, CAPACITY * block), f32), chunk_shape),
        in_specs=[HBM_SPEC] * 5,
        out_specs=(VMEM_SPEC,) * 7,
        scratch_shapes=[
            pltpu.SMEM(slot_offset.shape, jnp.int32),
            pltpu.VMEM(queries.shape, bf16),
            pltpu.VMEM((samples, 2, length, head_dim), bf16),
            pltpu.SemaphoreType.DMA((4,)),
            pltpu.SemaphoreType.DMA((SPREAD, CAPACITY, 2)),
        ],
        compiler_params=PARAMS,
        cost_estimate=pl.CostEstimate(
            flops=4 * rows * samples * length * head_dim,
            bytes_accessed=2 * suffix_kv.size + 2 * depth * width,
            transcendentals=rows * samples * length,
        ),
    )(*in_hbm)
    parts = {}
    for index, group in enumerate(GROUPS):
        out = pl.pallas_call(
            functools.partial(lag_kernel, group, 1 + index),
            out_shape=(jax.ShapeDtypeStruct((rows, 2 * head_dim), bf16),) * len(group) + (chunk_shape,),
            in_specs=[VMEM_SPEC] * 3 + [HBM_SPEC] + [VMEM_SPEC] * len(group),
            out_specs=(VMEM_SPEC,) * (len(group) + 1),
            scratch_shapes=[pltpu.SemaphoreType.DMA(())],
            compiler_params=PARAMS,
        )(keys, values, bias, in_hbm[-1], *[asked[lag] for lag in group])
        weights[1 + index] = out[-1]
        for lag, answer in zip(group, out):
            parts[lag] = shifted(answer, lag)
    last = out[0]
    weights[3] = pl.pallas_call(
        functools.partial(load_kernel, 3),
        out_shape=chunk_shape,
        in_specs=[HBM_SPEC, VMEM_SPEC],
        out_specs=VMEM_SPEC,
        scratch_shapes=[pltpu.SemaphoreType.DMA(())],
        compiler_params=PARAMS,
        cost_estimate=pl.CostEstimate(flops=0, bytes_accessed=2 * depth * width, transcendentals=0),
    )(in_hbm[-1], last)
    attended = pl.pallas_call(
        merge_kernel,
        out_shape=jax.ShapeDtypeStruct(queries.shape, bf16),
        in_specs=[VMEM_SPEC] * (3 + SPREAD - 1),
        out_specs=VMEM_SPEC,
        compiler_params=PARAMS,
    )(acc, peak, total, *[parts[lag] for lag in range(1, SPREAD)])
    if lax.axis_size("mp") == 4:
        return summed_over_four(attended, weights)
    return summed_over_any(attended, weights)


def solution(mesh):
    placed = (
        P("dp", "mp"),
        P("dp", None, None, None, None),
        P("dp"),
        P("dp", None, None, None, None),
        P("mp", None),
    )
    return jax.shard_map(
        local, mesh=mesh, in_specs=placed, out_specs=P("dp", None), check_vma=False
    )
```

time: 48.1 us -> 41.2 us (0.86)
  local copies, waits for them, and re-layouts: 8.15 us -> 0 us
  Pallas kernels: 4.58 us -> 10.6 us
  starting transfers between devices: 22.6 us -> 20.1 us
  waiting for transfers between devices: 11.4 us -> 10 us
  other arithmetic: 0.87 us -> 0.09 us
    unnamed x12 -> x0, local copies, waits for them, and re-layouts: 8.15 us -> none
    pallas_call x6 -> x9, Pallas kernels: 4.41 us -> 10.4 us  [the longest x2 3.96 us: local(): pl.pallas_call(functools.partial(lag_kernel, group, 1 + index), out_shape...]
    ppermute x8 -> x7, waiting for transfers between devices: 8.95 us -> 6.72 us  [swapped(): return lax.ppermute(block, 'mp', [(i, i ^ step) for i in range(size)])]
    ppermute x8 -> x7, starting transfers between devices: 11.2 us -> 9.5 us  [swapped(): return lax.ppermute(block, 'mp', [(i, i ^ step) for i in range(size)])]
    ppermute x10, waiting for transfers between devices: 2.47 us -> 3.32 us  [shifted(): lax.ppermute(block, 'dp', [(i, (i + distance) % size) for i in range(size)])]
    ppermute x10, starting transfers between devices: 11.4 us -> 10.6 us  [shifted(): lax.ppermute(block, 'dp', [(i, (i + distance) % size) for i in range(size)])]
    concatenate x1 -> x0, other arithmetic: 0.72 us -> none  [summed_over_mp(): return jnp.concatenate(chunks, axis=1)]
  transfers between devices with their start and end apart: 18 -> 17, of which waited for: 7 -> 5; matrix products, arithmetic and copies ran while one was open for 0% -> 0% of each run, Pallas kernels for 4% -> 23%
where the time goes in v2:
time: 41.2 us; the launch traced here: 40.9 us
  starting transfers between devices  20.1 us (49%)
  Pallas kernels  10.6 us (26%)
  waiting for transfers between devices  10 us (24%)
    ppermute x10, starting transfers between devices, shifted(): lax.ppermute(block, 'dp', [(i, (i + distance) % size) for i in range(size)])  10.6 us
    ppermute x7, starting transfers between devices, swapped(): return lax.ppermute(block, 'mp', [(i, i ^ step) for i in range(size)])  9.5 us
    ppermute x7, waiting for transfers between devices, swapped(): return lax.ppermute(block, 'mp', [(i, i ^ step) for i in range(size)])  6.72 us
    pallas_call x2, Pallas kernels, local(): pl.pallas_call(functools.partial(lag_kernel, group, 1 + index), out_shape...  3.96 us
    ppermute x10, waiting for transfers between devices, shifted(): lax.ppermute(block, 'dp', [(i, (i + distance) % size) for i in range(size)])  3.32 us
    pallas_call x1, Pallas kernels, local(): pl.pallas_call(functools.partial(own_kernel, local_heads, 0), out_shape=(...  2.63 us
    pallas_call x1, Pallas kernels, local(): pl.pallas_call(functools.partial(load_kernel, 3), out_shape=chunk_shape,...  1.6 us
    pallas_call x4, Pallas kernels, project(): pl.pallas_call(project_kernel, out_shape=jax.ShapeDtypeStruct((attended.s...  1.49 us
  transfers between devices with their start and end apart: 17, of which 5 were waited for; matrix products, arithmetic and copies ran while one was open for 0% of the time, Pallas kernels for 23%

profile of v2, /device:TPU:0, one launch (start us, length us, event | category | flops | bytes accessed | tf_op | source)
XLA Modules:
  0.0 40.9 jit_solution(7861224679159802407)
XLA Ops:
  0.0 2.4 %collective-permute-start = (bf16[16,512]{1,0:T(8,128)(2,1)}, bf16[16,512]{1,0:T(8,128)(2,1)S(1)}, u32[]{:S(2)}, u32[]{:S(2)}) collective-permute-start(bf16[16,512]{1,0:T(8,128)(2,1)} %query_hbm.1), channel_id=1, source_target_pairs={{0,20},{4,24},{8,28},{12,0},{16,4},{20,8},{24,12},{28,16},{1,21},{... | collective-permute-start | bytes 49160 | tf_op jit(solution)/shard_map/ppermute | solution.py:24
  2.4 1.5 %collective-permute-start.1 = (bf16[16,512]{1,0:T(8,128)(2,1)}, bf16[16,512]{1,0:T(8,128)(2,1)S(1)}, u32[]{:S(2)}, u32[]{:S(2)}) collective-permute-start(bf16[16,512]{1,0:T(8,128)(2,1)} %query_hbm.1), channel_id=1, source_target_pairs={{0,24},{4,28},{8,0},{12,4},{16,8},{20,12},{24,16},{28,20},{1,25},{... | collective-permute-start | bytes 49160 | tf_op jit(solution)/shard_map/ppermute | solution.py:24
  3.9 1.4 %collective-permute-start.2 = (bf16[16,512]{1,0:T(8,128)(2,1)}, bf16[16,512]{1,0:T(8,128)(2,1)S(1)}, u32[]{:S(2)}, u32[]{:S(2)}) collective-permute-start(bf16[16,512]{1,0:T(8,128)(2,1)} %query_hbm.1), channel_id=1, source_target_pairs={{0,28},{4,0},{8,4},{12,8},{16,12},{20,16},{24,20},{28,24},{1,29},{... | collective-permute-start | bytes 49160 | tf_op jit(solution)/shard_map/ppermute | solution.py:24
  5.3 0.1 collective-permute-start.6
  5.4 1.5 %collective-permute-start.7 = (bf16[16,512]{1,0:T(8,128)(2,1)}, bf16[16,512]{1,0:T(8,128)(2,1)S(1)}, u32[]{:S(2)}, u32[]{:S(2)}) collective-permute-start(bf16[16,512]{1,0:T(8,128)(2,1)} %query_hbm.1), channel_id=1, source_target_pairs={{0,16},{4,20},{8,24},{12,28},{16,0},{20,4},{24,8},{28,12},{1,17},{... | collective-permute-start | bytes 49160 | tf_op jit(solution)/shard_map/ppermute | solution.py:24
  6.9 2.6 %shard_map.55 = (f32[64,128]{1,0:T(8,128)S(1)}, f32[64,128]{1,0:T(8,128)S(1)}, f32[64,128]{1,0:T(8,128)S(1)}, bf16[6,256,128]{2,1,0:T(8,128)(2,1)S(1)}, bf16[6,2...) custom-call(s32[6]{0:T(128)} %offset_hbm.1, bf16[16,512]{1,0:T(8,128)(2,1)} %query_hbm.1, ...), custom_call_target="tpu_custom_call" | custom-call | flops 25165824 | bytes 2883584 | tf_op jit(solution)/shard_map/pallas_call | solution.py:253
  9.5 0.0 collective-permute-done.refs_0_
  9.5 0.0 collective-permute-done.1.refs_1_
  9.5 0.0 collective-permute-done.2.refs_2_
  9.5 2.3 %shard_map.56 = (bf16[64,256]{1,0:T(8,128)(2,1)S(1)}, bf16[64,256]{1,0:T(8,128)(2,1)S(1)}, bf16[64,256]{1,0:T(8,128)(2,1)S(1)}, bf16[512,2048]{1,0:T(8,128)(2,1)S(1)}) custom-call(bf16[6,256,128]{2,1,0:T(8,128)(2,1)S(1)} %get-tuple-element.22.key_ref, bf16[6,256,128]{2,1,0:T(8,128)(2,1)S(1)} %get-tuple-element.23.value_ref, ...), custom_call_target="tpu_custom_call" | custom-call | tf_op jit(solution)/shard_map/pallas_call | solution.py:275
  11.9 0.3 collective-permute-start.3
  12.2 0.6 %collective-permute-start.4 = (bf16[64,256]{1,0:T(8,128)(2,1)S(1)}, bf16[64,256]{1,0:T(8,128)(2,1)S(1)}, u32[]{:S(2)}, u32[]{:S(2)}) collective-permute-start(bf16[64,256]{1,0:T(8,128)(2,1)S(1)} %get-tuple-element.26), channel_id=1, source_target_pairs={{0,8},{4,12},{8,16},{12,20},{16,24},{20,28},{24,0},{28,4},{1,9},{5... | collective-permute-start | bytes 98312 | tf_op jit(solution)/shard_map/ppermute | solution.py:24
  12.8 2.1 %collective-permute-start.5 = (bf16[64,256]{1,0:T(8,128)(2,1)S(1)}, bf16[64,256]{1,0:T(8,128)(2,1)S(1)}, u32[]{:S(2)}, u32[]{:S(2)}) collective-permute-start(bf16[64,256]{1,0:T(8,128)(2,1)S(1)} %get-tuple-element.27), channel_id=1, source_target_pairs={{0,12},{4,16},{8,20},{12,24},{16,28},{20,0},{24,4},{28,8},{1,13},{... | collective-permute-start | bytes 98312 | tf_op jit(solution)/shard_map/ppermute | solution.py:24
  15.0 0.0 collective-permute-done.6.refs_0_
  15.0 0.0 collective-permute-done.7.refs_1_
  15.0 1.6 %shard_map.57 = (bf16[64,256]{1,0:T(8,128)(2,1)S(1)}, bf16[64,256]{1,0:T(8,128)(2,1)S(1)}, bf16[512,2048]{1,0:T(8,128)(2,1)S(1)}) custom-call(bf16[6,256,128]{2,1,0:T(8,128)(2,1)S(1)} %get-tuple-element.22.key_ref, bf16[6,256,128]{2,1,0:T(8,128)(2,1)S(1)} %get-tuple-element.23.value_ref, f32[6,8,256]{2,1,0:T(8,128)S(1)} %get-tuple-element.24.bias_ref, ...), custom_call_target="tpu_custom_call" | custom-call | tf_op jit(solution)/shard_map/pallas_call | solution.py:275
  16.6 0.6 %collective-permute-start.8 = (bf16[64,256]{1,0:T(8,128)(2,1)S(1)}, bf16[64,256]{1,0:T(8,128)(2,1)S(1)}, u32[]{:S(2)}, u32[]{:S(2)}) collective-permute-start(bf16[64,256]{1,0:T(8,128)(2,1)S(1)} %get-tuple-element.28), channel_id=1, source_target_pairs={{0,16},{4,20},{8,24},{12,28},{16,0},{20,4},{24,8},{28,12},{1,17},{... | collective-permute-start | bytes 98312 | tf_op jit(solution)/shard_map/ppermute | solution.py:24
  17.2 0.0 collective-permute-start.9
  17.2 0.0 collective-permute-done.3.refs_0_
  17.2 0.0 collective-permute-done.4.refs_1_
  17.2 0.0 collective-permute-done.5.refs_2_
  17.3 3.3 %collective-permute-done.8.refs_3_ = bf16[64,256]{1,0:T(8,128)(2,1)S(1)} collective-permute-done((bf16[64,256]{1,0:T(8,128)(2,1)S(1)}, bf16[64,256]{1,0:T(8,128)(2,1)S(1)}, u32[]{:S(2)}, u32[]{:S(2)}) %collective-permute-start.8) | collective-permute-done | bytes 32800 | tf_op jit(solution)/shard_map/ppermute | solution.py:24
  20.6 0.0 collective-permute-done.9.refs_4_
  20.6 0.2 shard_map.58.attended_ref
  20.7 0.4 shard_map.60
  21.1 1.6 %collective-permute-start.10 = (bf16[16,2048]{1,0:T(8,128)(2,1)S(1)}, bf16[16,2048]{1,0:T(8,128)(2,1)S(1)}, u32[]{:S(2)}, u32[]{:S(2)}) collective-permute-start(bf16[16,2048]{1,0:T(8,128)(2,1)S(1)} %shard_map.60), channel_id=1, source_target_pairs={{0,1},{1,0},{2,3},{3,2},{4,5},{5,4},{6,7},{7,6},{8,9},{9,8},{10,11... | collective-permute-start | bytes 196616 | tf_op jit(solution)/shard_map/ppermute | solution.py:29
  22.7 1.6 %shard_map.62.weight_ref = bf16[512,2048]{1,0:T(8,128)(2,1)S(1)} custom-call(bf16[512,8192]{1,0:T(8,128)(2,1)} %weight_hbm.7, bf16[64,256]{1,0:T(8,128)(2,1)S(1)} %get-tuple-element.29.after_hbm), custom_call_target="tpu_custom_call" | custom-call | bytes 2097152 | tf_op jit(solution)/shard_map/pallas_call | solution.py:287
  24.3 0.4 shard_map.61
  24.7 0.5 %collective-permute-start.13 = (bf16[16,2048]{1,0:T(8,128)(2,1)S(1)}, bf16[16,2048]{1,0:T(8,128)(2,1)S(1)}, u32[]{:S(2)}, u32[]{:S(2)}) collective-permute-start(bf16[16,2048]{1,0:T(8,128)(2,1)S(1)} %shard_map.61), channel_id=1, source_target_pairs={{0,1},{1,0},{2,3},{3,2},{4,5},{5,4},{6,7},{7,6},{8,9},{9,8},{10,11... | collective-permute-start | bytes 196616 | tf_op jit(solution)/shard_map/ppermute | solution.py:29
  25.2 0.4 shard_map.63
  25.5 1.6 %collective-permute-start.15 = (bf16[16,2048]{1,0:T(8,128)(2,1)S(1)}, bf16[16,2048]{1,0:T(8,128)(2,1)S(1)}, u32[]{:S(2)}, u32[]{:S(2)}) collective-permute-start(bf16[16,2048]{1,0:T(8,128)(2,1)S(1)} %shard_map.63), channel_id=1, source_target_pairs={{0,1},{1,0},{2,3},{3,2},{4,5},{5,4},{6,7},{7,6},{8,9},{9,8},{10,11... | collective-permute-start | bytes 196616 | tf_op jit(solution)/shard_map/ppermute | solution.py:29
  27.1 0.4 shard_map.59
  27.5 0.0 collective-permute-done.10
  27.5 2.7 %collective-permute-start.11 = (bf16[16,2048]{1,0:T(8,128)(2,1)S(1)}, bf16[16,2048]{1,0:T(8,128)(2,1)S(1)}, u32[]{:S(2)}, u32[]{:S(2)}) collective-permute-start(bf16[16,2048]{1,0:T(8,128)(2,1)S(1)} %add_convert_fusion.3), channel_id=1, source_target_pairs={{0,2},{1,3},{2,0},{3,1},{4,6},{5,7},{6,4},{7,5},{8,10},{9,11},{10,... | collective-permute-start | bytes 196616 | tf_op jit(solution)/shard_map/ppermute | solution.py:29
  30.2 0.0 collective-permute-done.13
  30.2 2.1 %collective-permute-start.14 = (bf16[16,2048]{1,0:T(8,128)(2,1)S(1)}, bf16[16,2048]{1,0:T(8,128)(2,1)S(1)}, u32[]{:S(2)}, u32[]{:S(2)}) collective-permute-start(bf16[16,2048]{1,0:T(8,128)(2,1)S(1)} %add_convert_fusion.1.refs_0_), channel_id=1, source_target_pairs={{0,2},{1,3},{2,0},{3,1},{4,6},{5,7},{6,4},{7,5},{8,10},{9,11},{10,... | collective-permute-start | bytes 196616 | tf_op jit(solution)/shard_map/ppermute | solution.py:29
  32.3 0.0 collective-permute-done.15
  32.4 1.0 %collective-permute-start.16 = (bf16[16,2048]{1,0:T(8,128)(2,1)S(1)}, bf16[16,2048]{1,0:T(8,128)(2,1)S(1)}, u32[]{:S(2)}, u32[]{:S(2)}) collective-permute-start(bf16[16,2048]{1,0:T(8,128)(2,1)S(1)} %add_convert_fusion.refs_2_), channel_id=1, source_target_pairs={{0,2},{1,3},{2,0},{3,1},{4,6},{5,7},{6,4},{7,5},{8,10},{9,11},{10,... | collective-permute-start | bytes 196616 | tf_op jit(solution)/shard_map/ppermute | solution.py:29
  33.4 2.5 %collective-permute-done.11 = bf16[16,2048]{1,0:T(8,128)(2,1)S(1)} collective-permute-done((bf16[16,2048]{1,0:T(8,128)(2,1)S(1)}, bf16[16,2048]{1,0:T(8,128)(2,1)S(1)}, u32[]{:S(2)}, u32[]{:S(2)}) %collective-permute-start.11) | collective-permute-done | bytes 65568 | tf_op jit(solution)/shard_map/ppermute | solution.py:29
  35.8 0.1 collective-permute-start.12
  35.9 2.0 %collective-permute-done.14.refs_1_ = bf16[16,2048]{1,0:T(8,128)(2,1)S(1)} collective-permute-done((bf16[16,2048]{1,0:T(8,128)(2,1)S(1)}, bf16[16,2048]{1,0:T(8,128)(2,1)S(1)}, u32[]{:S(2)}, u32[]{:S(2)}) %collective-permute-start.14) | collective-permute-done | bytes 65568 | tf_op jit(solution)/shard_map/ppermute | solution.py:29
  37.9 1.3 %collective-permute-done.16.refs_3_ = bf16[16,2048]{1,0:T(8,128)(2,1)S(1)} collective-permute-done((bf16[16,2048]{1,0:T(8,128)(2,1)S(1)}, bf16[16,2048]{1,0:T(8,128)(2,1)S(1)}, u32[]{:S(2)}, u32[]{:S(2)}) %collective-permute-start.16) | collective-permute-done | bytes 65568 | tf_op jit(solution)/shard_map/ppermute | solution.py:29
  39.2 1.0 %collective-permute-done.12.other_ref = bf16[16,2048]{1,0:T(8,128)(2,1)S(1)} collective-permute-done((bf16[16,2048]{1,0:T(8,128)(2,1)S(1)}, bf16[16,2048]{1,0:T(8,128)(2,1)S(1)}, u32[]{:S(2)}, u32[]{:S(2)}) %collective-permute-start.12) | collective-permute-done | bytes 65568 | tf_op jit(solution)/shard_map/ppermute | solution.py:29
  40.2 0.7 %shard_map.64 = bf16[16,8192]{1,0:T(8,128)(2,1)} custom-call(bf16[16,2048]{1,0:T(8,128)(2,1)S(1)} %add_convert_fusion.2.kept_ref, bf16[16,2048]{1,0:T(8,128)(2,1)S(1)} %collective-permute-done.12.other_ref, bf16[16,2048]{1,0:T(8,128)(2,1)S(1)} %add_convert_fusion.1.refs_0_, bf16[16,2048]{1,0:T(8,128)(2,1)S(1)} %collective-permute-done.14.refs_1_, ...), custom_call_target="tpu_custom_call" | custom-call | tf_op jit(solution)/shard_map/pallas_call | solution.py:220
  (4 shorter events, 0.1 us)
Async XLA Ops:
  0.0 9.5 %collective-permute-start = (bf16[16,512]{1,0:T(8,128)(2,1)}, bf16[16,512]{1,0:T(8,128)(2,1)S(1)}, u32[]{:S(2)}, u32[]{:S(2)}) collective-permute-start(bf16[16,512]{1,0:T(8,128)(2,1)} %query_hbm.1), channel_id=1, source_target_pairs={{0,20},{4,24},{8,28},{12,0},{16,4},{20,8},{24,12},{28,16},{1,21},{... | collective-permute-start | bytes 49160 | tf_op jit(solution)/shard_map/ppermute | solution.py:24
  2.4 7.1 %collective-permute-start.1 = (bf16[16,512]{1,0:T(8,128)(2,1)}, bf16[16,512]{1,0:T(8,128)(2,1)S(1)}, u32[]{:S(2)}, u32[]{:S(2)}) collective-permute-start(bf16[16,512]{1,0:T(8,128)(2,1)} %query_hbm.1), channel_id=1, source_target_pairs={{0,24},{4,28},{8,0},{12,4},{16,8},{20,12},{24,16},{28,20},{1,25},{... | collective-permute-start | bytes 49160 | tf_op jit(solution)/shard_map/ppermute | solution.py:24
  3.9 5.6 %collective-permute-start.2 = (bf16[16,512]{1,0:T(8,128)(2,1)}, bf16[16,512]{1,0:T(8,128)(2,1)S(1)}, u32[]{:S(2)}, u32[]{:S(2)}) collective-permute-start(bf16[16,512]{1,0:T(8,128)(2,1)} %query_hbm.1), channel_id=1, source_target_pairs={{0,28},{4,0},{8,4},{12,8},{16,12},{20,16},{24,20},{28,24},{1,29},{... | collective-permute-start | bytes 49160 | tf_op jit(solution)/shard_map/ppermute | solution.py:24
  5.3 9.6 %collective-permute-start.6 = (bf16[16,512]{1,0:T(8,128)(2,1)}, bf16[16,512]{1,0:T(8,128)(2,1)S(1)}, u32[]{:S(2)}, u32[]{:S(2)}) collective-permute-start(bf16[16,512]{1,0:T(8,128)(2,1)} %query_hbm.1), channel_id=1, source_target_pairs={{0,12},{4,16},{8,20},{12,24},{16,28},{20,0},{24,4},{28,8},{1,13},{... | collective-permute-start | bytes 49160 | tf_op jit(solution)/shard_map/ppermute | solution.py:24
  5.4 9.6 %collective-permute-start.7 = (bf16[16,512]{1,0:T(8,128)(2,1)}, bf16[16,512]{1,0:T(8,128)(2,1)S(1)}, u32[]{:S(2)}, u32[]{:S(2)}) collective-permute-start(bf16[16,512]{1,0:T(8,128)(2,1)} %query_hbm.1), channel_id=1, source_target_pairs={{0,16},{4,20},{8,24},{12,28},{16,0},{20,4},{24,8},{28,12},{1,17},{... | collective-permute-start | bytes 49160 | tf_op jit(solution)/shard_map/ppermute | solution.py:24
  11.9 5.4 %collective-permute-start.3 = (bf16[64,256]{1,0:T(8,128)(2,1)S(1)}, bf16[64,256]{1,0:T(8,128)(2,1)S(1)}, u32[]{:S(2)}, u32[]{:S(2)}) collective-permute-start(bf16[64,256]{1,0:T(8,128)(2,1)S(1)} %get-tuple-element.25), channel_id=1, source_target_pairs={{0,4},{4,8},{8,12},{12,16},{16,20},{20,24},{24,28},{28,0},{1,5},{5... | collective-permute-start | bytes 98312 | tf_op jit(solution)/shard_map/ppermute | solution.py:24
  12.2 5.0 %collective-permute-start.4 = (bf16[64,256]{1,0:T(8,128)(2,1)S(1)}, bf16[64,256]{1,0:T(8,128)(2,1)S(1)}, u32[]{:S(2)}, u32[]{:S(2)}) collective-permute-start(bf16[64,256]{1,0:T(8,128)(2,1)S(1)} %get-tuple-element.26), channel_id=1, source_target_pairs={{0,8},{4,12},{8,16},{12,20},{16,24},{20,28},{24,0},{28,4},{1,9},{5... | collective-permute-start | bytes 98312 | tf_op jit(solution)/shard_map/ppermute | solution.py:24
  12.8 4.4 %collective-permute-start.5 = (bf16[64,256]{1,0:T(8,128)(2,1)S(1)}, bf16[64,256]{1,0:T(8,128)(2,1)S(1)}, u32[]{:S(2)}, u32[]{:S(2)}) collective-permute-start(bf16[64,256]{1,0:T(8,128)(2,1)S(1)} %get-tuple-element.27), channel_id=1, source_target_pairs={{0,12},{4,16},{8,20},{12,24},{16,28},{20,0},{24,4},{28,8},{1,13},{... | collective-permute-start | bytes 98312 | tf_op jit(solution)/shard_map/ppermute | solution.py:24
  16.6 4.0 %collective-permute-start.8 = (bf16[64,256]{1,0:T(8,128)(2,1)S(1)}, bf16[64,256]{1,0:T(8,128)(2,1)S(1)}, u32[]{:S(2)}, u32[]{:S(2)}) collective-permute-start(bf16[64,256]{1,0:T(8,128)(2,1)S(1)} %get-tuple-element.28), channel_id=1, source_target_pairs={{0,16},{4,20},{8,24},{12,28},{16,0},{20,4},{24,8},{28,12},{1,17},{... | collective-permute-start | bytes 98312 | tf_op jit(solution)/shard_map/ppermute | solution.py:24
  17.2 3.4 %collective-permute-start.9 = (bf16[64,256]{1,0:T(8,128)(2,1)S(1)}, bf16[64,256]{1,0:T(8,128)(2,1)S(1)}, u32[]{:S(2)}, u32[]{:S(2)}) collective-permute-start(bf16[64,256]{1,0:T(8,128)(2,1)S(1)} %get-tuple-element.29.after_hbm), channel_id=1, source_target_pairs={{0,20},{4,24},{8,28},{12,0},{16,4},{20,8},{24,12},{28,16},{1,21},{... | collective-permute-start | bytes 98312 | tf_op jit(solution)/shard_map/ppermute | solution.py:24
  21.1 6.4 %collective-permute-start.10 = (bf16[16,2048]{1,0:T(8,128)(2,1)S(1)}, bf16[16,2048]{1,0:T(8,128)(2,1)S(1)}, u32[]{:S(2)}, u32[]{:S(2)}) collective-permute-start(bf16[16,2048]{1,0:T(8,128)(2,1)S(1)} %shard_map.60), channel_id=1, source_target_pairs={{0,1},{1,0},{2,3},{3,2},{4,5},{5,4},{6,7},{7,6},{8,9},{9,8},{10,11... | collective-permute-start | bytes 196616 | tf_op jit(solution)/shard_map/ppermute | solution.py:29
  24.7 5.5 %collective-permute-start.13 = (bf16[16,2048]{1,0:T(8,128)(2,1)S(1)}, bf16[16,2048]{1,0:T(8,128)(2,1)S(1)}, u32[]{:S(2)}, u32[]{:S(2)}) collective-permute-start(bf16[16,2048]{1,0:T(8,128)(2,1)S(1)} %shard_map.61), channel_id=1, source_target_pairs={{0,1},{1,0},{2,3},{3,2},{4,5},{5,4},{6,7},{7,6},{8,9},{9,8},{10,11... | collective-permute-start | bytes 196616 | tf_op jit(solution)/shard_map/ppermute | solution.py:29
  25.5 6.8 %collective-permute-start.15 = (bf16[16,2048]{1,0:T(8,128)(2,1)S(1)}, bf16[16,2048]{1,0:T(8,128)(2,1)S(1)}, u32[]{:S(2)}, u32[]{:S(2)}) collective-permute-start(bf16[16,2048]{1,0:T(8,128)(2,1)S(1)} %shard_map.63), channel_id=1, source_target_pairs={{0,1},{1,0},{2,3},{3,2},{4,5},{5,4},{6,7},{7,6},{8,9},{9,8},{10,11... | collective-permute-start | bytes 196616 | tf_op jit(solution)/shard_map/ppermute | solution.py:29
  27.5 8.3 %collective-permute-start.11 = (bf16[16,2048]{1,0:T(8,128)(2,1)S(1)}, bf16[16,2048]{1,0:T(8,128)(2,1)S(1)}, u32[]{:S(2)}, u32[]{:S(2)}) collective-permute-start(bf16[16,2048]{1,0:T(8,128)(2,1)S(1)} %add_convert_fusion.3), channel_id=1, source_target_pairs={{0,2},{1,3},{2,0},{3,1},{4,6},{5,7},{6,4},{7,5},{8,10},{9,11},{10,... | collective-permute-start | bytes 196616 | tf_op jit(solution)/shard_map/ppermute | solution.py:29
  30.2 7.7 %collective-permute-start.14 = (bf16[16,2048]{1,0:T(8,128)(2,1)S(1)}, bf16[16,2048]{1,0:T(8,128)(2,1)S(1)}, u32[]{:S(2)}, u32[]{:S(2)}) collective-permute-start(bf16[16,2048]{1,0:T(8,128)(2,1)S(1)} %add_convert_fusion.1.refs_0_), channel_id=1, source_target_pairs={{0,2},{1,3},{2,0},{3,1},{4,6},{5,7},{6,4},{7,5},{8,10},{9,11},{10,... | collective-permute-start | bytes 196616 | tf_op jit(solution)/shard_map/ppermute | solution.py:29
  32.4 6.8 %collective-permute-start.16 = (bf16[16,2048]{1,0:T(8,128)(2,1)S(1)}, bf16[16,2048]{1,0:T(8,128)(2,1)S(1)}, u32[]{:S(2)}, u32[]{:S(2)}) collective-permute-start(bf16[16,2048]{1,0:T(8,128)(2,1)S(1)} %add_convert_fusion.refs_2_), channel_id=1, source_target_pairs={{0,2},{1,3},{2,0},{3,1},{4,6},{5,7},{6,4},{7,5},{8,10},{9,11},{10,... | collective-permute-start | bytes 196616 | tf_op jit(solution)/shard_map/ppermute | solution.py:29
  35.8 4.3 %collective-permute-start.12 = (bf16[16,2048]{1,0:T(8,128)(2,1)S(1)}, bf16[16,2048]{1,0:T(8,128)(2,1)S(1)}, u32[]{:S(2)}, u32[]{:S(2)}) collective-permute-start(bf16[16,2048]{1,0:T(8,128)(2,1)S(1)} %add_convert_fusion.2.kept_ref), channel_id=1, source_target_pairs={{0,1},{1,0},{2,3},{3,2},{4,5},{5,4},{6,7},{7,6},{8,9},{9,8},{10,11... | collective-permute-start | bytes 196616 | tf_op jit(solution)/shard_map/ppermute | solution.py:29

commit v3 on v2

--- a/solution.py
+++ b/solution.py
@@ -64,38 +64,71 @@
     )
 
 
-def own_kernel(local_heads, chunk, offset_hbm, query_hbm, pool_hbm, suffix_hbm, weight_hbm,
-               acc_ref, peak_ref, total_ref, key_ref, value_ref, bias_ref, weight_ref,
-               offset_ref, query_ref, suffix_ref, sems, slot_sems):
+def gather_kernel(local_heads, chunk, offset_hbm, pool_hbm, weight_hbm,
+                  key_ref, value_ref, bias_ref, weight_ref, offset_ref, pool_ref, sems):
+    kv = lax.axis_index("mp") * local_heads // GQA
+    block = pool_ref.shape[2]
+    copies = [
+        pltpu.make_async_copy(offset_hbm, offset_ref, sems.at[0]),
+        pltpu.make_async_copy(pool_hbm.at[:, kv], pool_ref, sems.at[1]),
+        weight_copy(weight_hbm, chunk, weight_ref, sems.at[2]),
+    ]
+    for copy in copies:
+        copy.start()
+    copies[0].wait()
+    found = [slots_of(offset_ref, lag) for lag in range(SPREAD)]
+    at = lax.broadcasted_iota(jnp.int32, bias_ref.shape[1:], 1)
+    for lag, (_, count) in enumerate(found):
+        bias_ref[lag] = jnp.where(at < count * block, 0.0, NEG)
+    copies[1].wait()
+    for lag, (slots, _) in enumerate(found):
+        for position, slot in enumerate(slots):
+            key_ref[lag, position * block : (position + 1) * block] = pool_ref[slot, 0]
+            value_ref[lag, position * block : (position + 1) * block] = pool_ref[slot, 1]
+    copies[2].wait()
+
+
+def lag_kernel(lags, key_ref, value_ref, bias_ref, *refs):
+    query_refs, out_refs = refs[: len(lags)], refs[len(lags) :]
+    head_dim = key_ref.shape[-1]
+    scale = head_dim ** (-0.5)
+    rows = [head_rows(ref[...], head_dim) for ref in query_refs]
+    scores = [dot_nt(r, key_ref[lag]) * scale + bias_ref[lag][:1] for r, lag in zip(rows, lags)]
+    peaks = [jnp.max(x, axis=1, keepdims=True).astype(jnp.bfloat16) for x in scores]
+    weights = [jnp.exp(x - peak.astype(jnp.float32)) for x, peak in zip(scores, peaks)]
+    accs = [
+        jnp.dot(w.astype(jnp.bfloat16), value_ref[lag], preferred_element_type=jnp.float32)
+        for w, lag in zip(weights, lags)
+    ]
+    totals = [jnp.sum(w, axis=1, keepdims=True).astype(jnp.bfloat16) for w in weights]
+    half = (rows[0].shape[0], head_dim // 2)
+    for out_ref, acc, peak, total in zip(out_refs, accs, peaks, totals):
+        out_ref[:, :head_dim] = acc.astype(jnp.bfloat16)
+        out_ref[:, head_dim:] = jnp.concatenate(
+            [jnp.broadcast_to(peak, half), jnp.broadcast_to(total, half)], axis=1
+        )
+
+
+def own_kernel(local_heads, chunks, key_ref, value_ref, bias_ref, after_ref, query_hbm, suffix_hbm, weight_hbm, *refs):
+    acc_ref, peak_ref, total_ref = refs[:3]
+    weight_refs = refs[3 : 3 + len(chunks)]
+    query_ref, suffix_ref, sems = refs[3 + len(chunks) :]
     kv = lax.axis_index("mp") * local_heads // GQA
     samples, _, length, head_dim = suffix_ref.shape
-    block = key_ref.shape[1] // CAPACITY
     scale = head_dim ** (-0.5)
-    offset_copy = pltpu.make_async_copy(offset_hbm, offset_ref, sems.at[0])
-    query_copy = pltpu.make_async_copy(query_hbm, query_ref, sems.at[1])
-    suffix_copy = pltpu.make_async_copy(suffix_hbm.at[:, kv], suffix_ref, sems.at[2])
-    weight_load = weight_copy(weight_hbm, chunk, weight_ref, sems.at[3])
-    offset_copy.start()
-    query_copy.start()
-    suffix_copy.start()
-    weight_load.start()
-    offset_copy.wait()
-    slot_copies = []
-    for lag in range(SPREAD):
-        slots, count = slots_of(offset_ref, lag)
-        for position, slot in enumerate(slots):
-            place = pl.ds(position * block, block)
-            for part, out_ref in enumerate((key_ref, value_ref)):
-                copy = pltpu.make_async_copy(
-                    pool_hbm.at[slot, kv, part], out_ref.at[lag, place], slot_sems.at[lag, position, part]
-                )
-                copy.start()
-                slot_copies.append(copy)
-        at = lax.broadcasted_iota(jnp.int32, bias_ref.shape[1:], 1)
-        bias_ref[lag] = jnp.where(at < count * block, 0.0, NEG)
-    query_copy.wait()
+    copies = [
+        pltpu.make_async_copy(query_hbm, query_ref, sems.at[0]),
+        pltpu.make_async_copy(suffix_hbm.at[:, kv], suffix_ref, sems.at[1]),
+    ] + [
+        weight_copy(weight_hbm, chunk, ref, sems.at[2 + i])
+        for i, (chunk, ref) in enumerate(zip(chunks, weight_refs))
+    ]
+    for copy in copies:
+        copy.start()
+    copies[0].wait()
     rows = head_rows(query_ref[...], head_dim)
-    suffix_copy.wait()
+    scores = dot_nt(rows, key_ref[0]) * scale + bias_ref[0][:1]
+    copies[1].wait()
     suffix_keys = suffix_ref[:, 0].reshape(samples * length, head_dim)
     suffix_values = suffix_ref[:, 1].reshape(samples * length, head_dim)
     suffix_scores = dot_nt(rows, suffix_keys) * scale
@@ -103,9 +136,6 @@
     key_at = lax.broadcasted_iota(jnp.int32, suffix_scores.shape, 1)
     mine = (key_at >= row_sample * length) & (key_at < (row_sample + 1) * length)
     suffix_scores = jnp.where(mine, suffix_scores, NEG)
-    for copy in slot_copies:
-        copy.wait()
-    scores = dot_nt(rows, key_ref[0]) * scale + bias_ref[0][:1]
     peak = jnp.maximum(
         jnp.max(suffix_scores, axis=1, keepdims=True), jnp.max(scores, axis=1, keepdims=True)
     )
@@ -117,36 +147,8 @@
     ) + jnp.dot(weight.astype(jnp.bfloat16), value_ref[0], preferred_element_type=jnp.float32)
     peak_ref[...] = jnp.broadcast_to(peak, peak_ref.shape)
     total_ref[...] = jnp.broadcast_to(total, total_ref.shape)
-    weight_load.wait()
-
-
-def lag_kernel(lags, chunk, key_ref, value_ref, bias_ref, weight_hbm, *refs):
-    query_refs = refs[: len(lags)]
-    out_refs = refs[len(lags) : 2 * len(lags)]
-    weight_ref, sem = refs[2 * len(lags) :]
-    load = weight_copy(weight_hbm, chunk, weight_ref, sem)
-    load.start()
-    head_dim = key_ref.shape[-1]
-    scale = head_dim ** (-0.5)
-    for lag, query_ref, out_ref in zip(lags, query_refs, out_refs):
-        rows = head_rows(query_ref[...], head_dim)
-        scores = dot_nt(rows, key_ref[lag]) * scale + bias_ref[lag][:1]
-        peak = jnp.max(scores, axis=1, keepdims=True).astype(jnp.bfloat16)
-        weight = jnp.exp(scores - peak.astype(jnp.float32))
-        total = jnp.sum(weight, axis=1, keepdims=True).astype(jnp.bfloat16)
-        acc = jnp.dot(weight.astype(jnp.bfloat16), value_ref[lag], preferred_element_type=jnp.float32)
-        half = (rows.shape[0], head_dim // 2)
-        out_ref[:, :head_dim] = acc.astype(jnp.bfloat16)
-        out_ref[:, head_dim:] = jnp.concatenate(
-            [jnp.broadcast_to(peak, half), jnp.broadcast_to(total, half)], axis=1
-        )
-    load.wait()
-
-
-def load_kernel(chunk, weight_hbm, after_hbm, weight_ref, sem):
-    load = weight_copy(weight_hbm, chunk, weight_ref, sem)
-    load.start()
-    load.wait()
+    for copy in copies[2:]:
+        copy.wait()
 
 
 def merge_kernel(acc_ref, peak_ref, total_ref, *refs):
@@ -249,50 +251,50 @@
     chunk_shape = pltpu.VMEM((depth, width), bf16)
     gathered_shape = pltpu.VMEM((SPREAD, CAPACITY * block, head_dim), bf16)
     asked = {lag: shifted(queries, -lag) for group in GROUPS for lag in group}
-    weights = [None] * CHUNKS
-    acc, peak, total, keys, values, bias, weights[0] = pl.pallas_call(
-        functools.partial(own_kernel, local_heads, 0),
-        out_shape=(pltpu.VMEM((rows, head_dim), f32),) * 3
-        + (gathered_shape, gathered_shape, pltpu.VMEM((SPREAD, 8, CAPACITY * block), f32), chunk_shape),
-        in_specs=[HBM_SPEC] * 5,
-        out_specs=(VMEM_SPEC,) * 7,
+    offsets, queries_hbm, pool, suffix, weight = in_hbm
+    keys, values, bias, first_chunk = pl.pallas_call(
+        functools.partial(gather_kernel, local_heads, 0),
+        out_shape=(gathered_shape, gathered_shape, pltpu.VMEM((SPREAD, 8, CAPACITY * block), f32), chunk_shape),
+        in_specs=[HBM_SPEC] * 3,
+        out_specs=(VMEM_SPEC,) * 4,
         scratch_shapes=[
             pltpu.SMEM(slot_offset.shape, jnp.int32),
+            pltpu.VMEM((blocks, 2, block, head_dim), bf16),
+            pltpu.SemaphoreType.DMA((3,)),
+        ],
+        compiler_params=PARAMS,
+        cost_estimate=pl.CostEstimate(flops=0, bytes_accessed=2 * depth * width, transcendentals=0),
+    )(offsets, pool, weight)
+    parts = {}
+    for group in GROUPS:
+        out = pl.pallas_call(
+            functools.partial(lag_kernel, group),
+            out_shape=(jax.ShapeDtypeStruct((rows, 2 * head_dim), bf16),) * len(group),
+            in_specs=[VMEM_SPEC] * (3 + len(group)),
+            out_specs=(VMEM_SPEC,) * len(group),
+            compiler_params=PARAMS,
+        )(keys, values, bias, *[asked[lag] for lag in group])
+        for lag, answer in zip(group, out):
+            parts[lag] = shifted(answer, lag)
+    later = tuple(range(1, CHUNKS))
+    acc, peak, total, *chunks = pl.pallas_call(
+        functools.partial(own_kernel, local_heads, later),
+        out_shape=(pltpu.VMEM((rows, head_dim), f32),) * 3 + (chunk_shape,) * len(later),
+        in_specs=[VMEM_SPEC] * 4 + [HBM_SPEC] * 3,
+        out_specs=(VMEM_SPEC,) * (3 + len(later)),
+        scratch_shapes=[
             pltpu.VMEM(queries.shape, bf16),
             pltpu.VMEM((samples, 2, length, head_dim), bf16),
-            pltpu.SemaphoreType.DMA((4,)),
-            pltpu.SemaphoreType.DMA((SPREAD, CAPACITY, 2)),
+            pltpu.SemaphoreType.DMA((2 + len(later),)),
         ],
         compiler_params=PARAMS,
         cost_estimate=pl.CostEstimate(
             flops=4 * rows * samples * length * head_dim,
-            bytes_accessed=2 * suffix_kv.size + 2 * depth * width,
+            bytes_accessed=2 * suffix_kv.size + 2 * depth * width * len(later),
             transcendentals=rows * samples * length,
         ),
-    )(*in_hbm)
-    parts = {}
-    for index, group in enumerate(GROUPS):
-        out = pl.pallas_call(
-            functools.partial(lag_kernel, group, 1 + index),
-            out_shape=(jax.ShapeDtypeStruct((rows, 2 * head_dim), bf16),) * len(group) + (chunk_shape,),
-            in_specs=[VMEM_SPEC] * 3 + [HBM_SPEC] + [VMEM_SPEC] * len(group),
-            out_specs=(VMEM_SPEC,) * (len(group) + 1),
-            scratch_shapes=[pltpu.SemaphoreType.DMA(())],
-            compiler_params=PARAMS,
-        )(keys, values, bias, in_hbm[-1], *[asked[lag] for lag in group])
-        weights[1 + index] = out[-1]
-        for lag, answer in zip(group, out):
-            parts[lag] = shifted(answer, lag)
-    last = out[0]
-    weights[3] = pl.pallas_call(
-        functools.partial(load_kernel, 3),
-        out_shape=chunk_shape,
-        in_specs=[HBM_SPEC, VMEM_SPEC],
-        out_specs=VMEM_SPEC,
-        scratch_shapes=[pltpu.SemaphoreType.DMA(())],
-        compiler_params=PARAMS,
-        cost_estimate=pl.CostEstimate(flops=0, bytes_accessed=2 * depth * width, transcendentals=0),
-    )(in_hbm[-1], last)
+    )(keys, values, bias, out[-1], queries_hbm, suffix, weight)
+    weights = [first_chunk, *chunks]
     attended = pl.pallas_call(
         merge_kernel,
         out_shape=jax.ShapeDtypeStruct(queries.shape, bf16),

time: 41.2 us -> 36.3 us (0.88)
  waiting for transfers between devices: 10 us -> 3.46 us
  starting transfers between devices: 20.1 us -> 24.4 us
  Pallas kernels: 10.6 us -> 8.04 us
    ppermute x7, starting transfers between devices: 9.5 us -> 13.1 us  [swapped(): return lax.ppermute(block, 'mp', [(i, i ^ step) for i in range(size)])]
    ppermute x10, waiting for transfers between devices: 3.32 us -> 0.03 us  [shifted(): lax.ppermute(block, 'dp', [(i, (i + distance) % size) for i in range(size)])]
    ppermute x7, waiting for transfers between devices: 6.72 us -> 3.44 us  [swapped(): return lax.ppermute(block, 'mp', [(i, i ^ step) for i in range(size)])]
    pallas_call x4, Pallas kernels: 8.19 us -> 5.63 us  [the longest x1 3.06 us: local(): pl.pallas_call(functools.partial(own_kernel, local_heads, later), out_sha...]
    ppermute x10, starting transfers between devices: 10.6 us -> 11.3 us  [shifted(): lax.ppermute(block, 'dp', [(i, (i + distance) % size) for i in range(size)])]
  transfers between devices with their start and end apart: 17 -> 17, of which waited for: 5 -> 4; matrix products, arithmetic and copies ran while one was open for 0% -> 0% of each run, Pallas kernels for 23% -> 19%
where the time goes in v3:
time: 36.3 us; the launch traced here: 36.1 us
  starting transfers between devices  24.4 us (67%)
  Pallas kernels  8.04 us (22%)
  waiting for transfers between devices  3.46 us (10%)
    ppermute x7, starting transfers between devices, swapped(): return lax.ppermute(block, 'mp', [(i, i ^ step) for i in range(size)])  13.1 us
    ppermute x10, starting transfers between devices, shifted(): lax.ppermute(block, 'dp', [(i, (i + distance) % size) for i in range(size)])  11.3 us
    ppermute x7, waiting for transfers between devices, swapped(): return lax.ppermute(block, 'mp', [(i, i ^ step) for i in range(size)])  3.44 us
    pallas_call x1, Pallas kernels, local(): pl.pallas_call(functools.partial(own_kernel, local_heads, later), out_sha...  3.06 us
    pallas_call x1, Pallas kernels, local(): pl.pallas_call(functools.partial(gather_kernel, local_heads, 0), out_shap...  1.75 us
    pallas_call x4, Pallas kernels, project(): pl.pallas_call(project_kernel, out_shape=jax.ShapeDtypeStruct((attended.s...  1.49 us
    pallas_call x2, Pallas kernels, local(): pl.pallas_call(functools.partial(lag_kernel, group), out_shape=(jax.Shape...  0.81 us
    pallas_call x1, Pallas kernels, summed_over_four(): pl.pallas_call(final_kernel, out_shape=jax.ShapeDtypeStruct((samples, wid...  0.74 us
  transfers between devices with their start and end apart: 17, of which 4 were waited for; matrix products, arithmetic and copies ran while one was open for 0% of the time, Pallas kernels for 19%

profile of v3, /device:TPU:0, one launch (start us, length us, event | category | flops | bytes accessed | tf_op | source)
XLA Modules:
  0.0 36.1 jit_solution(9808859064251249377)
XLA Ops:
  0.0 3.0 %collective-permute-start.1 = (bf16[16,512]{1,0:T(8,128)(2,1)}, bf16[16,512]{1,0:T(8,128)(2,1)S(1)}, u32[]{:S(2)}, u32[]{:S(2)}) collective-permute-start(bf16[16,512]{1,0:T(8,128)(2,1)} %query_hbm.1), channel_id=1, source_target_pairs={{0,16},{4,20},{8,24},{12,28},{16,0},{20,4},{24,8},{28,12},{1,17},{... | collective-permute-start | bytes 49160 | tf_op jit(solution)/shard_map/ppermute | solution.py:24
  3.0 0.7 %collective-permute-start = (bf16[16,512]{1,0:T(8,128)(2,1)}, bf16[16,512]{1,0:T(8,128)(2,1)S(1)}, u32[]{:S(2)}, u32[]{:S(2)}) collective-permute-start(bf16[16,512]{1,0:T(8,128)(2,1)} %query_hbm.1), channel_id=1, source_target_pairs={{0,12},{4,16},{8,20},{12,24},{16,28},{20,0},{24,4},{28,8},{1,13},{... | collective-permute-start | bytes 49160 | tf_op jit(solution)/shard_map/ppermute | solution.py:24
  3.6 1.1 %collective-permute-start.2 = (bf16[16,512]{1,0:T(8,128)(2,1)}, bf16[16,512]{1,0:T(8,128)(2,1)S(1)}, u32[]{:S(2)}, u32[]{:S(2)}) collective-permute-start(bf16[16,512]{1,0:T(8,128)(2,1)} %query_hbm.1), channel_id=1, source_target_pairs={{0,20},{4,24},{8,28},{12,0},{16,4},{20,8},{24,12},{28,16},{1,21},{... | collective-permute-start | bytes 49160 | tf_op jit(solution)/shard_map/ppermute | solution.py:24
  4.7 0.9 %collective-permute-start.4 = (bf16[16,512]{1,0:T(8,128)(2,1)}, bf16[16,512]{1,0:T(8,128)(2,1)S(1)}, u32[]{:S(2)}, u32[]{:S(2)}) collective-permute-start(bf16[16,512]{1,0:T(8,128)(2,1)} %query_hbm.1), channel_id=1, source_target_pairs={{0,28},{4,0},{8,4},{12,8},{16,12},{20,16},{24,20},{28,24},{1,29},{... | collective-permute-start | bytes 49160 | tf_op jit(solution)/shard_map/ppermute | solution.py:24
  5.6 1.5 %collective-permute-start.3 = (bf16[16,512]{1,0:T(8,128)(2,1)}, bf16[16,512]{1,0:T(8,128)(2,1)S(1)}, u32[]{:S(2)}, u32[]{:S(2)}) collective-permute-start(bf16[16,512]{1,0:T(8,128)(2,1)} %query_hbm.1), channel_id=1, source_target_pairs={{0,24},{4,28},{8,0},{12,4},{16,8},{20,12},{24,16},{28,20},{1,25},{... | collective-permute-start | bytes 49160 | tf_op jit(solution)/shard_map/ppermute | solution.py:24
  7.1 1.8 %shard_map.55 = (bf16[6,256,128]{2,1,0:T(8,128)(2,1)S(1)}, bf16[6,256,128]{2,1,0:T(8,128)(2,1)S(1)}, f32[6,8,256]{2,1,0:T(8,128)S(1)}, bf16[512,2048]{1,0:T(8,128)(2,1)S(1)}) custom-call(s32[6]{0:T(128)} %offset_hbm.1, bf16[6,2,2,128,128]{4,3,2,1,0:T(8,128)(2,1)} %pool_hbm.1, bf16[512,8192]{1,0:T(8,128)(2,1)} %weight_hbm.3), custom_call_target="tpu_custom_call" | custom-call | bytes 2097152 | tf_op jit(solution)/shard_map/pallas_call | solution.py:255
  8.9 0.0 collective-permute-done.1.refs_1_
  8.9 0.0 collective-permute-done.refs_0_
  8.9 0.4 %shard_map.56 = (bf16[64,256]{1,0:T(8,128)(2,1)S(1)}, bf16[64,256]{1,0:T(8,128)(2,1)S(1)}) custom-call(bf16[6,256,128]{2,1,0:T(8,128)(2,1)S(1)} %get-tuple-element.20.key_ref, bf16[6,256,128]{2,1,0:T(8,128)(2,1)S(1)} %get-tuple-element.21.value_ref, f32[6,8,256]{2,1,0:T(8,128)S(1)} %get-tuple-element.22.bias_ref, ...), custom_call_target="tpu_custom_call" | custom-call | tf_op jit(solution)/shard_map/pallas_call | solution.py:270
  9.3 0.4 %collective-permute-start.9 = (bf16[64,256]{1,0:T(8,128)(2,1)S(1)}, bf16[64,256]{1,0:T(8,128)(2,1)S(1)}, u32[]{:S(2)}, u32[]{:S(2)}) collective-permute-start(bf16[64,256]{1,0:T(8,128)(2,1)S(1)} %get-tuple-element.30), channel_id=1, source_target_pairs={{0,20},{4,24},{8,28},{12,0},{16,4},{20,8},{24,12},{28,16},{1,21},{... | collective-permute-start | bytes 98312 | tf_op jit(solution)/shard_map/ppermute | solution.py:24
  9.7 0.8 %collective-permute-start.8 = (bf16[64,256]{1,0:T(8,128)(2,1)S(1)}, bf16[64,256]{1,0:T(8,128)(2,1)S(1)}, u32[]{:S(2)}, u32[]{:S(2)}) collective-permute-start(bf16[64,256]{1,0:T(8,128)(2,1)S(1)} %get-tuple-element.23.after_ref), channel_id=1, source_target_pairs={{0,16},{4,20},{8,24},{12,28},{16,0},{20,4},{24,8},{28,12},{1,17},{... | collective-permute-start | bytes 98312 | tf_op jit(solution)/shard_map/ppermute | solution.py:24
  10.6 0.0 collective-permute-done.2.refs_0_
  10.6 0.0 collective-permute-done.4.refs_2_
  10.6 0.0 collective-permute-done.3.refs_1_
  10.6 0.4 %shard_map.58 = (bf16[64,256]{1,0:T(8,128)(2,1)S(1)}, bf16[64,256]{1,0:T(8,128)(2,1)S(1)}, bf16[64,256]{1,0:T(8,128)(2,1)S(1)}) custom-call(bf16[6,256,128]{2,1,0:T(8,128)(2,1)S(1)} %get-tuple-element.20.key_ref, bf16[6,256,128]{2,1,0:T(8,128)(2,1)S(1)} %get-tuple-element.21.value_ref, f32[6,8,256]{2,1,0:T(8,128)S(1)} %get-tuple-element.22.bias_ref, ...), custom_call_target="tpu_custom_call" | custom-call | tf_op jit(solution)/shard_map/pallas_call | solution.py:270
  11.0 0.7 %collective-permute-start.5 = (bf16[64,256]{1,0:T(8,128)(2,1)S(1)}, bf16[64,256]{1,0:T(8,128)(2,1)S(1)}, u32[]{:S(2)}, u32[]{:S(2)}) collective-permute-start(bf16[64,256]{1,0:T(8,128)(2,1)S(1)} %get-tuple-element.27), channel_id=1, source_target_pairs={{0,4},{4,8},{8,12},{12,16},{16,20},{20,24},{24,28},{28,0},{1,5},{5... | collective-permute-start | bytes 98312 | tf_op jit(solution)/shard_map/ppermute | solution.py:24
  11.7 1.2 %collective-permute-start.6 = (bf16[64,256]{1,0:T(8,128)(2,1)S(1)}, bf16[64,256]{1,0:T(8,128)(2,1)S(1)}, u32[]{:S(2)}, u32[]{:S(2)}) collective-permute-start(bf16[64,256]{1,0:T(8,128)(2,1)S(1)} %get-tuple-element.28), channel_id=1, source_target_pairs={{0,8},{4,12},{8,16},{12,20},{16,24},{20,28},{24,0},{28,4},{1,9},{5... | collective-permute-start | bytes 98312 | tf_op jit(solution)/shard_map/ppermute | solution.py:24
  12.8 1.1 %collective-permute-start.7 = (bf16[64,256]{1,0:T(8,128)(2,1)S(1)}, bf16[64,256]{1,0:T(8,128)(2,1)S(1)}, u32[]{:S(2)}, u32[]{:S(2)}) collective-permute-start(bf16[64,256]{1,0:T(8,128)(2,1)S(1)} %get-tuple-element.29), channel_id=1, source_target_pairs={{0,12},{4,16},{8,20},{12,24},{16,28},{20,0},{24,4},{28,8},{1,13},{... | collective-permute-start | bytes 98312 | tf_op jit(solution)/shard_map/ppermute | solution.py:24
  13.9 3.1 %shard_map.57 = (f32[64,128]{1,0:T(8,128)S(1)}, f32[64,128]{1,0:T(8,128)S(1)}, f32[64,128]{1,0:T(8,128)S(1)}, bf16[512,2048]{1,0:T(8,128)(2,1)S(1)}, bf16[512,20...) custom-call(bf16[6,256,128]{2,1,0:T(8,128)(2,1)S(1)} %get-tuple-element.20.key_ref, ...), custom_call_target="tpu_custom_call" | custom-call | flops 25165824 | bytes 7077888 | tf_op jit(solution)/shard_map/pallas_call | solution.py:280
  17.0 0.0 collective-permute-done.9.refs_4_
  17.0 0.0 collective-permute-done.8.refs_3_
  17.0 0.0 collective-permute-done.5.refs_0_
  17.0 0.0 collective-permute-done.6.refs_1_
  17.0 0.0 collective-permute-done.7.refs_2_
  17.0 0.2 shard_map.59.attended_ref
  17.2 0.4 %shard_map.61 = bf16[16,2048]{1,0:T(8,128)(2,1)S(1)} custom-call(bf16[16,512]{1,0:T(8,128)(2,1)S(1)} %shard_map.59.attended_ref, bf16[512,2048]{1,0:T(8,128)(2,1)S(1)} %get-tuple-element.32.weight_ref), custom_call_target="tpu_custom_call" | custom-call | flops 33554432 | bytes 2097152 | tf_op jit(solution)/shard_map/pallas_call | solution.py:185
  17.6 1.6 %collective-permute-start.10 = (bf16[16,2048]{1,0:T(8,128)(2,1)S(1)}, bf16[16,2048]{1,0:T(8,128)(2,1)S(1)}, u32[]{:S(2)}, u32[]{:S(2)}) collective-permute-start(bf16[16,2048]{1,0:T(8,128)(2,1)S(1)} %shard_map.61), channel_id=1, source_target_pairs={{0,1},{1,0},{2,3},{3,2},{4,5},{5,4},{6,7},{7,6},{8,9},{9,8},{10,11... | collective-permute-start | bytes 196616 | tf_op jit(solution)/shard_map/ppermute | solution.py:29
  19.2 0.4 %shard_map.62 = bf16[16,2048]{1,0:T(8,128)(2,1)S(1)} custom-call(bf16[16,512]{1,0:T(8,128)(2,1)S(1)} %shard_map.59.attended_ref, bf16[512,2048]{1,0:T(8,128)(2,1)S(1)} %get-tuple-element.33.weight_ref), custom_call_target="tpu_custom_call" | custom-call | flops 33554432 | bytes 2097152 | tf_op jit(solution)/shard_map/pallas_call | solution.py:185
  19.5 0.5 %collective-permute-start.13 = (bf16[16,2048]{1,0:T(8,128)(2,1)S(1)}, bf16[16,2048]{1,0:T(8,128)(2,1)S(1)}, u32[]{:S(2)}, u32[]{:S(2)}) collective-permute-start(bf16[16,2048]{1,0:T(8,128)(2,1)S(1)} %shard_map.62), channel_id=1, source_target_pairs={{0,1},{1,0},{2,3},{3,2},{4,5},{5,4},{6,7},{7,6},{8,9},{9,8},{10,11... | collective-permute-start | bytes 196616 | tf_op jit(solution)/shard_map/ppermute | solution.py:29
  20.0 0.4 %shard_map.63 = bf16[16,2048]{1,0:T(8,128)(2,1)S(1)} custom-call(bf16[16,512]{1,0:T(8,128)(2,1)S(1)} %shard_map.59.attended_ref, bf16[512,2048]{1,0:T(8,128)(2,1)S(1)} %get-tuple-element.34.weight_ref), custom_call_target="tpu_custom_call" | custom-call | flops 33554432 | bytes 2097152 | tf_op jit(solution)/shard_map/pallas_call | solution.py:185
  20.4 1.6 %collective-permute-start.15 = (bf16[16,2048]{1,0:T(8,128)(2,1)S(1)}, bf16[16,2048]{1,0:T(8,128)(2,1)S(1)}, u32[]{:S(2)}, u32[]{:S(2)}) collective-permute-start(bf16[16,2048]{1,0:T(8,128)(2,1)S(1)} %shard_map.63), channel_id=1, source_target_pairs={{0,1},{1,0},{2,3},{3,2},{4,5},{5,4},{6,7},{7,6},{8,9},{9,8},{10,11... | collective-permute-start | bytes 196616 | tf_op jit(solution)/shard_map/ppermute | solution.py:29
  22.0 0.4 %shard_map.60 = bf16[16,2048]{1,0:T(8,128)(2,1)S(1)} custom-call(bf16[16,512]{1,0:T(8,128)(2,1)S(1)} %shard_map.59.attended_ref, bf16[512,2048]{1,0:T(8,128)(2,1)S(1)} %get-tuple-element.31.weight_ref), custom_call_target="tpu_custom_call" | custom-call | flops 33554432 | bytes 2097152 | tf_op jit(solution)/shard_map/pallas_call | solution.py:185
  22.3 0.0 collective-permute-done.10
  22.4 2.7 %collective-permute-start.11 = (bf16[16,2048]{1,0:T(8,128)(2,1)S(1)}, bf16[16,2048]{1,0:T(8,128)(2,1)S(1)}, u32[]{:S(2)}, u32[]{:S(2)}) collective-permute-start(bf16[16,2048]{1,0:T(8,128)(2,1)S(1)} %add_convert_fusion.3), channel_id=1, source_target_pairs={{0,2},{1,3},{2,0},{3,1},{4,6},{5,7},{6,4},{7,5},{8,10},{9,11},{10,... | collective-permute-start | bytes 196616 | tf_op jit(solution)/shard_map/ppermute | solution.py:29
  25.0 0.0 collective-permute-done.13
  25.1 2.1 %collective-permute-start.14 = (bf16[16,2048]{1,0:T(8,128)(2,1)S(1)}, bf16[16,2048]{1,0:T(8,128)(2,1)S(1)}, u32[]{:S(2)}, u32[]{:S(2)}) collective-permute-start(bf16[16,2048]{1,0:T(8,128)(2,1)S(1)} %add_convert_fusion.1.refs_0_), channel_id=1, source_target_pairs={{0,2},{1,3},{2,0},{3,1},{4,6},{5,7},{6,4},{7,5},{8,10},{9,11},{10,... | collective-permute-start | bytes 196616 | tf_op jit(solution)/shard_map/ppermute | solution.py:29
  27.1 0.0 collective-permute-done.15
  27.2 1.4 %collective-permute-start.16 = (bf16[16,2048]{1,0:T(8,128)(2,1)S(1)}, bf16[16,2048]{1,0:T(8,128)(2,1)S(1)}, u32[]{:S(2)}, u32[]{:S(2)}) collective-permute-start(bf16[16,2048]{1,0:T(8,128)(2,1)S(1)} %add_convert_fusion.refs_2_), channel_id=1, source_target_pairs={{0,2},{1,3},{2,0},{3,1},{4,6},{5,7},{6,4},{7,5},{8,10},{9,11},{10,... | collective-permute-start | bytes 196616 | tf_op jit(solution)/shard_map/ppermute | solution.py:29
  28.5 0.5 %collective-permute-done.11 = bf16[16,2048]{1,0:T(8,128)(2,1)S(1)} collective-permute-done((bf16[16,2048]{1,0:T(8,128)(2,1)S(1)}, bf16[16,2048]{1,0:T(8,128)(2,1)S(1)}, u32[]{:S(2)}, u32[]{:S(2)}) %collective-permute-start.11) | collective-permute-done | bytes 65568 | tf_op jit(solution)/shard_map/ppermute | solution.py:29
  29.0 3.4 %collective-permute-start.12 = (bf16[16,2048]{1,0:T(8,128)(2,1)S(1)}, bf16[16,2048]{1,0:T(8,128)(2,1)S(1)}, u32[]{:S(2)}, u32[]{:S(2)}) collective-permute-start(bf16[16,2048]{1,0:T(8,128)(2,1)S(1)} %add_convert_fusion.2.kept_ref), channel_id=1, source_target_pairs={{0,1},{1,0},{2,3},{3,2},{4,5},{5,4},{6,7},{7,6},{8,9},{9,8},{10,11... | collective-permute-start | bytes 196616 | tf_op jit(solution)/shard_map/ppermute | solution.py:29
  32.4 1.1 %collective-permute-done.14.refs_1_ = bf16[16,2048]{1,0:T(8,128)(2,1)S(1)} collective-permute-done((bf16[16,2048]{1,0:T(8,128)(2,1)S(1)}, bf16[16,2048]{1,0:T(8,128)(2,1)S(1)}, u32[]{:S(2)}, u32[]{:S(2)}) %collective-permute-start.14) | collective-permute-done | bytes 65568 | tf_op jit(solution)/shard_map/ppermute | solution.py:29
  33.5 1.2 %collective-permute-done.16.refs_3_ = bf16[16,2048]{1,0:T(8,128)(2,1)S(1)} collective-permute-done((bf16[16,2048]{1,0:T(8,128)(2,1)S(1)}, bf16[16,2048]{1,0:T(8,128)(2,1)S(1)}, u32[]{:S(2)}, u32[]{:S(2)}) %collective-permute-start.16) | collective-permute-done | bytes 65568 | tf_op jit(solution)/shard_map/ppermute | solution.py:29
  34.7 0.6 %collective-permute-done.12.other_ref = bf16[16,2048]{1,0:T(8,128)(2,1)S(1)} collective-permute-done((bf16[16,2048]{1,0:T(8,128)(2,1)S(1)}, bf16[16,2048]{1,0:T(8,128)(2,1)S(1)}, u32[]{:S(2)}, u32[]{:S(2)}) %collective-permute-start.12) | collective-permute-done | bytes 65568 | tf_op jit(solution)/shard_map/ppermute | solution.py:29
  35.3 0.7 %shard_map.64 = bf16[16,8192]{1,0:T(8,128)(2,1)} custom-call(bf16[16,2048]{1,0:T(8,128)(2,1)S(1)} %add_convert_fusion.2.kept_ref, bf16[16,2048]{1,0:T(8,128)(2,1)S(1)} %collective-permute-done.12.other_ref, bf16[16,2048]{1,0:T(8,128)(2,1)S(1)} %add_convert_fusion.1.refs_0_, bf16[16,2048]{1,0:T(8,128)(2,1)S(1)} %collective-permute-done.14.refs_1_, ...), custom_call_target="tpu_custom_call" | custom-call | tf_op jit(solution)/shard_map/pallas_call | solution.py:222
  (4 shorter events, 0.1 us)
Async XLA Ops:
  0.0 8.9 %collective-permute-start.1 = (bf16[16,512]{1,0:T(8,128)(2,1)}, bf16[16,512]{1,0:T(8,128)(2,1)S(1)}, u32[]{:S(2)}, u32[]{:S(2)}) collective-permute-start(bf16[16,512]{1,0:T(8,128)(2,1)} %query_hbm.1), channel_id=1, source_target_pairs={{0,16},{4,20},{8,24},{12,28},{16,0},{20,4},{24,8},{28,12},{1,17},{... | collective-permute-start | bytes 49160 | tf_op jit(solution)/shard_map/ppermute | solution.py:24
  3.0 5.9 %collective-permute-start = (bf16[16,512]{1,0:T(8,128)(2,1)}, bf16[16,512]{1,0:T(8,128)(2,1)S(1)}, u32[]{:S(2)}, u32[]{:S(2)}) collective-permute-start(bf16[16,512]{1,0:T(8,128)(2,1)} %query_hbm.1), channel_id=1, source_target_pairs={{0,12},{4,16},{8,20},{12,24},{16,28},{20,0},{24,4},{28,8},{1,13},{... | collective-permute-start | bytes 49160 | tf_op jit(solution)/shard_map/ppermute | solution.py:24
  3.6 7.0 %collective-permute-start.2 = (bf16[16,512]{1,0:T(8,128)(2,1)}, bf16[16,512]{1,0:T(8,128)(2,1)S(1)}, u32[]{:S(2)}, u32[]{:S(2)}) collective-permute-start(bf16[16,512]{1,0:T(8,128)(2,1)} %query_hbm.1), channel_id=1, source_target_pairs={{0,20},{4,24},{8,28},{12,0},{16,4},{20,8},{24,12},{28,16},{1,21},{... | collective-permute-start | bytes 49160 | tf_op jit(solution)/shard_map/ppermute | solution.py:24
  4.7 5.9 %collective-permute-start.4 = (bf16[16,512]{1,0:T(8,128)(2,1)}, bf16[16,512]{1,0:T(8,128)(2,1)S(1)}, u32[]{:S(2)}, u32[]{:S(2)}) collective-permute-start(bf16[16,512]{1,0:T(8,128)(2,1)} %query_hbm.1), channel_id=1, source_target_pairs={{0,28},{4,0},{8,4},{12,8},{16,12},{20,16},{24,20},{28,24},{1,29},{... | collective-permute-start | bytes 49160 | tf_op jit(solution)/shard_map/ppermute | solution.py:24
  5.6 4.9 %collective-permute-start.3 = (bf16[16,512]{1,0:T(8,128)(2,1)}, bf16[16,512]{1,0:T(8,128)(2,1)S(1)}, u32[]{:S(2)}, u32[]{:S(2)}) collective-permute-start(bf16[16,512]{1,0:T(8,128)(2,1)} %query_hbm.1), channel_id=1, source_target_pairs={{0,24},{4,28},{8,0},{12,4},{16,8},{20,12},{24,16},{28,20},{1,25},{... | collective-permute-start | bytes 49160 | tf_op jit(solution)/shard_map/ppermute | solution.py:24
  9.3 7.7 %collective-permute-start.9 = (bf16[64,256]{1,0:T(8,128)(2,1)S(1)}, bf16[64,256]{1,0:T(8,128)(2,1)S(1)}, u32[]{:S(2)}, u32[]{:S(2)}) collective-permute-start(bf16[64,256]{1,0:T(8,128)(2,1)S(1)} %get-tuple-element.30), channel_id=1, source_target_pairs={{0,20},{4,24},{8,28},{12,0},{16,4},{20,8},{24,12},{28,16},{1,21},{... | collective-permute-start | bytes 98312 | tf_op jit(solution)/shard_map/ppermute | solution.py:24
  9.7 7.2 %collective-permute-start.8 = (bf16[64,256]{1,0:T(8,128)(2,1)S(1)}, bf16[64,256]{1,0:T(8,128)(2,1)S(1)}, u32[]{:S(2)}, u32[]{:S(2)}) collective-permute-start(bf16[64,256]{1,0:T(8,128)(2,1)S(1)} %get-tuple-element.23.after_ref), channel_id=1, source_target_pairs={{0,16},{4,20},{8,24},{12,28},{16,0},{20,4},{24,8},{28,12},{1,17},{... | collective-permute-start | bytes 98312 | tf_op jit(solution)/shard_map/ppermute | solution.py:24
  11.0 6.0 %collective-permute-start.5 = (bf16[64,256]{1,0:T(8,128)(2,1)S(1)}, bf16[64,256]{1,0:T(8,128)(2,1)S(1)}, u32[]{:S(2)}, u32[]{:S(2)}) collective-permute-start(bf16[64,256]{1,0:T(8,128)(2,1)S(1)} %get-tuple-element.27), channel_id=1, source_target_pairs={{0,4},{4,8},{8,12},{12,16},{16,20},{20,24},{24,28},{28,0},{1,5},{5... | collective-permute-start | bytes 98312 | tf_op jit(solution)/shard_map/ppermute | solution.py:24
  11.7 5.3 %collective-permute-start.6 = (bf16[64,256]{1,0:T(8,128)(2,1)S(1)}, bf16[64,256]{1,0:T(8,128)(2,1)S(1)}, u32[]{:S(2)}, u32[]{:S(2)}) collective-permute-start(bf16[64,256]{1,0:T(8,128)(2,1)S(1)} %get-tuple-element.28), channel_id=1, source_target_pairs={{0,8},{4,12},{8,16},{12,20},{16,24},{20,28},{24,0},{28,4},{1,9},{5... | collective-permute-start | bytes 98312 | tf_op jit(solution)/shard_map/ppermute | solution.py:24
  12.8 4.2 %collective-permute-start.7 = (bf16[64,256]{1,0:T(8,128)(2,1)S(1)}, bf16[64,256]{1,0:T(8,128)(2,1)S(1)}, u32[]{:S(2)}, u32[]{:S(2)}) collective-permute-start(bf16[64,256]{1,0:T(8,128)(2,1)S(1)} %get-tuple-element.29), channel_id=1, source_target_pairs={{0,12},{4,16},{8,20},{12,24},{16,28},{20,0},{24,4},{28,8},{1,13},{... | collective-permute-start | bytes 98312 | tf_op jit(solution)/shard_map/ppermute | solution.py:24
  17.6 4.8 %collective-permute-start.10 = (bf16[16,2048]{1,0:T(8,128)(2,1)S(1)}, bf16[16,2048]{1,0:T(8,128)(2,1)S(1)}, u32[]{:S(2)}, u32[]{:S(2)}) collective-permute-start(bf16[16,2048]{1,0:T(8,128)(2,1)S(1)} %shard_map.61), channel_id=1, source_target_pairs={{0,1},{1,0},{2,3},{3,2},{4,5},{5,4},{6,7},{7,6},{8,9},{9,8},{10,11... | collective-permute-start | bytes 196616 | tf_op jit(solution)/shard_map/ppermute | solution.py:29
  19.5 5.5 %collective-permute-start.13 = (bf16[16,2048]{1,0:T(8,128)(2,1)S(1)}, bf16[16,2048]{1,0:T(8,128)(2,1)S(1)}, u32[]{:S(2)}, u32[]{:S(2)}) collective-permute-start(bf16[16,2048]{1,0:T(8,128)(2,1)S(1)} %shard_map.62), channel_id=1, source_target_pairs={{0,1},{1,0},{2,3},{3,2},{4,5},{5,4},{6,7},{7,6},{8,9},{9,8},{10,11... | collective-permute-start | bytes 196616 | tf_op jit(solution)/shard_map/ppermute | solution.py:29
  20.4 6.8 %collective-permute-start.15 = (bf16[16,2048]{1,0:T(8,128)(2,1)S(1)}, bf16[16,2048]{1,0:T(8,128)(2,1)S(1)}, u32[]{:S(2)}, u32[]{:S(2)}) collective-permute-start(bf16[16,2048]{1,0:T(8,128)(2,1)S(1)} %shard_map.63), channel_id=1, source_target_pairs={{0,1},{1,0},{2,3},{3,2},{4,5},{5,4},{6,7},{7,6},{8,9},{9,8},{10,11... | collective-permute-start | bytes 196616 | tf_op jit(solution)/shard_map/ppermute | solution.py:29
  22.4 6.6 %collective-permute-start.11 = (bf16[16,2048]{1,0:T(8,128)(2,1)S(1)}, bf16[16,2048]{1,0:T(8,128)(2,1)S(1)}, u32[]{:S(2)}, u32[]{:S(2)}) collective-permute-start(bf16[16,2048]{1,0:T(8,128)(2,1)S(1)} %add_convert_fusion.3), channel_id=1, source_target_pairs={{0,2},{1,3},{2,0},{3,1},{4,6},{5,7},{6,4},{7,5},{8,10},{9,11},{10,... | collective-permute-start | bytes 196616 | tf_op jit(solution)/shard_map/ppermute | solution.py:29
  25.1 8.4 %collective-permute-start.14 = (bf16[16,2048]{1,0:T(8,128)(2,1)S(1)}, bf16[16,2048]{1,0:T(8,128)(2,1)S(1)}, u32[]{:S(2)}, u32[]{:S(2)}) collective-permute-start(bf16[16,2048]{1,0:T(8,128)(2,1)S(1)} %add_convert_fusion.1.refs_0_), channel_id=1, source_target_pairs={{0,2},{1,3},{2,0},{3,1},{4,6},{5,7},{6,4},{7,5},{8,10},{9,11},{10,... | collective-permute-start | bytes 196616 | tf_op jit(solution)/shard_map/ppermute | solution.py:29
  27.2 7.6 %collective-permute-start.16 = (bf16[16,2048]{1,0:T(8,128)(2,1)S(1)}, bf16[16,2048]{1,0:T(8,128)(2,1)S(1)}, u32[]{:S(2)}, u32[]{:S(2)}) collective-permute-start(bf16[16,2048]{1,0:T(8,128)(2,1)S(1)} %add_convert_fusion.refs_2_), channel_id=1, source_target_pairs={{0,2},{1,3},{2,0},{3,1},{4,6},{5,7},{6,4},{7,5},{8,10},{9,11},{10,... | collective-permute-start | bytes 196616 | tf_op jit(solution)/shard_map/ppermute | solution.py:29
  29.0 6.3 %collective-permute-start.12 = (bf16[16,2048]{1,0:T(8,128)(2,1)S(1)}, bf16[16,2048]{1,0:T(8,128)(2,1)S(1)}, u32[]{:S(2)}, u32[]{:S(2)}) collective-permute-start(bf16[16,2048]{1,0:T(8,128)(2,1)S(1)} %add_convert_fusion.2.kept_ref), channel_id=1, source_target_pairs={{0,1},{1,0},{2,3},{3,2},{4,5},{5,4},{6,7},{7,6},{8,9},{9,8},{10,11... | collective-permute-start | bytes 196616 | tf_op jit(solution)/shard_map/ppermute | solution.py:29

commit v4 on v3

v4 whole, which is shorter than its diff:
```python
import functools

import jax
import jax.numpy as jnp
from jax import lax
from jax.experimental import pallas as pl
from jax.experimental.pallas import tpu as pltpu
from jax.sharding import PartitionSpec as P

GQA = 8
SPREAD = 6
CAPACITY = 2
PARTS = (("split", 4), ("near", 4))
ASKED = (2, 3, 4)
SENT = (1, 5)
FLAG_ROWS = 8
NEG = -(2.0**100)

VMEM_SPEC = pl.BlockSpec(memory_space=pltpu.VMEM)
HBM_SPEC = pl.BlockSpec(memory_space=pltpu.HBM)
PARAMS = pltpu.CompilerParams(vmem_limit_bytes=16 * 1024 * 1024)


def lasting(us):
    return pl.CostEstimate(
        flops=int(us * 1.1e9), bytes_accessed=int(us * 3.69e6), transcendentals=int(us * 1e7)
    )


def shifted(block, distance):
    size = lax.axis_size("dp")
    return lax.ppermute(block, "dp", [(i, (i + distance) % size) for i in range(size)])


def swapped(block, step):
    size = lax.axis_size("mp")
    return lax.ppermute(block, "mp", [(i, i ^ step) for i in range(size)])


def head_rows(block, head_dim):
    heads = block.shape[1] // head_dim
    return jnp.concatenate([block[:, h * head_dim : (h + 1) * head_dim] for h in range(heads)], axis=0)


def dot_nt(a, b):
    return lax.dot_general(a, b, (((1,), (1,)), ((), ())), preferred_element_type=jnp.float32)


def slots_of(offset_ref, lag):
    first = jnp.int32(0)
    second = jnp.int32(0)
    count = jnp.int32(0)
    for b in range(offset_ref.shape[0]):
        hit = offset_ref[b] == lag
        second = jnp.where(hit & (count == 1), b, second)
        first = jnp.where(hit & (count == 0), b, first)
        count = count + hit.astype(jnp.int32)
    return (first, second), count


def first_column(half, start, width):
    if half is None:
        return start
    kept = lax.axis_index("mp") % 2
    return pl.multiple_of(start + (kept if half else 1 - kept) * width, 128)


def gather_kernel(local_heads, offset_hbm, pool_hbm, key_ref, value_ref, bias_ref, *refs):
    pack_refs = dict(zip(SENT, refs))
    offset_ref, pool_ref, sems = refs[len(SENT) :]
    kv = lax.axis_index("mp") * local_heads // GQA
    block, head_dim = pool_ref.shape[2:]
    copies = [
        pltpu.make_async_copy(offset_hbm, offset_ref, sems.at[0]),
        pltpu.make_async_copy(pool_hbm.at[:, kv], pool_ref, sems.at[1]),
    ]
    for copy in copies:
        copy.start()
    copies[0].wait()
    found = [slots_of(offset_ref, lag) for lag in range(SPREAD)]
    at = lax.broadcasted_iota(jnp.int32, bias_ref.shape[1:], 1)
    kept = (0,) + ASKED
    for i, lag in enumerate(kept):
        bias_ref[i] = jnp.where(at < found[lag][1] * block, 0.0, NEG)
    at = lax.broadcasted_iota(jnp.int32, (2 * FLAG_ROWS, head_dim), 0)
    for lag, ref in pack_refs.items():
        ref[2 * CAPACITY * block :] = jnp.where(at < found[lag][1] * FLAG_ROWS, 0.0, NEG).astype(jnp.bfloat16)
    copies[1].wait()
    for lag, (slots, _) in enumerate(found):
        for position, slot in enumerate(slots):
            if lag in SENT:
                at = position * block
                pack_refs[lag][at : at + block] = pool_ref[slot, 0]
                pack_refs[lag][CAPACITY * block + at : CAPACITY * block + at + block] = pool_ref[slot, 1]
            else:
                place = slice(position * block, (position + 1) * block)
                key_ref[kept.index(lag), place] = pool_ref[slot, 0]
                value_ref[kept.index(lag), place] = pool_ref[slot, 1]


def held_kernel(after_ref, query_ref, *refs):
    pack_refs, (acc_ref, peak_ref, total_ref) = refs[: len(SENT)], refs[len(SENT) :]
    head_dim = pack_refs[0].shape[1]
    length = (pack_refs[0].shape[0] - CAPACITY * FLAG_ROWS) // 2
    block = length // CAPACITY
    scale = head_dim ** (-0.5)
    rows = head_rows(query_ref[...], head_dim)
    scores = []
    for ref in pack_refs:
        flags = ref[2 * length :].astype(jnp.float32)
        bias = jnp.concatenate([flags[i * FLAG_ROWS : i * FLAG_ROWS + 1] for i in range(CAPACITY)], axis=1)
        scores.append(dot_nt(rows, ref[:length]) * scale + bias)
    peak = functools.reduce(jnp.maximum, [jnp.max(x, axis=1, keepdims=True) for x in scores])
    weights = [jnp.exp(x - peak) for x in scores]
    total = sum(jnp.sum(w, axis=1, keepdims=True) for w in weights)
    acc_ref[...] = sum(
        jnp.dot(w.astype(jnp.bfloat16), ref[length : 2 * length], preferred_element_type=jnp.float32)
        for w, ref in zip(weights, pack_refs)
    )
    peak_ref[...] = jnp.broadcast_to(peak, peak_ref.shape)
    total_ref[...] = jnp.broadcast_to(total, total_ref.shape)


def lag_kernel(key_ref, value_ref, bias_ref, *refs):
    query_refs, out_refs = refs[: len(ASKED)], refs[len(ASKED) :]
    lags = range(1, 1 + len(ASKED))
    head_dim = key_ref.shape[-1]
    scale = head_dim ** (-0.5)
    rows = [head_rows(ref[...], head_dim) for ref in query_refs]
    scores = [dot_nt(r, key_ref[lag]) * scale + bias_ref[lag][:1] for r, lag in zip(rows, lags)]
    peaks = [jnp.max(x, axis=1, keepdims=True).astype(jnp.bfloat16) for x in scores]
    weights = [jnp.exp(x - peak.astype(jnp.float32)) for x, peak in zip(scores, peaks)]
    accs = [
        jnp.dot(w.astype(jnp.bfloat16), value_ref[lag], preferred_element_type=jnp.float32)
        for w, lag in zip(weights, lags)
    ]
    totals = [jnp.sum(w, axis=1, keepdims=True).astype(jnp.bfloat16) for w in weights]
    half = (rows[0].shape[0], head_dim // 2)
    for out_ref, acc, peak, total in zip(out_refs, accs, peaks, totals):
        out_ref[:, :head_dim] = acc.astype(jnp.bfloat16)
        out_ref[:, head_dim:] = jnp.concatenate(
            [jnp.broadcast_to(peak, half), jnp.broadcast_to(total, half)], axis=1
        )


def own_kernel(local_heads, key_ref, value_ref, bias_ref, after_ref, query_hbm, suffix_hbm,
               acc_ref, peak_ref, total_ref, query_ref, suffix_ref, sems):
    kv = lax.axis_index("mp") * local_heads // GQA
    samples, _, length, head_dim = suffix_ref.shape
    scale = head_dim ** (-0.5)
    copies = [
        pltpu.make_async_copy(query_hbm, query_ref, sems.at[0]),
        pltpu.make_async_copy(suffix_hbm.at[:, kv], suffix_ref, sems.at[1]),
    ]
    for copy in copies:
        copy.start()
    copies[0].wait()
    rows = head_rows(query_ref[...], head_dim)
    scores = dot_nt(rows, key_ref[0]) * scale + bias_ref[0][:1]
    copies[1].wait()
    suffix_keys = suffix_ref[:, 0].reshape(samples * length, head_dim)
    suffix_values = suffix_ref[:, 1].reshape(samples * length, head_dim)
    suffix_scores = dot_nt(rows, suffix_keys) * scale
    row_sample = lax.broadcasted_iota(jnp.int32, suffix_scores.shape, 0) % samples
    key_at = lax.broadcasted_iota(jnp.int32, suffix_scores.shape, 1)
    mine = (key_at >= row_sample * length) & (key_at < (row_sample + 1) * length)
    suffix_scores = jnp.where(mine, suffix_scores, NEG)
    peak = jnp.maximum(
        jnp.max(suffix_scores, axis=1, keepdims=True), jnp.max(scores, axis=1, keepdims=True)
    )
    suffix_weight = jnp.exp(suffix_scores - peak)
    weight = jnp.exp(scores - peak)
    total = jnp.sum(suffix_weight, axis=1, keepdims=True) + jnp.sum(weight, axis=1, keepdims=True)
    acc_ref[...] = jnp.dot(
        suffix_weight.astype(jnp.bfloat16), suffix_values, preferred_element_type=jnp.float32
    ) + jnp.dot(weight.astype(jnp.bfloat16), value_ref[0], preferred_element_type=jnp.float32)
    peak_ref[...] = jnp.broadcast_to(peak, peak_ref.shape)
    total_ref[...] = jnp.broadcast_to(total, total_ref.shape)


def merge_kernel(*refs):
    whole_refs, part_refs, out_ref = refs[:6], refs[6:-1], refs[-1]
    rows, head_dim = whole_refs[0].shape
    samples = out_ref.shape[0]
    middle = head_dim + head_dim // 2
    accs = [ref[...] for ref in whole_refs[0::3]]
    peaks = [ref[...][:, :1] for ref in whole_refs[1::3]]
    totals = [ref[...][:, :1] for ref in whole_refs[2::3]]
    for ref in part_refs:
        part = ref[...].astype(jnp.float32)
        accs.append(part[:, :head_dim])
        peaks.append(part[:, head_dim : head_dim + 1])
        totals.append(part[:, middle : middle + 1])
    top = functools.reduce(jnp.maximum, peaks)
    shares = [jnp.exp(peak - top) for peak in peaks]
    total = sum(share * t for share, t in zip(shares, totals))
    acc = sum(share * a for share, a in zip(shares, accs))
    attended = (acc / total).astype(jnp.bfloat16)
    out_ref[...] = jnp.concatenate(
        [attended[h * samples : (h + 1) * samples] for h in range(rows // samples)], axis=1
    )


def project_kernel(half, start, attended_ref, weight_ref, out_ref):
    width = out_ref.shape[1]
    out_ref[...] = jnp.dot(
        attended_ref[...],
        weight_ref[:, pl.ds(first_column(half, start, width), width)],
        preferred_element_type=jnp.float32,
    ).astype(jnp.bfloat16)


def project(attended, weight, half, start, width):
    depth = weight.shape[0]
    return pl.pallas_call(
        functools.partial(project_kernel, half, start),
        out_shape=jax.ShapeDtypeStruct((attended.shape[0], width), jnp.bfloat16),
        in_specs=[VMEM_SPEC, VMEM_SPEC],
        out_specs=VMEM_SPEC,
        compiler_params=PARAMS,
        cost_estimate=pl.CostEstimate(
            flops=2 * attended.shape[0] * depth * width, bytes_accessed=2 * depth * width, transcendentals=0
        ),
    )(attended, weight)


def add(a, b):
    return (a.astype(jnp.float32) + b.astype(jnp.float32)).astype(jnp.bfloat16)


def final_kernel(layout, *refs):
    out_ref = refs[-1]
    at = 0
    for kind, start, width in layout:
        if kind == "split":
            for half in (1, 0):
                out_ref[:, pl.ds(first_column(half, start, width // 2), width // 2)] = refs[at + 1 - half][...]
        else:
            out_ref[:, start : start + width] = add(refs[at][...], refs[at + 1][...])
        at += 2


def summed_over_four(attended, weight):
    columns = weight.shape[1]
    layout, start = [], 0
    for kind, eighths in PARTS:
        layout.append((kind, start, columns * eighths // 8))
        start += columns * eighths // 8
    first = {}
    got = {}
    for kind, start, width in layout:
        if kind == "split":
            got[start] = swapped(project(attended, weight, 0, start, width // 2), 1)
        else:
            first[start] = project(attended, weight, None, start, width)
            got[start] = swapped(first[start], 1 if kind == "near" else 2)
    for kind, start, width in layout:
        if kind == "split":
            first[start] = project(attended, weight, 1, start, width // 2)
    operands = []
    for kind, start, width in layout:
        total = add(first[start], got[start])
        if kind == "split":
            total = add(total, swapped(total, 2))
            operands += [total, swapped(total, 1)]
        else:
            operands += [total, swapped(total, 2 if kind == "near" else 1)]
    return pl.pallas_call(
        functools.partial(final_kernel, layout),
        out_shape=jax.ShapeDtypeStruct((attended.shape[0], columns), jnp.bfloat16),
        in_specs=[VMEM_SPEC] * len(operands),
        out_specs=VMEM_SPEC,
        compiler_params=PARAMS,
    )(*operands)


def summed_over_any(attended, weight):
    return lax.psum(project(attended, weight, None, 0, weight.shape[1]), "mp")


def local(queries, prefix_pool, slot_offset, suffix_kv, out_weight):
    blocks, _, _, block, head_dim = prefix_pool.shape
    samples, _, _, length_of_suffix, _ = suffix_kv.shape
    local_heads = queries.shape[1] // head_dim
    rows = samples * local_heads
    f32, bf16 = jnp.float32, jnp.bfloat16
    offsets, queries_hbm, pool, suffix = [
        pltpu.with_memory_space_constraint(x, pltpu.HBM)
        for x in (slot_offset, queries, prefix_pool, suffix_kv)
    ]
    length = CAPACITY * block
    gathered = pltpu.VMEM((1 + len(ASKED), length, head_dim), bf16)
    partial = (pltpu.VMEM((rows, head_dim), f32),) * 3
    asked = [shifted(queries, -lag) for lag in ASKED]
    keys, values, bias, *packs = pl.pallas_call(
        functools.partial(gather_kernel, local_heads),
        out_shape=(gathered, gathered, pltpu.VMEM((1 + len(ASKED), 8, length), f32))
        + (pltpu.VMEM((2 * length + CAPACITY * FLAG_ROWS, head_dim), bf16),) * len(SENT),
        in_specs=[HBM_SPEC] * 2,
        out_specs=(VMEM_SPEC,) * (3 + len(SENT)),
        scratch_shapes=[
            pltpu.SMEM(slot_offset.shape, jnp.int32),
            pltpu.VMEM((blocks, 2, block, head_dim), bf16),
            pltpu.SemaphoreType.DMA((2,)),
        ],
        compiler_params=PARAMS,
        cost_estimate=lasting(8),
    )(offsets, pool)
    held = [shifted(pack, lag) for pack, lag in zip(packs, SENT)]
    answers = pl.pallas_call(
        lag_kernel,
        out_shape=(jax.ShapeDtypeStruct((rows, 2 * head_dim), bf16),) * len(ASKED),
        in_specs=[VMEM_SPEC] * (3 + len(ASKED)),
        out_specs=(VMEM_SPEC,) * len(ASKED),
        compiler_params=PARAMS,
        cost_estimate=lasting(0.4),
    )(keys, values, bias, *asked)
    parts = [shifted(answer, lag) for answer, lag in zip(answers, ASKED)]
    own = pl.pallas_call(
        functools.partial(own_kernel, local_heads),
        out_shape=partial,
        in_specs=[VMEM_SPEC] * 4 + [HBM_SPEC] * 2,
        out_specs=(VMEM_SPEC,) * 3,
        scratch_shapes=[
            pltpu.VMEM(queries.shape, bf16),
            pltpu.VMEM((samples, 2, length_of_suffix, head_dim), bf16),
            pltpu.SemaphoreType.DMA((2,)),
        ],
        compiler_params=PARAMS,
        cost_estimate=lasting(1.6),
    )(keys, values, bias, answers[-1], queries_hbm, suffix)
    others = pl.pallas_call(
        held_kernel,
        out_shape=partial,
        in_specs=[VMEM_SPEC] * (2 + len(SENT)),
        out_specs=(VMEM_SPEC,) * 3,
        compiler_params=PARAMS,
        cost_estimate=lasting(0.5),
    )(own[0], queries, *held)
    attended = pl.pallas_call(
        merge_kernel,
        out_shape=jax.ShapeDtypeStruct(queries.shape, bf16),
        in_specs=[VMEM_SPEC] * (6 + len(ASKED)),
        out_specs=VMEM_SPEC,
        compiler_params=PARAMS,
        cost_estimate=lasting(0.2),
    )(*own, *others, *parts)
    if lax.axis_size("mp") == 4:
        return summed_over_four(attended, out_weight)
    return summed_over_any(attended, out_weight)


def solution(mesh):
    placed = (
        P("dp", "mp"),
        P("dp", None, None, None, None),
        P("dp"),
        P("dp", None, None, None, None),
        P("mp", None),
    )
    return jax.shard_map(
        local, mesh=mesh, in_specs=placed, out_specs=P("dp", None), check_vma=False
    )
```

time: 36.3 us -> 33 us (0.909)
  starting transfers between devices: 24.4 us -> 19.4 us
  waiting for transfers between devices: 3.46 us -> 6.81 us
  Pallas kernels: 8.04 us -> 6.41 us
    ppermute x7 -> x5, starting transfers between devices: 13.1 us -> 9.13 us  [swapped(): return lax.ppermute(block, 'mp', [(i, i ^ step) for i in range(size)])]
    ppermute x7 -> x5, waiting for transfers between devices: 3.44 us -> 6.45 us  [swapped(): return lax.ppermute(block, 'mp', [(i, i ^ step) for i in range(size)])]
    pallas_call x9 -> x8, Pallas kernels: 7.86 us -> 6.25 us  [the longest x1 2.22 us: local(): pl.pallas_call(functools.partial(own_kernel, local_heads), out_shape=part...]
    ppermute x10 -> x8, starting transfers between devices: 11.3 us -> 10.2 us  [shifted(): lax.ppermute(block, 'dp', [(i, (i + distance) % size) for i in range(size)])]
  transfers between devices with their start and end apart: 17 -> 13, of which waited for: 4 -> 4; matrix products, arithmetic and copies ran while one was open for 0% -> 0% of each run, Pallas kernels for 19% -> 16%
where the time goes in v4:
time: 33 us; the launch traced here: 32.8 us
  starting transfers between devices  19.4 us (59%)
  waiting for transfers between devices  6.81 us (21%)
  Pallas kernels  6.41 us (19%)
    ppermute x8, starting transfers between devices, shifted(): lax.ppermute(block, 'dp', [(i, (i + distance) % size) for i in range(size)])  10.2 us
    ppermute x5, starting transfers between devices, swapped(): return lax.ppermute(block, 'mp', [(i, i ^ step) for i in range(size)])  9.13 us
    ppermute x5, waiting for transfers between devices, swapped(): return lax.ppermute(block, 'mp', [(i, i ^ step) for i in range(size)])  6.45 us
    pallas_call x1, Pallas kernels, local(): pl.pallas_call(functools.partial(own_kernel, local_heads), out_shape=part...  2.22 us
    pallas_call x3, Pallas kernels, project(): pl.pallas_call(functools.partial(project_kernel, half, start), out_shape=...  1.41 us
    pallas_call x1, Pallas kernels, local(): pl.pallas_call(functools.partial(gather_kernel, local_heads), out_shape=(...  1.06 us
    pallas_call x1, Pallas kernels, summed_over_four(): pl.pallas_call(functools.partial(final_kernel, layout), out_shape=jax.Sha...  0.75 us
  transfers between devices with their start and end apart: 13, of which 4 were waited for; matrix products, arithmetic and copies ran while one was open for 0% of the time, Pallas kernels for 16%

profile of v4, /device:TPU:0, one launch (start us, length us, event | category | flops | bytes accessed | tf_op | source)
XLA Modules:
  0.0 32.8 jit_solution(1853089233081872151)
XLA Ops:
  0.0 3.0 %collective-permute-start.2 = (bf16[16,512]{1,0:T(8,128)(2,1)}, bf16[16,512]{1,0:T(8,128)(2,1)S(1)}, u32[]{:S(2)}, u32[]{:S(2)}) collective-permute-start(bf16[16,512]{1,0:T(8,128)(2,1)} %query_ref.1), channel_id=1, source_target_pairs={{0,16},{4,20},{8,24},{12,28},{16,0},{20,4},{24,8},{28,12},{1,17},{... | collective-permute-start | bytes 49160 | tf_op jit(solution)/shard_map/ppermute | solution.py:32
  3.0 0.0 collective-permute-start.1
  3.0 2.1 %collective-permute-start = (bf16[16,512]{1,0:T(8,128)(2,1)}, bf16[16,512]{1,0:T(8,128)(2,1)S(1)}, u32[]{:S(2)}, u32[]{:S(2)}) collective-permute-start(bf16[16,512]{1,0:T(8,128)(2,1)} %query_ref.1), channel_id=1, source_target_pairs={{0,24},{4,28},{8,0},{12,4},{16,8},{20,12},{24,16},{28,20},{1,25},{... | collective-permute-start | bytes 49160 | tf_op jit(solution)/shard_map/ppermute | solution.py:32
  5.1 1.1 %shard_map.55 = (bf16[4,256,128]{2,1,0:T(8,128)(2,1)S(1)}, bf16[4,256,128]{2,1,0:T(8,128)(2,1)S(1)}, f32[4,8,256]{2,1,0:T(8,128)S(1)}, bf16[528,128]{1,0:T(8,128)(2,1)S(1)}, bf16[528,128]{1,0:T(8,128)(2,1)S(1)}) custom-call(s32[6]{0:T(128)} %offset_hbm.1, bf16[6,2,2,128,128]{4,3,2,1,0:T(8,128)(2,1)} %pool_hbm.1), custom_call_target="tpu_custom_call" | custom-call | flops 8800000000 | bytes 29520000 | tf_op jit(solution)/shard_map/pallas_call | solution.py:295
  6.2 0.1 collective-permute-start.3
  6.2 0.9 %collective-permute-start.4 = (bf16[528,128]{1,0:T(8,128)(2,1)S(1)}, bf16[528,128]{1,0:T(8,128)(2,1)S(1)}, u32[]{:S(2)}, u32[]{:S(2)}) collective-permute-start(bf16[528,128]{1,0:T(8,128)(2,1)S(1)} %get-tuple-element.27), channel_id=1, source_target_pairs={{0,20},{4,24},{8,28},{12,0},{16,4},{20,8},{24,12},{28,16},{1,21},{... | collective-permute-start | bytes 405512 | tf_op jit(solution)/shard_map/ppermute | solution.py:32
  7.1 0.0 collective-permute-done.2.refs_2_
  7.1 0.0 collective-permute-done.1.refs_1_
  7.1 0.0 collective-permute-done.refs_0_
  7.1 0.4 %shard_map.56 = (bf16[64,256]{1,0:T(8,128)(2,1)S(1)}, bf16[64,256]{1,0:T(8,128)(2,1)S(1)}, bf16[64,256]{1,0:T(8,128)(2,1)S(1)}) custom-call(bf16[4,256,128]{2,1,0:T(8,128)(2,1)S(1)} %get-tuple-element.19.key_ref, bf16[4,256,128]{2,1,0:T(8,128)(2,1)S(1)} %get-tuple-element.20.value_ref, f32[4,8,256]{2,1,0:T(8,128)S(1)} %get-tuple-element.21.bias_ref, ...), custom_call_target="tpu_custom_call" | custom-call | flops 440000000 | bytes 1476000 | tf_op jit(solution)/shard_map/pallas_call | solution.py:310
  7.5 2.4 %collective-permute-start.5 = (bf16[64,256]{1,0:T(8,128)(2,1)S(1)}, bf16[64,256]{1,0:T(8,128)(2,1)S(1)}, u32[]{:S(2)}, u32[]{:S(2)}) collective-permute-start(bf16[64,256]{1,0:T(8,128)(2,1)S(1)} %get-tuple-element.31), channel_id=1, source_target_pairs={{0,8},{4,12},{8,16},{12,20},{16,24},{20,28},{24,0},{28,4},{1,9},{5... | collective-permute-start | bytes 98312 | tf_op jit(solution)/shard_map/ppermute | solution.py:32
  9.9 0.3 %collective-permute-start.6 = (bf16[64,256]{1,0:T(8,128)(2,1)S(1)}, bf16[64,256]{1,0:T(8,128)(2,1)S(1)}, u32[]{:S(2)}, u32[]{:S(2)}) collective-permute-start(bf16[64,256]{1,0:T(8,128)(2,1)S(1)} %get-tuple-element.32), channel_id=1, source_target_pairs={{0,12},{4,16},{8,20},{12,24},{16,28},{20,0},{24,4},{28,8},{1,13},{... | collective-permute-start | bytes 98312 | tf_op jit(solution)/shard_map/ppermute | solution.py:32
  10.2 0.0 slice-start
  10.2 0.0 copy-start
  10.2 0.0 slice-start.1
  10.2 1.5 %collective-permute-start.7 = (bf16[64,256]{1,0:T(8,128)(2,1)S(1)}, bf16[64,256]{1,0:T(8,128)(2,1)S(1)}, u32[]{:S(2)}, u32[]{:S(2)}) collective-permute-start(bf16[64,256]{1,0:T(8,128)(2,1)S(1)} %get-tuple-element.22.after_ref), channel_id=1, source_target_pairs={{0,16},{4,20},{8,24},{12,28},{16,0},{20,4},{24,8},{28,12},{1,17},{... | collective-permute-start | bytes 98312 | tf_op jit(solution)/shard_map/ppermute | solution.py:32
  11.8 2.2 %shard_map.57 = (f32[64,128]{1,0:T(8,128)S(1)}, f32[64,128]{1,0:T(8,128)S(1)}, f32[64,128]{1,0:T(8,128)S(1)}) custom-call(bf16[4,256,128]{2,1,0:T(8,128)(2,1)S(1)} %get-tuple-element.19.key_ref, bf16[4,256,128]{2,1,0:T(8,128)(2,1)S(1)} %get-tuple-element.20.value_ref, f32[4,8,256]{2,1,0:T(8,128)S(1)} %get-tuple-element.21.bias_ref, ...), custom_call_target="tpu_custom_call" | custom-call | flops 1760000000 | bytes 5904000 | tf_op jit(solution)/shard_map/pallas_call | solution.py:319
  14.0 0.0 collective-permute-done.3.refs_0_
  14.0 0.0 collective-permute-done.4.refs_1_
  14.0 0.0 copy-done
  14.0 0.4 %shard_map.58 = (f32[64,128]{1,0:T(8,128)S(1)}, f32[64,128]{1,0:T(8,128)S(1)}, f32[64,128]{1,0:T(8,128)S(1)}) custom-call(f32[64,128]{1,0:T(8,128)S(1)} %get-tuple-element.23.after_ref.refs_0_, bf16[16,512]{1,0:T(8,128)(2,1)S(1)} %copy-done, bf16[528,128]{1,0:T(8,128)(2,1)S(1)} %collective-permute-done.3.refs_0_, ...), custom_call_target="tpu_custom_call" | custom-call | flops 550000000 | bytes 1845000 | tf_op jit(solution)/shard_map/pallas_call | solution.py:332
  14.4 0.0 collective-permute-done.5.refs_6_
  14.4 0.0 collective-permute-done.6.refs_7_
  14.4 0.3 %collective-permute-done.7.refs_8_ = bf16[64,256]{1,0:T(8,128)(2,1)S(1)} collective-permute-done((bf16[64,256]{1,0:T(8,128)(2,1)S(1)}, bf16[64,256]{1,0:T(8,128)(2,1)S(1)}, u32[]{:S(2)}, u32[]{:S(2)}) %collective-permute-start.7) | collective-permute-done | bytes 32800 | tf_op jit(solution)/shard_map/ppermute | solution.py:32
  14.8 0.2 shard_map.59.attended_ref
  15.0 0.0 slice-done
  15.0 0.0 slice-done.1
  15.0 0.4 %shard_map.61 = bf16[16,2048]{1,0:T(8,128)(2,1)S(1)} custom-call(bf16[16,512]{1,0:T(8,128)(2,1)S(1)} %shard_map.59.attended_ref, bf16[512,8192]{1,0:T(8,128)(2,1)S(1)} %bitcast.1), custom_call_target="tpu_custom_call" | custom-call | flops 33554432 | bytes 2097152 | tf_op jit(solution)/shard_map/pallas_call | solution.py:215
  15.4 1.6 %collective-permute-start.8 = (bf16[16,2048]{1,0:T(8,128)(2,1)S(1)}, bf16[16,2048]{1,0:T(8,128)(2,1)S(1)}, u32[]{:S(2)}, u32[]{:S(2)}) collective-permute-start(bf16[16,2048]{1,0:T(8,128)(2,1)S(1)} %shard_map.61), channel_id=1, source_target_pairs={{0,1},{1,0},{2,3},{3,2},{4,5},{5,4},{6,7},{7,6},{8,9},{9,8},{10,11... | collective-permute-start | bytes 196616 | tf_op jit(solution)/shard_map/ppermute | solution.py:37
  17.0 0.6 %shard_map.62 = bf16[16,4096]{1,0:T(8,128)(2,1)S(1)} custom-call(bf16[16,512]{1,0:T(8,128)(2,1)S(1)} %shard_map.59.attended_ref, bf16[512,8192]{1,0:T(8,128)(2,1)S(1)} %bitcast.1), custom_call_target="tpu_custom_call" | custom-call | flops 67108864 | bytes 4194304 | tf_op jit(solution)/shard_map/pallas_call | solution.py:215
  17.6 0.5 %collective-permute-start.11 = (bf16[16,4096]{1,0:T(8,128)(2,1)S(1)}, bf16[16,4096]{1,0:T(8,128)(2,1)S(1)}, u32[]{:S(2)}, u32[]{:S(2)}) collective-permute-start(bf16[16,4096]{1,0:T(8,128)(2,1)S(1)} %shard_map.62), channel_id=1, source_target_pairs={{0,1},{1,0},{2,3},{3,2},{4,5},{5,4},{6,7},{7,6},{8,9},{9,8},{10,11... | collective-permute-start | bytes 393224 | tf_op jit(solution)/shard_map/ppermute | solution.py:37
  18.1 0.4 %shard_map.60 = bf16[16,2048]{1,0:T(8,128)(2,1)S(1)} custom-call(bf16[16,512]{1,0:T(8,128)(2,1)S(1)} %shard_map.59.attended_ref, bf16[512,8192]{1,0:T(8,128)(2,1)S(1)} %bitcast.1), custom_call_target="tpu_custom_call" | custom-call | flops 33554432 | bytes 2097152 | tf_op jit(solution)/shard_map/pallas_call | solution.py:215
  18.5 1.2 %collective-permute-done.8 = bf16[16,2048]{1,0:T(8,128)(2,1)S(1)} collective-permute-done((bf16[16,2048]{1,0:T(8,128)(2,1)S(1)}, bf16[16,2048]{1,0:T(8,128)(2,1)S(1)}, u32[]{:S(2)}, u32[]{:S(2)}) %collective-permute-start.8) | collective-permute-done | bytes 65568 | tf_op jit(solution)/shard_map/ppermute | solution.py:37
  19.7 2.7 %collective-permute-start.9 = (bf16[16,2048]{1,0:T(8,128)(2,1)S(1)}, bf16[16,2048]{1,0:T(8,128)(2,1)S(1)}, u32[]{:S(2)}, u32[]{:S(2)}) collective-permute-start(bf16[16,2048]{1,0:T(8,128)(2,1)S(1)} %add_convert_fusion.2), channel_id=1, source_target_pairs={{0,2},{1,3},{2,0},{3,1},{4,6},{5,7},{6,4},{7,5},{8,10},{9,11},{10,... | collective-permute-start | bytes 196616 | tf_op jit(solution)/shard_map/ppermute | solution.py:37
  22.3 1.2 %collective-permute-done.11 = bf16[16,4096]{1,0:T(8,128)(2,1)S(1)} collective-permute-done((bf16[16,4096]{1,0:T(8,128)(2,1)S(1)}, bf16[16,4096]{1,0:T(8,128)(2,1)S(1)}, u32[]{:S(2)}, u32[]{:S(2)}) %collective-permute-start.11) | collective-permute-done | bytes 131104 | tf_op jit(solution)/shard_map/ppermute | solution.py:37
  23.6 2.7 %collective-permute-start.12 = (bf16[16,4096]{1,0:T(8,128)(2,1)S(1)}, bf16[16,4096]{1,0:T(8,128)(2,1)S(1)}, u32[]{:S(2)}, u32[]{:S(2)}) collective-permute-start(bf16[16,4096]{1,0:T(8,128)(2,1)S(1)} %add_convert_fusion.refs_2_), channel_id=1, source_target_pairs={{0,2},{1,3},{2,0},{3,1},{4,6},{5,7},{6,4},{7,5},{8,10},{9,11},{10,... | collective-permute-start | bytes 393224 | tf_op jit(solution)/shard_map/ppermute | solution.py:37
  26.3 0.0 collective-permute-done.9
  26.3 1.8 %collective-permute-start.10 = (bf16[16,2048]{1,0:T(8,128)(2,1)S(1)}, bf16[16,2048]{1,0:T(8,128)(2,1)S(1)}, u32[]{:S(2)}, u32[]{:S(2)}) collective-permute-start(bf16[16,2048]{1,0:T(8,128)(2,1)S(1)} %add_convert_fusion.1.refs_0_), channel_id=1, source_target_pairs={{0,1},{1,0},{2,3},{3,2},{4,5},{5,4},{6,7},{7,6},{8,9},{9,8},{10,11... | collective-permute-start | bytes 196616 | tf_op jit(solution)/shard_map/ppermute | solution.py:37
  28.0 4.0 %collective-permute-done.10.refs_1_ = bf16[16,2048]{1,0:T(8,128)(2,1)S(1)} collective-permute-done((bf16[16,2048]{1,0:T(8,128)(2,1)S(1)}, bf16[16,2048]{1,0:T(8,128)(2,1)S(1)}, u32[]{:S(2)}, u32[]{:S(2)}) %collective-permute-start.10) | collective-permute-done | bytes 65568 | tf_op jit(solution)/shard_map/ppermute | solution.py:37
  32.1 0.0 collective-permute-done.12.refs_3_
  32.1 0.7 %shard_map.63 = bf16[16,8192]{1,0:T(8,128)(2,1)} custom-call(bf16[16,2048]{1,0:T(8,128)(2,1)S(1)} %add_convert_fusion.1.refs_0_, bf16[16,2048]{1,0:T(8,128)(2,1)S(1)} %collective-permute-done.10.refs_1_, bf16[16,4096]{1,0:T(8,128)(2,1)S(1)} %add_convert_fusion.refs_2_, bf16[16,4096]{1,0:T(8,128)(2,1)S(1)} %collective-permute-done.12.refs_3_), custom_call_target="tpu_custom_call" | custom-call | tf_op jit(solution)/shard_map/pallas_call | solution.py:268
  (4 shorter events, 0.1 us)
Async XLA Ops:
  0.0 7.1 %collective-permute-start.2 = (bf16[16,512]{1,0:T(8,128)(2,1)}, bf16[16,512]{1,0:T(8,128)(2,1)S(1)}, u32[]{:S(2)}, u32[]{:S(2)}) collective-permute-start(bf16[16,512]{1,0:T(8,128)(2,1)} %query_ref.1), channel_id=1, source_target_pairs={{0,16},{4,20},{8,24},{12,28},{16,0},{20,4},{24,8},{28,12},{1,17},{... | collective-permute-start | bytes 49160 | tf_op jit(solution)/shard_map/ppermute | solution.py:32
  3.0 4.1 %collective-permute-start.1 = (bf16[16,512]{1,0:T(8,128)(2,1)}, bf16[16,512]{1,0:T(8,128)(2,1)S(1)}, u32[]{:S(2)}, u32[]{:S(2)}) collective-permute-start(bf16[16,512]{1,0:T(8,128)(2,1)} %query_ref.1), channel_id=1, source_target_pairs={{0,20},{4,24},{8,28},{12,0},{16,4},{20,8},{24,12},{28,16},{1,21},{... | collective-permute-start | bytes 49160 | tf_op jit(solution)/shard_map/ppermute | solution.py:32
  3.0 4.1 %collective-permute-start = (bf16[16,512]{1,0:T(8,128)(2,1)}, bf16[16,512]{1,0:T(8,128)(2,1)S(1)}, u32[]{:S(2)}, u32[]{:S(2)}) collective-permute-start(bf16[16,512]{1,0:T(8,128)(2,1)} %query_ref.1), channel_id=1, source_target_pairs={{0,24},{4,28},{8,0},{12,4},{16,8},{20,12},{24,16},{28,20},{1,25},{... | collective-permute-start | bytes 49160 | tf_op jit(solution)/shard_map/ppermute | solution.py:32
  6.2 7.8 %collective-permute-start.3 = (bf16[528,128]{1,0:T(8,128)(2,1)S(1)}, bf16[528,128]{1,0:T(8,128)(2,1)S(1)}, u32[]{:S(2)}, u32[]{:S(2)}) collective-permute-start(bf16[528,128]{1,0:T(8,128)(2,1)S(1)} %get-tuple-element.26), channel_id=1, source_target_pairs={{0,4},{4,8},{8,12},{12,16},{16,20},{20,24},{24,28},{28,0},{1,5},{5... | collective-permute-start | bytes 405512 | tf_op jit(solution)/shard_map/ppermute | solution.py:32
  6.2 7.8 %collective-permute-start.4 = (bf16[528,128]{1,0:T(8,128)(2,1)S(1)}, bf16[528,128]{1,0:T(8,128)(2,1)S(1)}, u32[]{:S(2)}, u32[]{:S(2)}) collective-permute-start(bf16[528,128]{1,0:T(8,128)(2,1)S(1)} %get-tuple-element.27), channel_id=1, source_target_pairs={{0,20},{4,24},{8,28},{12,0},{16,4},{20,8},{24,12},{28,16},{1,21},{... | collective-permute-start | bytes 405512 | tf_op jit(solution)/shard_map/ppermute | solution.py:32
  7.5 6.9 %collective-permute-start.5 = (bf16[64,256]{1,0:T(8,128)(2,1)S(1)}, bf16[64,256]{1,0:T(8,128)(2,1)S(1)}, u32[]{:S(2)}, u32[]{:S(2)}) collective-permute-start(bf16[64,256]{1,0:T(8,128)(2,1)S(1)} %get-tuple-element.31), channel_id=1, source_target_pairs={{0,8},{4,12},{8,16},{12,20},{16,24},{20,28},{24,0},{28,4},{1,9},{5... | collective-permute-start | bytes 98312 | tf_op jit(solution)/shard_map/ppermute | solution.py:32
  9.9 4.5 %collective-permute-start.6 = (bf16[64,256]{1,0:T(8,128)(2,1)S(1)}, bf16[64,256]{1,0:T(8,128)(2,1)S(1)}, u32[]{:S(2)}, u32[]{:S(2)}) collective-permute-start(bf16[64,256]{1,0:T(8,128)(2,1)S(1)} %get-tuple-element.32), channel_id=1, source_target_pairs={{0,12},{4,16},{8,20},{12,24},{16,28},{20,0},{24,4},{28,8},{1,13},{... | collective-permute-start | bytes 98312 | tf_op jit(solution)/shard_map/ppermute | solution.py:32
  10.2 4.7 %slice-start = ((s8[8388608]{0:T(1024)(128)(4,1)}), s8[4194304]{0:T(1024)(128)(4,1)S(1)}, s32[]{:S(2)}) async-start(s8[8388608]{0:T(1024)(128)(4,1)} %bitcast), calls=%async_computation | async-start | bytes 8388608
  10.2 3.8 %copy-start = (bf16[16,512]{1,0:T(8,128)(2,1)S(1)}, bf16[16,512]{1,0:T(8,128)(2,1)}, u32[]{:S(2)}) copy-start(bf16[16,512]{1,0:T(8,128)(2,1)} %query_ref.1) | copy-start | bytes 49156
  10.2 4.7 %slice-start.1 = ((s8[8388608]{0:T(1024)(128)(4,1)}), s8[4194304]{0:T(1024)(128)(4,1)S(1)}, s32[]{:S(2)}) async-start(s8[8388608]{0:T(1024)(128)(4,1)} %bitcast), calls=%async_computation.1 | async-start | bytes 8388608
  10.2 4.5 %collective-permute-start.7 = (bf16[64,256]{1,0:T(8,128)(2,1)S(1)}, bf16[64,256]{1,0:T(8,128)(2,1)S(1)}, u32[]{:S(2)}, u32[]{:S(2)}) collective-permute-start(bf16[64,256]{1,0:T(8,128)(2,1)S(1)} %get-tuple-element.22.after_ref), channel_id=1, source_target_pairs={{0,16},{4,20},{8,24},{12,28},{16,0},{20,4},{24,8},{28,12},{1,17},{... | collective-permute-start | bytes 98312 | tf_op jit(solution)/shard_map/ppermute | solution.py:32
  15.4 4.3 %collective-permute-start.8 = (bf16[16,2048]{1,0:T(8,128)(2,1)S(1)}, bf16[16,2048]{1,0:T(8,128)(2,1)S(1)}, u32[]{:S(2)}, u32[]{:S(2)}) collective-permute-start(bf16[16,2048]{1,0:T(8,128)(2,1)S(1)} %shard_map.61), channel_id=1, source_target_pairs={{0,1},{1,0},{2,3},{3,2},{4,5},{5,4},{6,7},{7,6},{8,9},{9,8},{10,11... | collective-permute-start | bytes 196616 | tf_op jit(solution)/shard_map/ppermute | solution.py:37
  17.6 5.9 %collective-permute-start.11 = (bf16[16,4096]{1,0:T(8,128)(2,1)S(1)}, bf16[16,4096]{1,0:T(8,128)(2,1)S(1)}, u32[]{:S(2)}, u32[]{:S(2)}) collective-permute-start(bf16[16,4096]{1,0:T(8,128)(2,1)S(1)} %shard_map.62), channel_id=1, source_target_pairs={{0,1},{1,0},{2,3},{3,2},{4,5},{5,4},{6,7},{7,6},{8,9},{9,8},{10,11... | collective-permute-start | bytes 393224 | tf_op jit(solution)/shard_map/ppermute | solution.py:37
  19.7 6.6 %collective-permute-start.9 = (bf16[16,2048]{1,0:T(8,128)(2,1)S(1)}, bf16[16,2048]{1,0:T(8,128)(2,1)S(1)}, u32[]{:S(2)}, u32[]{:S(2)}) collective-permute-start(bf16[16,2048]{1,0:T(8,128)(2,1)S(1)} %add_convert_fusion.2), channel_id=1, source_target_pairs={{0,2},{1,3},{2,0},{3,1},{4,6},{5,7},{6,4},{7,5},{8,10},{9,11},{10,... | collective-permute-start | bytes 196616 | tf_op jit(solution)/shard_map/ppermute | solution.py:37
  23.6 8.5 %collective-permute-start.12 = (bf16[16,4096]{1,0:T(8,128)(2,1)S(1)}, bf16[16,4096]{1,0:T(8,128)(2,1)S(1)}, u32[]{:S(2)}, u32[]{:S(2)}) collective-permute-start(bf16[16,4096]{1,0:T(8,128)(2,1)S(1)} %add_convert_fusion.refs_2_), channel_id=1, source_target_pairs={{0,2},{1,3},{2,0},{3,1},{4,6},{5,7},{6,4},{7,5},{8,10},{9,11},{10,... | collective-permute-start | bytes 393224 | tf_op jit(solution)/shard_map/ppermute | solution.py:37
  26.3 5.8 %collective-permute-start.10 = (bf16[16,2048]{1,0:T(8,128)(2,1)S(1)}, bf16[16,2048]{1,0:T(8,128)(2,1)S(1)}, u32[]{:S(2)}, u32[]{:S(2)}) collective-permute-start(bf16[16,2048]{1,0:T(8,128)(2,1)S(1)} %add_convert_fusion.1.refs_0_), channel_id=1, source_target_pairs={{0,1},{1,0},{2,3},{3,2},{4,5},{5,4},{6,7},{7,6},{8,9},{9,8},{10,11... | collective-permute-start | bytes 196616 | tf_op jit(solution)/shard_map/ppermute | solution.py:37

commit v5 on v4

--- a/solution.py
+++ b/solution.py
@@ -10,9 +10,9 @@
 GQA = 8
 SPREAD = 6
 CAPACITY = 2
-PARTS = (("split", 4), ("near", 4))
-ASKED = (2, 3, 4)
-SENT = (1, 5)
+PARTS = (("split", 4), ("far", 2), ("near", 2))
+ASKED = (1, 2, 3)
+SENT = (4, 5)
 FLAG_ROWS = 8
 NEG = -(2.0**100)
 

time: 33 us -> 32.1 us (0.973)
  waiting for transfers between devices: 6.81 us -> 5.25 us
  starting transfers between devices: 19.4 us -> 20.5 us
  Pallas kernels: 6.41 us -> 5.95 us
    ppermute x5 -> x7, waiting for transfers between devices: 6.45 us -> 3.74 us  [swapped(): return lax.ppermute(block, 'mp', [(i, i ^ step) for i in range(size)])]
    ppermute x5 -> x7, starting transfers between devices: 9.13 us -> 11.3 us  [swapped(): return lax.ppermute(block, 'mp', [(i, i ^ step) for i in range(size)])]
    ppermute x8, waiting for transfers between devices: 0.37 us -> 1.5 us  [shifted(): lax.ppermute(block, 'dp', [(i, (i + distance) % size) for i in range(size)])]
    ppermute x8, starting transfers between devices: 10.2 us -> 9.2 us  [shifted(): lax.ppermute(block, 'dp', [(i, (i + distance) % size) for i in range(size)])]
    pallas_call x1, Pallas kernels: 2.22 us -> 1.66 us  [local(): pl.pallas_call(functools.partial(own_kernel, local_heads), out_shape=part...]
    pallas_call x3 -> x4, Pallas kernels: 1.41 us -> 1.5 us  [project(): pl.pallas_call(functools.partial(project_kernel, half, start), out_shape=...]
  transfers between devices with their start and end apart: 13 -> 15, of which waited for: 4 -> 8; matrix products, arithmetic and copies ran while one was open for 0% -> 0% of each run, Pallas kernels for 16% -> 15%
where the time goes in v5:
time: 32.1 us; the launch traced here: 31.9 us
  starting transfers between devices  20.5 us (64%)
  Pallas kernels  5.95 us (19%)
  waiting for transfers between devices  5.25 us (16%)
    ppermute x7, starting transfers between devices, swapped(): return lax.ppermute(block, 'mp', [(i, i ^ step) for i in range(size)])  11.3 us
    ppermute x8, starting transfers between devices, shifted(): lax.ppermute(block, 'dp', [(i, (i + distance) % size) for i in range(size)])  9.2 us
    ppermute x7, waiting for transfers between devices, swapped(): return lax.ppermute(block, 'mp', [(i, i ^ step) for i in range(size)])  3.74 us
    pallas_call x1, Pallas kernels, local(): pl.pallas_call(functools.partial(own_kernel, local_heads), out_shape=part...  1.66 us
    ppermute x8, waiting for transfers between devices, shifted(): lax.ppermute(block, 'dp', [(i, (i + distance) % size) for i in range(size)])  1.5 us
    pallas_call x4, Pallas kernels, project(): pl.pallas_call(functools.partial(project_kernel, half, start), out_shape=...  1.5 us
    pallas_call x1, Pallas kernels, local(): pl.pallas_call(functools.partial(gather_kernel, local_heads), out_shape=(...  1.06 us
    pallas_call x1, Pallas kernels, summed_over_four(): pl.pallas_call(functools.partial(final_kernel, layout), out_shape=jax.Sha...  0.74 us
  transfers between devices with their start and end apart: 15, of which 8 were waited for; matrix products, arithmetic and copies ran while one was open for 0% of the time, Pallas kernels for 15%

profile of v5, /device:TPU:0, one launch (start us, length us, event | category | flops | bytes accessed | tf_op | source)
XLA Modules:
  0.0 31.9 jit_solution(14712916389690423686)
XLA Ops:
  0.0 2.4 %collective-permute-start.2 = (bf16[16,512]{1,0:T(8,128)(2,1)}, bf16[16,512]{1,0:T(8,128)(2,1)S(1)}, u32[]{:S(2)}, u32[]{:S(2)}) collective-permute-start(bf16[16,512]{1,0:T(8,128)(2,1)} %query_ref.1), channel_id=1, source_target_pairs={{0,20},{4,24},{8,28},{12,0},{16,4},{20,8},{24,12},{28,16},{1,21},{... | collective-permute-start | bytes 49160 | tf_op jit(solution)/shard_map/ppermute | solution.py:32
  2.4 1.5 %collective-permute-start.1 = (bf16[16,512]{1,0:T(8,128)(2,1)}, bf16[16,512]{1,0:T(8,128)(2,1)S(1)}, u32[]{:S(2)}, u32[]{:S(2)}) collective-permute-start(bf16[16,512]{1,0:T(8,128)(2,1)} %query_ref.1), channel_id=1, source_target_pairs={{0,24},{4,28},{8,0},{12,4},{16,8},{20,12},{24,16},{28,20},{1,25},{... | collective-permute-start | bytes 49160 | tf_op jit(solution)/shard_map/ppermute | solution.py:32
  3.9 1.4 %collective-permute-start = (bf16[16,512]{1,0:T(8,128)(2,1)}, bf16[16,512]{1,0:T(8,128)(2,1)S(1)}, u32[]{:S(2)}, u32[]{:S(2)}) collective-permute-start(bf16[16,512]{1,0:T(8,128)(2,1)} %query_ref.1), channel_id=1, source_target_pairs={{0,28},{4,0},{8,4},{12,8},{16,12},{20,16},{24,20},{28,24},{1,29},{... | collective-permute-start | bytes 49160 | tf_op jit(solution)/shard_map/ppermute | solution.py:32
  5.3 1.1 %shard_map.55 = (bf16[4,256,128]{2,1,0:T(8,128)(2,1)S(1)}, bf16[4,256,128]{2,1,0:T(8,128)(2,1)S(1)}, f32[4,8,256]{2,1,0:T(8,128)S(1)}, bf16[528,128]{1,0:T(8,128)(2,1)S(1)}, bf16[528,128]{1,0:T(8,128)(2,1)S(1)}) custom-call(s32[6]{0:T(128)} %offset_hbm.1, bf16[6,2,2,128,128]{4,3,2,1,0:T(8,128)(2,1)} %pool_hbm.1), custom_call_target="tpu_custom_call" | custom-call | flops 8800000000 | bytes 29520000 | tf_op jit(solution)/shard_map/pallas_call | solution.py:295
  6.4 1.6 %collective-permute-start.3 = (bf16[528,128]{1,0:T(8,128)(2,1)S(1)}, bf16[528,128]{1,0:T(8,128)(2,1)S(1)}, u32[]{:S(2)}, u32[]{:S(2)}) collective-permute-start(bf16[528,128]{1,0:T(8,128)(2,1)S(1)} %get-tuple-element.26), channel_id=1, source_target_pairs={{0,16},{4,20},{8,24},{12,28},{16,0},{20,4},{24,8},{28,12},{1,17},{... | collective-permute-start | bytes 405512 | tf_op jit(solution)/shard_map/ppermute | solution.py:32
  8.0 0.0 collective-permute-start.4
  8.0 0.0 collective-permute-done.2.refs_2_
  8.0 0.0 collective-permute-done.1.refs_1_
  8.0 0.0 collective-permute-done.refs_0_
  8.0 0.4 %shard_map.56 = (bf16[64,256]{1,0:T(8,128)(2,1)S(1)}, bf16[64,256]{1,0:T(8,128)(2,1)S(1)}, bf16[64,256]{1,0:T(8,128)(2,1)S(1)}) custom-call(bf16[4,256,128]{2,1,0:T(8,128)(2,1)S(1)} %get-tuple-element.19.key_ref, bf16[4,256,128]{2,1,0:T(8,128)(2,1)S(1)} %get-tuple-element.20.value_ref, f32[4,8,256]{2,1,0:T(8,128)S(1)} %get-tuple-element.21.bias_ref, ...), custom_call_target="tpu_custom_call" | custom-call | flops 440000000 | bytes 1476000 | tf_op jit(solution)/shard_map/pallas_call | solution.py:310
  8.4 0.7 %collective-permute-start.5 = (bf16[64,256]{1,0:T(8,128)(2,1)S(1)}, bf16[64,256]{1,0:T(8,128)(2,1)S(1)}, u32[]{:S(2)}, u32[]{:S(2)}) collective-permute-start(bf16[64,256]{1,0:T(8,128)(2,1)S(1)} %get-tuple-element.31), channel_id=1, source_target_pairs={{0,4},{4,8},{8,12},{12,16},{16,20},{20,24},{24,28},{28,0},{1,5},{5... | collective-permute-start | bytes 98312 | tf_op jit(solution)/shard_map/ppermute | solution.py:32
  9.1 1.5 %collective-permute-start.6 = (bf16[64,256]{1,0:T(8,128)(2,1)S(1)}, bf16[64,256]{1,0:T(8,128)(2,1)S(1)}, u32[]{:S(2)}, u32[]{:S(2)}) collective-permute-start(bf16[64,256]{1,0:T(8,128)(2,1)S(1)} %get-tuple-element.32), channel_id=1, source_target_pairs={{0,8},{4,12},{8,16},{12,20},{16,24},{20,28},{24,0},{28,4},{1,9},{5... | collective-permute-start | bytes 98312 | tf_op jit(solution)/shard_map/ppermute | solution.py:32
  10.6 0.0 slice-start
  10.6 0.0 copy-start
  10.6 0.0 slice-start.1
  10.6 0.1 collective-permute-start.7
  10.7 1.7 %shard_map.57 = (f32[64,128]{1,0:T(8,128)S(1)}, f32[64,128]{1,0:T(8,128)S(1)}, f32[64,128]{1,0:T(8,128)S(1)}) custom-call(bf16[4,256,128]{2,1,0:T(8,128)(2,1)S(1)} %get-tuple-element.19.key_ref, bf16[4,256,128]{2,1,0:T(8,128)(2,1)S(1)} %get-tuple-element.20.value_ref, f32[4,8,256]{2,1,0:T(8,128)S(1)} %get-tuple-element.21.bias_ref, ...), custom_call_target="tpu_custom_call" | custom-call | flops 1760000000 | bytes 5904000 | tf_op jit(solution)/shard_map/pallas_call | solution.py:319
  12.4 0.0 collective-permute-done.3.refs_0_
  12.4 1.0 %collective-permute-done.4.refs_1_ = bf16[528,128]{1,0:T(8,128)(2,1)S(1)} collective-permute-done((bf16[528,128]{1,0:T(8,128)(2,1)S(1)}, bf16[528,128]{1,0:T(8,128)(2,1)S(1)}, u32[]{:S(2)}, u32[]{:S(2)}) %collective-permute-start.4) | collective-permute-done | bytes 135200 | tf_op jit(solution)/shard_map/ppermute | solution.py:32
  13.4 0.0 copy-done
  13.4 0.4 %shard_map.58 = (f32[64,128]{1,0:T(8,128)S(1)}, f32[64,128]{1,0:T(8,128)S(1)}, f32[64,128]{1,0:T(8,128)S(1)}) custom-call(f32[64,128]{1,0:T(8,128)S(1)} %get-tuple-element.23.after_ref.refs_0_, bf16[16,512]{1,0:T(8,128)(2,1)S(1)} %copy-done, bf16[528,128]{1,0:T(8,128)(2,1)S(1)} %collective-permute-done.3.refs_0_, ...), custom_call_target="tpu_custom_call" | custom-call | flops 550000000 | bytes 1845000 | tf_op jit(solution)/shard_map/pallas_call | solution.py:332
  13.8 0.0 collective-permute-done.5.refs_6_
  13.8 0.2 collective-permute-done.6.refs_7_
  14.0 0.4 %collective-permute-done.7.refs_8_ = bf16[64,256]{1,0:T(8,128)(2,1)S(1)} collective-permute-done((bf16[64,256]{1,0:T(8,128)(2,1)S(1)}, bf16[64,256]{1,0:T(8,128)(2,1)S(1)}, u32[]{:S(2)}, u32[]{:S(2)}) %collective-permute-start.7) | collective-permute-done | bytes 32800 | tf_op jit(solution)/shard_map/ppermute | solution.py:32
  14.3 0.2 shard_map.59.attended_ref
  14.5 0.0 slice-done
  14.5 0.0 slice-done.1
  14.5 0.4 %shard_map.61 = bf16[16,2048]{1,0:T(8,128)(2,1)S(1)} custom-call(bf16[16,512]{1,0:T(8,128)(2,1)S(1)} %shard_map.59.attended_ref, bf16[512,8192]{1,0:T(8,128)(2,1)S(1)} %bitcast.1), custom_call_target="tpu_custom_call" | custom-call | flops 33554432 | bytes 2097152 | tf_op jit(solution)/shard_map/pallas_call | solution.py:215
  14.9 1.6 %collective-permute-start.8 = (bf16[16,2048]{1,0:T(8,128)(2,1)S(1)}, bf16[16,2048]{1,0:T(8,128)(2,1)S(1)}, u32[]{:S(2)}, u32[]{:S(2)}) collective-permute-start(bf16[16,2048]{1,0:T(8,128)(2,1)S(1)} %shard_map.61), channel_id=1, source_target_pairs={{0,1},{1,0},{2,3},{3,2},{4,5},{5,4},{6,7},{7,6},{8,9},{9,8},{10,11... | collective-permute-start | bytes 196616 | tf_op jit(solution)/shard_map/ppermute | solution.py:37
  16.5 0.4 %shard_map.62 = bf16[16,2048]{1,0:T(8,128)(2,1)S(1)} custom-call(bf16[16,512]{1,0:T(8,128)(2,1)S(1)} %shard_map.59.attended_ref, bf16[512,8192]{1,0:T(8,128)(2,1)S(1)} %bitcast.1), custom_call_target="tpu_custom_call" | custom-call | flops 33554432 | bytes 2097152 | tf_op jit(solution)/shard_map/pallas_call | solution.py:215
  16.9 2.6 %collective-permute-start.11 = (bf16[16,2048]{1,0:T(8,128)(2,1)S(1)}, bf16[16,2048]{1,0:T(8,128)(2,1)S(1)}, u32[]{:S(2)}, u32[]{:S(2)}) collective-permute-start(bf16[16,2048]{1,0:T(8,128)(2,1)S(1)} %shard_map.62), channel_id=1, source_target_pairs={{0,2},{1,3},{2,0},{3,1},{4,6},{5,7},{6,4},{7,5},{8,10},{9,11},{10,... | collective-permute-start | bytes 196616 | tf_op jit(solution)/shard_map/ppermute | solution.py:37
  19.5 0.4 %shard_map.63 = bf16[16,2048]{1,0:T(8,128)(2,1)S(1)} custom-call(bf16[16,512]{1,0:T(8,128)(2,1)S(1)} %shard_map.59.attended_ref, bf16[512,8192]{1,0:T(8,128)(2,1)S(1)} %bitcast.1), custom_call_target="tpu_custom_call" | custom-call | flops 33554432 | bytes 2097152 | tf_op jit(solution)/shard_map/pallas_call | solution.py:215
  19.8 0.5 %collective-permute-start.13 = (bf16[16,2048]{1,0:T(8,128)(2,1)S(1)}, bf16[16,2048]{1,0:T(8,128)(2,1)S(1)}, u32[]{:S(2)}, u32[]{:S(2)}) collective-permute-start(bf16[16,2048]{1,0:T(8,128)(2,1)S(1)} %shard_map.63), channel_id=1, source_target_pairs={{0,1},{1,0},{2,3},{3,2},{4,5},{5,4},{6,7},{7,6},{8,9},{9,8},{10,11... | collective-permute-start | bytes 196616 | tf_op jit(solution)/shard_map/ppermute | solution.py:37
  20.3 0.4 %shard_map.60 = bf16[16,2048]{1,0:T(8,128)(2,1)S(1)} custom-call(bf16[16,512]{1,0:T(8,128)(2,1)S(1)} %shard_map.59.attended_ref, bf16[512,8192]{1,0:T(8,128)(2,1)S(1)} %bitcast.1), custom_call_target="tpu_custom_call" | custom-call | flops 33554432 | bytes 2097152 | tf_op jit(solution)/shard_map/pallas_call | solution.py:215
  20.7 0.0 collective-permute-done.8
  20.7 1.8 %collective-permute-start.9 = (bf16[16,2048]{1,0:T(8,128)(2,1)S(1)}, bf16[16,2048]{1,0:T(8,128)(2,1)S(1)}, u32[]{:S(2)}, u32[]{:S(2)}) collective-permute-start(bf16[16,2048]{1,0:T(8,128)(2,1)S(1)} %add_convert_fusion.3), channel_id=1, source_target_pairs={{0,2},{1,3},{2,0},{3,1},{4,6},{5,7},{6,4},{7,5},{8,10},{9,11},{10,... | collective-permute-start | bytes 196616 | tf_op jit(solution)/shard_map/ppermute | solution.py:37
  22.5 0.7 %collective-permute-done.11 = bf16[16,2048]{1,0:T(8,128)(2,1)S(1)} collective-permute-done((bf16[16,2048]{1,0:T(8,128)(2,1)S(1)}, bf16[16,2048]{1,0:T(8,128)(2,1)S(1)}, u32[]{:S(2)}, u32[]{:S(2)}) %collective-permute-start.11) | collective-permute-done | bytes 65568 | tf_op jit(solution)/shard_map/ppermute | solution.py:37
  23.2 1.7 %collective-permute-start.12 = (bf16[16,2048]{1,0:T(8,128)(2,1)S(1)}, bf16[16,2048]{1,0:T(8,128)(2,1)S(1)}, u32[]{:S(2)}, u32[]{:S(2)}) collective-permute-start(bf16[16,2048]{1,0:T(8,128)(2,1)S(1)} %add_convert_fusion.1.refs_2_), channel_id=1, source_target_pairs={{0,1},{1,0},{2,3},{3,2},{4,5},{5,4},{6,7},{7,6},{8,9},{9,8},{10,11... | collective-permute-start | bytes 196616 | tf_op jit(solution)/shard_map/ppermute | solution.py:37
  24.9 0.1 collective-permute-done.13
  25.0 1.3 %collective-permute-start.14 = (bf16[16,2048]{1,0:T(8,128)(2,1)S(1)}, bf16[16,2048]{1,0:T(8,128)(2,1)S(1)}, u32[]{:S(2)}, u32[]{:S(2)}) collective-permute-start(bf16[16,2048]{1,0:T(8,128)(2,1)S(1)} %add_convert_fusion.refs_4_), channel_id=1, source_target_pairs={{0,2},{1,3},{2,0},{3,1},{4,6},{5,7},{6,4},{7,5},{8,10},{9,11},{10,... | collective-permute-start | bytes 196616 | tf_op jit(solution)/shard_map/ppermute | solution.py:37
  26.4 0.0 collective-permute-done.9
  26.4 1.9 %collective-permute-start.10 = (bf16[16,2048]{1,0:T(8,128)(2,1)S(1)}, bf16[16,2048]{1,0:T(8,128)(2,1)S(1)}, u32[]{:S(2)}, u32[]{:S(2)}) collective-permute-start(bf16[16,2048]{1,0:T(8,128)(2,1)S(1)} %add_convert_fusion.2.refs_0_), channel_id=1, source_target_pairs={{0,1},{1,0},{2,3},{3,2},{4,5},{5,4},{6,7},{7,6},{8,9},{9,8},{10,11... | collective-permute-start | bytes 196616 | tf_op jit(solution)/shard_map/ppermute | solution.py:37
  28.3 0.5 %collective-permute-done.12.refs_3_ = bf16[16,2048]{1,0:T(8,128)(2,1)S(1)} collective-permute-done((bf16[16,2048]{1,0:T(8,128)(2,1)S(1)}, bf16[16,2048]{1,0:T(8,128)(2,1)S(1)}, u32[]{:S(2)}, u32[]{:S(2)}) %collective-permute-start.12) | collective-permute-done | bytes 65568 | tf_op jit(solution)/shard_map/ppermute | solution.py:37
  28.8 2.3 %collective-permute-done.14.refs_5_ = bf16[16,2048]{1,0:T(8,128)(2,1)S(1)} collective-permute-done((bf16[16,2048]{1,0:T(8,128)(2,1)S(1)}, bf16[16,2048]{1,0:T(8,128)(2,1)S(1)}, u32[]{:S(2)}, u32[]{:S(2)}) %collective-permute-start.14) | collective-permute-done | bytes 65568 | tf_op jit(solution)/shard_map/ppermute | solution.py:37
  31.1 0.1 collective-permute-done.10.refs_1_
  31.2 0.7 %shard_map.64 = bf16[16,8192]{1,0:T(8,128)(2,1)} custom-call(bf16[16,2048]{1,0:T(8,128)(2,1)S(1)} %add_convert_fusion.2.refs_0_, bf16[16,2048]{1,0:T(8,128)(2,1)S(1)} %collective-permute-done.10.refs_1_, bf16[16,2048]{1,0:T(8,128)(2,1)S(1)} %add_convert_fusion.1.refs_2_, bf16[16,2048]{1,0:T(8,128)(2,1)S(1)} %collective-permute-done.12.refs_3_, ...), custom_call_target="tpu_custom_call" | custom-call | tf_op jit(solution)/shard_map/pallas_call | solution.py:268
  (5 shorter events, 0.1 us)
Async XLA Ops:
  0.0 8.0 %collective-permute-start.2 = (bf16[16,512]{1,0:T(8,128)(2,1)}, bf16[16,512]{1,0:T(8,128)(2,1)S(1)}, u32[]{:S(2)}, u32[]{:S(2)}) collective-permute-start(bf16[16,512]{1,0:T(8,128)(2,1)} %query_ref.1), channel_id=1, source_target_pairs={{0,20},{4,24},{8,28},{12,0},{16,4},{20,8},{24,12},{28,16},{1,21},{... | collective-permute-start | bytes 49160 | tf_op jit(solution)/shard_map/ppermute | solution.py:32
  2.4 5.6 %collective-permute-start.1 = (bf16[16,512]{1,0:T(8,128)(2,1)}, bf16[16,512]{1,0:T(8,128)(2,1)S(1)}, u32[]{:S(2)}, u32[]{:S(2)}) collective-permute-start(bf16[16,512]{1,0:T(8,128)(2,1)} %query_ref.1), channel_id=1, source_target_pairs={{0,24},{4,28},{8,0},{12,4},{16,8},{20,12},{24,16},{28,20},{1,25},{... | collective-permute-start | bytes 49160 | tf_op jit(solution)/shard_map/ppermute | solution.py:32
  3.9 4.0 %collective-permute-start = (bf16[16,512]{1,0:T(8,128)(2,1)}, bf16[16,512]{1,0:T(8,128)(2,1)S(1)}, u32[]{:S(2)}, u32[]{:S(2)}) collective-permute-start(bf16[16,512]{1,0:T(8,128)(2,1)} %query_ref.1), channel_id=1, source_target_pairs={{0,28},{4,0},{8,4},{12,8},{16,12},{20,16},{24,20},{28,24},{1,29},{... | collective-permute-start | bytes 49160 | tf_op jit(solution)/shard_map/ppermute | solution.py:32
  6.4 6.0 %collective-permute-start.3 = (bf16[528,128]{1,0:T(8,128)(2,1)S(1)}, bf16[528,128]{1,0:T(8,128)(2,1)S(1)}, u32[]{:S(2)}, u32[]{:S(2)}) collective-permute-start(bf16[528,128]{1,0:T(8,128)(2,1)S(1)} %get-tuple-element.26), channel_id=1, source_target_pairs={{0,16},{4,20},{8,24},{12,28},{16,0},{20,4},{24,8},{28,12},{1,17},{... | collective-permute-start | bytes 405512 | tf_op jit(solution)/shard_map/ppermute | solution.py:32
  8.0 5.4 %collective-permute-start.4 = (bf16[528,128]{1,0:T(8,128)(2,1)S(1)}, bf16[528,128]{1,0:T(8,128)(2,1)S(1)}, u32[]{:S(2)}, u32[]{:S(2)}) collective-permute-start(bf16[528,128]{1,0:T(8,128)(2,1)S(1)} %get-tuple-element.27), channel_id=1, source_target_pairs={{0,20},{4,24},{8,28},{12,0},{16,4},{20,8},{24,12},{28,16},{1,21},{... | collective-permute-start | bytes 405512 | tf_op jit(solution)/shard_map/ppermute | solution.py:32
  8.4 5.4 %collective-permute-start.5 = (bf16[64,256]{1,0:T(8,128)(2,1)S(1)}, bf16[64,256]{1,0:T(8,128)(2,1)S(1)}, u32[]{:S(2)}, u32[]{:S(2)}) collective-permute-start(bf16[64,256]{1,0:T(8,128)(2,1)S(1)} %get-tuple-element.31), channel_id=1, source_target_pairs={{0,4},{4,8},{8,12},{12,16},{16,20},{20,24},{24,28},{28,0},{1,5},{5... | collective-permute-start | bytes 98312 | tf_op jit(solution)/shard_map/ppermute | solution.py:32
  9.1 4.9 %collective-permute-start.6 = (bf16[64,256]{1,0:T(8,128)(2,1)S(1)}, bf16[64,256]{1,0:T(8,128)(2,1)S(1)}, u32[]{:S(2)}, u32[]{:S(2)}) collective-permute-start(bf16[64,256]{1,0:T(8,128)(2,1)S(1)} %get-tuple-element.32), channel_id=1, source_target_pairs={{0,8},{4,12},{8,16},{12,20},{16,24},{20,28},{24,0},{28,4},{1,9},{5... | collective-permute-start | bytes 98312 | tf_op jit(solution)/shard_map/ppermute | solution.py:32
  10.6 3.9 %slice-start = ((s8[8388608]{0:T(1024)(128)(4,1)}), s8[4194304]{0:T(1024)(128)(4,1)S(1)}, s32[]{:S(2)}) async-start(s8[8388608]{0:T(1024)(128)(4,1)} %bitcast), calls=%async_computation | async-start | bytes 8388608
  10.6 2.7 %copy-start = (bf16[16,512]{1,0:T(8,128)(2,1)S(1)}, bf16[16,512]{1,0:T(8,128)(2,1)}, u32[]{:S(2)}) copy-start(bf16[16,512]{1,0:T(8,128)(2,1)} %query_ref.1) | copy-start | bytes 49156
  10.6 3.9 %slice-start.1 = ((s8[8388608]{0:T(1024)(128)(4,1)}), s8[4194304]{0:T(1024)(128)(4,1)S(1)}, s32[]{:S(2)}) async-start(s8[8388608]{0:T(1024)(128)(4,1)} %bitcast), calls=%async_computation.1 | async-start | bytes 8388608
  10.6 3.7 %collective-permute-start.7 = (bf16[64,256]{1,0:T(8,128)(2,1)S(1)}, bf16[64,256]{1,0:T(8,128)(2,1)S(1)}, u32[]{:S(2)}, u32[]{:S(2)}) collective-permute-start(bf16[64,256]{1,0:T(8,128)(2,1)S(1)} %get-tuple-element.22.after_ref), channel_id=1, source_target_pairs={{0,12},{4,16},{8,20},{12,24},{16,28},{20,0},{24,4},{28,8},{1,13},{... | collective-permute-start | bytes 98312 | tf_op jit(solution)/shard_map/ppermute | solution.py:32
  14.9 5.8 %collective-permute-start.8 = (bf16[16,2048]{1,0:T(8,128)(2,1)S(1)}, bf16[16,2048]{1,0:T(8,128)(2,1)S(1)}, u32[]{:S(2)}, u32[]{:S(2)}) collective-permute-start(bf16[16,2048]{1,0:T(8,128)(2,1)S(1)} %shard_map.61), channel_id=1, source_target_pairs={{0,1},{1,0},{2,3},{3,2},{4,5},{5,4},{6,7},{7,6},{8,9},{9,8},{10,11... | collective-permute-start | bytes 196616 | tf_op jit(solution)/shard_map/ppermute | solution.py:37
  16.9 6.4 %collective-permute-start.11 = (bf16[16,2048]{1,0:T(8,128)(2,1)S(1)}, bf16[16,2048]{1,0:T(8,128)(2,1)S(1)}, u32[]{:S(2)}, u32[]{:S(2)}) collective-permute-start(bf16[16,2048]{1,0:T(8,128)(2,1)S(1)} %shard_map.62), channel_id=1, source_target_pairs={{0,2},{1,3},{2,0},{3,1},{4,6},{5,7},{6,4},{7,5},{8,10},{9,11},{10,... | collective-permute-start | bytes 196616 | tf_op jit(solution)/shard_map/ppermute | solution.py:37
  19.8 5.2 %collective-permute-start.13 = (bf16[16,2048]{1,0:T(8,128)(2,1)S(1)}, bf16[16,2048]{1,0:T(8,128)(2,1)S(1)}, u32[]{:S(2)}, u32[]{:S(2)}) collective-permute-start(bf16[16,2048]{1,0:T(8,128)(2,1)S(1)} %shard_map.63), channel_id=1, source_target_pairs={{0,1},{1,0},{2,3},{3,2},{4,5},{5,4},{6,7},{7,6},{8,9},{9,8},{10,11... | collective-permute-start | bytes 196616 | tf_op jit(solution)/shard_map/ppermute | solution.py:37
  20.7 5.6 %collective-permute-start.9 = (bf16[16,2048]{1,0:T(8,128)(2,1)S(1)}, bf16[16,2048]{1,0:T(8,128)(2,1)S(1)}, u32[]{:S(2)}, u32[]{:S(2)}) collective-permute-start(bf16[16,2048]{1,0:T(8,128)(2,1)S(1)} %add_convert_fusion.3), channel_id=1, source_target_pairs={{0,2},{1,3},{2,0},{3,1},{4,6},{5,7},{6,4},{7,5},{8,10},{9,11},{10,... | collective-permute-start | bytes 196616 | tf_op jit(solution)/shard_map/ppermute | solution.py:37
  23.2 5.5 %collective-permute-start.12 = (bf16[16,2048]{1,0:T(8,128)(2,1)S(1)}, bf16[16,2048]{1,0:T(8,128)(2,1)S(1)}, u32[]{:S(2)}, u32[]{:S(2)}) collective-permute-start(bf16[16,2048]{1,0:T(8,128)(2,1)S(1)} %add_convert_fusion.1.refs_2_), channel_id=1, source_target_pairs={{0,1},{1,0},{2,3},{3,2},{4,5},{5,4},{6,7},{7,6},{8,9},{9,8},{10,11... | collective-permute-start | bytes 196616 | tf_op jit(solution)/shard_map/ppermute | solution.py:37
  25.0 6.0 %collective-permute-start.14 = (bf16[16,2048]{1,0:T(8,128)(2,1)S(1)}, bf16[16,2048]{1,0:T(8,128)(2,1)S(1)}, u32[]{:S(2)}, u32[]{:S(2)}) collective-permute-start(bf16[16,2048]{1,0:T(8,128)(2,1)S(1)} %add_convert_fusion.refs_4_), channel_id=1, source_target_pairs={{0,2},{1,3},{2,0},{3,1},{4,6},{5,7},{6,4},{7,5},{8,10},{9,11},{10,... | collective-permute-start | bytes 196616 | tf_op jit(solution)/shard_map/ppermute | solution.py:37
  26.4 4.8 %collective-permute-start.10 = (bf16[16,2048]{1,0:T(8,128)(2,1)S(1)}, bf16[16,2048]{1,0:T(8,128)(2,1)S(1)}, u32[]{:S(2)}, u32[]{:S(2)}) collective-permute-start(bf16[16,2048]{1,0:T(8,128)(2,1)S(1)} %add_convert_fusion.2.refs_0_), channel_id=1, source_target_pairs={{0,1},{1,0},{2,3},{3,2},{4,5},{5,4},{6,7},{7,6},{8,9},{9,8},{10,11... | collective-permute-start | bytes 196616 | tf_op jit(solution)/shard_map/ppermute | solution.py:37

commit v6 on v5

--- a/solution.py
+++ b/solution.py
@@ -10,9 +10,9 @@
 GQA = 8
 SPREAD = 6
 CAPACITY = 2
-PARTS = (("split", 4), ("far", 2), ("near", 2))
-ASKED = (1, 2, 3)
-SENT = (4, 5)
+PARTS = (('split', 2, 4), ('near', 3, 4))
+ASKED = (1, 2, 4)
+SENT = (3, 5)
 FLAG_ROWS = 8
 NEG = -(2.0**100)
 
@@ -58,25 +58,27 @@
     return (first, second), count
 
 
-def first_column(half, start, width):
+def first_column(half, far, start, width):
     if half is None:
         return start
-    kept = lax.axis_index("mp") % 2
+    place = lax.axis_index("mp")
+    kept = place % 2 if far == 2 else (place + place // 2) % 2
     return pl.multiple_of(start + (kept if half else 1 - kept) * width, 128)
 
 
-def gather_kernel(local_heads, offset_hbm, pool_hbm, key_ref, value_ref, bias_ref, *refs):
+def mask_kernel(samples, out_ref):
+    rows, keys = out_ref.shape
+    length = keys // samples
+    row_sample = lax.broadcasted_iota(jnp.int32, (rows, keys), 0) % samples
+    key_at = lax.broadcasted_iota(jnp.int32, (rows, keys), 1)
+    mine = (key_at >= row_sample * length) & (key_at < (row_sample + 1) * length)
+    out_ref[...] = jnp.where(mine, 0.0, NEG)
+
+
+def gather_kernel(local_heads, after_ref, offset_ref, pool_ref, key_ref, value_ref, bias_ref, *refs):
     pack_refs = dict(zip(SENT, refs))
-    offset_ref, pool_ref, sems = refs[len(SENT) :]
     kv = lax.axis_index("mp") * local_heads // GQA
-    block, head_dim = pool_ref.shape[2:]
-    copies = [
-        pltpu.make_async_copy(offset_hbm, offset_ref, sems.at[0]),
-        pltpu.make_async_copy(pool_hbm.at[:, kv], pool_ref, sems.at[1]),
-    ]
-    for copy in copies:
-        copy.start()
-    copies[0].wait()
+    block, head_dim = pool_ref.shape[3:]
     found = [slots_of(offset_ref, lag) for lag in range(SPREAD)]
     at = lax.broadcasted_iota(jnp.int32, bias_ref.shape[1:], 1)
     kept = (0,) + ASKED
@@ -85,17 +87,16 @@
     at = lax.broadcasted_iota(jnp.int32, (2 * FLAG_ROWS, head_dim), 0)
     for lag, ref in pack_refs.items():
         ref[2 * CAPACITY * block :] = jnp.where(at < found[lag][1] * FLAG_ROWS, 0.0, NEG).astype(jnp.bfloat16)
-    copies[1].wait()
     for lag, (slots, _) in enumerate(found):
         for position, slot in enumerate(slots):
             if lag in SENT:
                 at = position * block
-                pack_refs[lag][at : at + block] = pool_ref[slot, 0]
-                pack_refs[lag][CAPACITY * block + at : CAPACITY * block + at + block] = pool_ref[slot, 1]
+                pack_refs[lag][at : at + block] = pool_ref[slot, kv, 0]
+                pack_refs[lag][CAPACITY * block + at : CAPACITY * block + at + block] = pool_ref[slot, kv, 1]
             else:
                 place = slice(position * block, (position + 1) * block)
-                key_ref[kept.index(lag), place] = pool_ref[slot, 0]
-                value_ref[kept.index(lag), place] = pool_ref[slot, 1]
+                key_ref[kept.index(lag), place] = pool_ref[slot, kv, 0]
+                value_ref[kept.index(lag), place] = pool_ref[slot, kv, 1]
 
 
 def held_kernel(after_ref, query_ref, *refs):
@@ -143,7 +144,7 @@
         )
 
 
-def own_kernel(local_heads, key_ref, value_ref, bias_ref, after_ref, query_hbm, suffix_hbm,
+def own_kernel(local_heads, key_ref, value_ref, bias_ref, mask_ref, after_ref, query_hbm, suffix_hbm,
                acc_ref, peak_ref, total_ref, query_ref, suffix_ref, sems):
     kv = lax.axis_index("mp") * local_heads // GQA
     samples, _, length, head_dim = suffix_ref.shape
@@ -160,11 +161,7 @@
     copies[1].wait()
     suffix_keys = suffix_ref[:, 0].reshape(samples * length, head_dim)
     suffix_values = suffix_ref[:, 1].reshape(samples * length, head_dim)
-    suffix_scores = dot_nt(rows, suffix_keys) * scale
-    row_sample = lax.broadcasted_iota(jnp.int32, suffix_scores.shape, 0) % samples
-    key_at = lax.broadcasted_iota(jnp.int32, suffix_scores.shape, 1)
-    mine = (key_at >= row_sample * length) & (key_at < (row_sample + 1) * length)
-    suffix_scores = jnp.where(mine, suffix_scores, NEG)
+    suffix_scores = dot_nt(rows, suffix_keys) * scale + mask_ref[...]
     peak = jnp.maximum(
         jnp.max(suffix_scores, axis=1, keepdims=True), jnp.max(scores, axis=1, keepdims=True)
     )
@@ -201,19 +198,19 @@
     )
 
 
-def project_kernel(half, start, attended_ref, weight_ref, out_ref):
+def project_kernel(half, far, start, attended_ref, weight_ref, out_ref):
     width = out_ref.shape[1]
     out_ref[...] = jnp.dot(
         attended_ref[...],
-        weight_ref[:, pl.ds(first_column(half, start, width), width)],
+        weight_ref[:, pl.ds(first_column(half, far, start, width), width)],
         preferred_element_type=jnp.float32,
     ).astype(jnp.bfloat16)
 
 
-def project(attended, weight, half, start, width):
+def project(attended, weight, half, far, start, width):
     depth = weight.shape[0]
     return pl.pallas_call(
-        functools.partial(project_kernel, half, start),
+        functools.partial(project_kernel, half, far, start),
         out_shape=jax.ShapeDtypeStruct((attended.shape[0], width), jnp.bfloat16),
         in_specs=[VMEM_SPEC, VMEM_SPEC],
         out_specs=VMEM_SPEC,
@@ -231,10 +228,10 @@
 def final_kernel(layout, *refs):
     out_ref = refs[-1]
     at = 0
-    for kind, start, width in layout:
+    for kind, far, start, width in layout:
         if kind == "split":
             for half in (1, 0):
-                out_ref[:, pl.ds(first_column(half, start, width // 2), width // 2)] = refs[at + 1 - half][...]
+                out_ref[:, pl.ds(first_column(half, far, start, width // 2), width // 2)] = refs[at + 1 - half][...]
         else:
             out_ref[:, start : start + width] = add(refs[at][...], refs[at + 1][...])
         at += 2
@@ -243,28 +240,28 @@
 def summed_over_four(attended, weight):
     columns = weight.shape[1]
     layout, start = [], 0
-    for kind, eighths in PARTS:
-        layout.append((kind, start, columns * eighths // 8))
+    for kind, far, eighths in PARTS:
+        layout.append((kind, far, start, columns * eighths // 8))
         start += columns * eighths // 8
     first = {}
     got = {}
-    for kind, start, width in layout:
+    for kind, far, start, width in layout:
         if kind == "split":
-            got[start] = swapped(project(attended, weight, 0, start, width // 2), 1)
+            got[start] = swapped(project(attended, weight, 0, far, start, width // 2), 1)
         else:
-            first[start] = project(attended, weight, None, start, width)
-            got[start] = swapped(first[start], 1 if kind == "near" else 2)
-    for kind, start, width in layout:
+            first[start] = project(attended, weight, None, far, start, width)
+            got[start] = swapped(first[start], 1 if kind == "near" else far)
+    for kind, far, start, width in layout:
         if kind == "split":
-            first[start] = project(attended, weight, 1, start, width // 2)
+            first[start] = project(attended, weight, 1, far, start, width // 2)
     operands = []
-    for kind, start, width in layout:
+    for kind, far, start, width in layout:
         total = add(first[start], got[start])
         if kind == "split":
-            total = add(total, swapped(total, 2))
+            total = add(total, swapped(total, far))
             operands += [total, swapped(total, 1)]
         else:
-            operands += [total, swapped(total, 2 if kind == "near" else 1)]
+            operands += [total, swapped(total, far if kind == "near" else 1)]
     return pl.pallas_call(
         functools.partial(final_kernel, layout),
         out_shape=jax.ShapeDtypeStruct((attended.shape[0], columns), jnp.bfloat16),
@@ -275,19 +272,23 @@
 
 
 def summed_over_any(attended, weight):
-    return lax.psum(project(attended, weight, None, 0, weight.shape[1]), "mp")
+    return lax.psum(project(attended, weight, None, 2, 0, weight.shape[1]), "mp")
 
 
 def local(queries, prefix_pool, slot_offset, suffix_kv, out_weight):
-    blocks, _, _, block, head_dim = prefix_pool.shape
+    _, _, _, block, head_dim = prefix_pool.shape
     samples, _, _, length_of_suffix, _ = suffix_kv.shape
     local_heads = queries.shape[1] // head_dim
     rows = samples * local_heads
     f32, bf16 = jnp.float32, jnp.bfloat16
-    offsets, queries_hbm, pool, suffix = [
-        pltpu.with_memory_space_constraint(x, pltpu.HBM)
-        for x in (slot_offset, queries, prefix_pool, suffix_kv)
-    ]
+    queries_hbm, suffix = [pltpu.with_memory_space_constraint(x, pltpu.HBM) for x in (queries, suffix_kv)]
+    mask = pl.pallas_call(
+        functools.partial(mask_kernel, samples),
+        out_shape=pltpu.VMEM((rows, samples * length_of_suffix), f32),
+        out_specs=VMEM_SPEC,
+        compiler_params=PARAMS,
+        cost_estimate=lasting(8),
+    )()
     length = CAPACITY * block
     gathered = pltpu.VMEM((1 + len(ASKED), length, head_dim), bf16)
     partial = (pltpu.VMEM((rows, head_dim), f32),) * 3
@@ -296,16 +297,11 @@
         functools.partial(gather_kernel, local_heads),
         out_shape=(gathered, gathered, pltpu.VMEM((1 + len(ASKED), 8, length), f32))
         + (pltpu.VMEM((2 * length + CAPACITY * FLAG_ROWS, head_dim), bf16),) * len(SENT),
-        in_specs=[HBM_SPEC] * 2,
+        in_specs=[VMEM_SPEC, pl.BlockSpec(memory_space=pltpu.SMEM), VMEM_SPEC],
         out_specs=(VMEM_SPEC,) * (3 + len(SENT)),
-        scratch_shapes=[
-            pltpu.SMEM(slot_offset.shape, jnp.int32),
-            pltpu.VMEM((blocks, 2, block, head_dim), bf16),
-            pltpu.SemaphoreType.DMA((2,)),
-        ],
         compiler_params=PARAMS,
         cost_estimate=lasting(8),
-    )(offsets, pool)
+    )(mask, slot_offset, prefix_pool)
     held = [shifted(pack, lag) for pack, lag in zip(packs, SENT)]
     answers = pl.pallas_call(
         lag_kernel,
@@ -319,7 +315,7 @@
     own = pl.pallas_call(
         functools.partial(own_kernel, local_heads),
         out_shape=partial,
-        in_specs=[VMEM_SPEC] * 4 + [HBM_SPEC] * 2,
+        in_specs=[VMEM_SPEC] * 5 + [HBM_SPEC] * 2,
         out_specs=(VMEM_SPEC,) * 3,
         scratch_shapes=[
             pltpu.VMEM(queries.shape, bf16),
@@ -328,7 +324,7 @@
         ],
         compiler_params=PARAMS,
         cost_estimate=lasting(1.6),
-    )(keys, values, bias, answers[-1], queries_hbm, suffix)
+    )(keys, values, bias, mask, answers[-1], queries_hbm, suffix)
     others = pl.pallas_call(
         held_kernel,
         out_shape=partial,

time: 32.1 us -> 31.6 us (0.984)
  starting transfers between devices: 20.5 us -> 19.1 us
  waiting for transfers between devices: 5.25 us -> 6.53 us
  Pallas kernels: 5.95 us -> 5.56 us
    ppermute x7 -> x5, starting transfers between devices: 11.3 us -> 9.88 us  [swapped(): return lax.ppermute(block, 'mp', [(i, i ^ step) for i in range(size)])]
    ppermute x7 -> x5, waiting for transfers between devices: 3.74 us -> 4.61 us  [swapped(): return lax.ppermute(block, 'mp', [(i, i ^ step) for i in range(size)])]
    ppermute x8, waiting for transfers between devices: 1.5 us -> 1.91 us  [shifted(): lax.ppermute(block, 'dp', [(i, (i + distance) % size) for i in range(size)])]
    pallas_call x1, Pallas kernels: 1.06 us -> 0.67 us  [local(): pl.pallas_call(functools.partial(gather_kernel, local_heads), out_shape=(...]
  transfers between devices with their start and end apart: 15 -> 13, of which waited for: 8 -> 6; matrix products, arithmetic and copies ran while one was open for 0% -> 0% of each run, Pallas kernels for 15% -> 14%
where the time goes in v6:
time: 31.6 us; the launch traced here: 31.4 us
  starting transfers between devices  19.1 us (60%)
  waiting for transfers between devices  6.53 us (21%)
  Pallas kernels  5.56 us (18%)
    ppermute x5, starting transfers between devices, swapped(): return lax.ppermute(block, 'mp', [(i, i ^ step) for i in range(size)])  9.88 us
    ppermute x8, starting transfers between devices, shifted(): lax.ppermute(block, 'dp', [(i, (i + distance) % size) for i in range(size)])  9.26 us
    ppermute x5, waiting for transfers between devices, swapped(): return lax.ppermute(block, 'mp', [(i, i ^ step) for i in range(size)])  4.61 us
    ppermute x8, waiting for transfers between devices, shifted(): lax.ppermute(block, 'dp', [(i, (i + distance) % size) for i in range(size)])  1.91 us
    pallas_call x1, Pallas kernels, local(): pl.pallas_call(functools.partial(own_kernel, local_heads), out_shape=part...  1.74 us
    pallas_call x3, Pallas kernels, project(): pl.pallas_call(functools.partial(project_kernel, half, far, start), out_s...  1.41 us
    pallas_call x1, Pallas kernels, summed_over_four(): pl.pallas_call(functools.partial(final_kernel, layout), out_shape=jax.Sha...  0.75 us
    pallas_call x1, Pallas kernels, local(): pl.pallas_call(functools.partial(gather_kernel, local_heads), out_shape=(...  0.67 us
  transfers between devices with their start and end apart: 13, of which 6 were waited for; matrix products, arithmetic and copies ran while one was open for 0% of the time, Pallas kernels for 14%

profile of v6, /device:TPU:0, one launch (start us, length us, event | category | flops | bytes accessed | tf_op | source)
XLA Modules:
  0.0 31.4 jit_solution(7528028293530432785)
XLA Ops:
  0.0 0.0 copy-start.2
  0.0 0.0 copy-start
  0.0 3.0 %collective-permute-start.2 = (bf16[16,512]{1,0:T(8,128)(2,1)}, bf16[16,512]{1,0:T(8,128)(2,1)S(1)}, u32[]{:S(2)}, u32[]{:S(2)}) collective-permute-start(bf16[16,512]{1,0:T(8,128)(2,1)} %query_ref.1), channel_id=1, source_target_pairs={{0,16},{4,20},{8,24},{12,28},{16,0},{20,4},{24,8},{28,12},{1,17},{... | collective-permute-start | bytes 49160 | tf_op jit(solution)/shard_map/ppermute | solution.py:32
  3.0 1.4 %collective-permute-start.1 = (bf16[16,512]{1,0:T(8,128)(2,1)}, bf16[16,512]{1,0:T(8,128)(2,1)S(1)}, u32[]{:S(2)}, u32[]{:S(2)}) collective-permute-start(bf16[16,512]{1,0:T(8,128)(2,1)} %query_ref.1), channel_id=1, source_target_pairs={{0,24},{4,28},{8,0},{12,4},{16,8},{20,12},{24,16},{28,20},{1,25},{... | collective-permute-start | bytes 49160 | tf_op jit(solution)/shard_map/ppermute | solution.py:32
  4.4 0.0 collective-permute-start
  4.4 0.0 copy-done.2
  4.5 0.0 copy-done
  4.5 0.7 %shard_map.56 = (bf16[4,256,128]{2,1,0:T(8,128)(2,1)S(1)}, bf16[4,256,128]{2,1,0:T(8,128)(2,1)S(1)}, f32[4,8,256]{2,1,0:T(8,128)S(1)}, bf16[528,128]{1,0:T(8,128)(2,1)S(1)}, bf16[528,128]{1,0:T(8,128)(2,1)S(1)}) custom-call(f32[64,768]{1,0:T(8,128)S(1)} %shard_map.55.after_ref.mask_ref, s32[6]{0:T(128)S(1)} %copy-done.2, bf16[6,2,2,128,128]{4,3,2,1,0:T(8,128)(2,1)S(1)} %copy-done), custom_call_target="tpu_custom_call" | custom-call | flops 8800000000 | bytes 29520000 | tf_op jit(solution)/shard_map/pallas_call | solution.py:296
  5.1 0.8 %collective-permute-start.3 = (bf16[528,128]{1,0:T(8,128)(2,1)S(1)}, bf16[528,128]{1,0:T(8,128)(2,1)S(1)}, u32[]{:S(2)}, u32[]{:S(2)}) collective-permute-start(bf16[528,128]{1,0:T(8,128)(2,1)S(1)} %get-tuple-element.26), channel_id=1, source_target_pairs={{0,12},{4,16},{8,20},{12,24},{16,28},{20,0},{24,4},{28,8},{1,13},{... | collective-permute-start | bytes 405512 | tf_op jit(solution)/shard_map/ppermute | solution.py:32
  5.9 1.0 %collective-permute-start.4 = (bf16[528,128]{1,0:T(8,128)(2,1)S(1)}, bf16[528,128]{1,0:T(8,128)(2,1)S(1)}, u32[]{:S(2)}, u32[]{:S(2)}) collective-permute-start(bf16[528,128]{1,0:T(8,128)(2,1)S(1)} %get-tuple-element.27), channel_id=1, source_target_pairs={{0,20},{4,24},{8,28},{12,0},{16,4},{20,8},{24,12},{28,16},{1,21},{... | collective-permute-start | bytes 405512 | tf_op jit(solution)/shard_map/ppermute | solution.py:32
  6.9 0.0 collective-permute-done.2.refs_2_
  6.9 0.0 collective-permute-done.1.refs_1_
  6.9 0.0 collective-permute-done.refs_0_
  7.0 0.4 %shard_map.57 = (bf16[64,256]{1,0:T(8,128)(2,1)S(1)}, bf16[64,256]{1,0:T(8,128)(2,1)S(1)}, bf16[64,256]{1,0:T(8,128)(2,1)S(1)}) custom-call(bf16[4,256,128]{2,1,0:T(8,128)(2,1)S(1)} %get-tuple-element.19.key_ref, bf16[4,256,128]{2,1,0:T(8,128)(2,1)S(1)} %get-tuple-element.20.value_ref, f32[4,8,256]{2,1,0:T(8,128)S(1)} %get-tuple-element.21.bias_ref, ...), custom_call_target="tpu_custom_call" | custom-call | flops 440000000 | bytes 1476000 | tf_op jit(solution)/shard_map/pallas_call | solution.py:306
  7.4 1.5 %collective-permute-start.5 = (bf16[64,256]{1,0:T(8,128)(2,1)S(1)}, bf16[64,256]{1,0:T(8,128)(2,1)S(1)}, u32[]{:S(2)}, u32[]{:S(2)}) collective-permute-start(bf16[64,256]{1,0:T(8,128)(2,1)S(1)} %get-tuple-element.31), channel_id=1, source_target_pairs={{0,4},{4,8},{8,12},{12,16},{16,20},{20,24},{24,28},{28,0},{1,5},{5... | collective-permute-start | bytes 98312 | tf_op jit(solution)/shard_map/ppermute | solution.py:32
  8.8 1.1 %collective-permute-start.6 = (bf16[64,256]{1,0:T(8,128)(2,1)S(1)}, bf16[64,256]{1,0:T(8,128)(2,1)S(1)}, u32[]{:S(2)}, u32[]{:S(2)}) collective-permute-start(bf16[64,256]{1,0:T(8,128)(2,1)S(1)} %get-tuple-element.32), channel_id=1, source_target_pairs={{0,8},{4,12},{8,16},{12,20},{16,24},{20,28},{24,0},{28,4},{1,9},{5... | collective-permute-start | bytes 98312 | tf_op jit(solution)/shard_map/ppermute | solution.py:32
  10.0 0.0 slice-start
  10.0 0.0 copy-start.1
  10.0 0.0 slice-start.1
  10.0 0.5 %collective-permute-start.7 = (bf16[64,256]{1,0:T(8,128)(2,1)S(1)}, bf16[64,256]{1,0:T(8,128)(2,1)S(1)}, u32[]{:S(2)}, u32[]{:S(2)}) collective-permute-start(bf16[64,256]{1,0:T(8,128)(2,1)S(1)} %get-tuple-element.22.after_ref), channel_id=1, source_target_pairs={{0,16},{4,20},{8,24},{12,28},{16,0},{20,4},{24,8},{28,12},{1,17},{... | collective-permute-start | bytes 98312 | tf_op jit(solution)/shard_map/ppermute | solution.py:32
  10.4 1.7 %shard_map.58 = (f32[64,128]{1,0:T(8,128)S(1)}, f32[64,128]{1,0:T(8,128)S(1)}, f32[64,128]{1,0:T(8,128)S(1)}) custom-call(bf16[4,256,128]{2,1,0:T(8,128)(2,1)S(1)} %get-tuple-element.19.key_ref, bf16[4,256,128]{2,1,0:T(8,128)(2,1)S(1)} %get-tuple-element.20.value_ref, f32[4,8,256]{2,1,0:T(8,128)S(1)} %get-tuple-element.21.bias_ref, ...), custom_call_target="tpu_custom_call" | custom-call | flops 1760000000 | bytes 5904000 | tf_op jit(solution)/shard_map/pallas_call | solution.py:315
  12.2 0.0 collective-permute-done.3.refs_0_
  12.2 0.8 %collective-permute-done.4.refs_1_ = bf16[528,128]{1,0:T(8,128)(2,1)S(1)} collective-permute-done((bf16[528,128]{1,0:T(8,128)(2,1)S(1)}, bf16[528,128]{1,0:T(8,128)(2,1)S(1)}, u32[]{:S(2)}, u32[]{:S(2)}) %collective-permute-start.4) | collective-permute-done | bytes 135200 | tf_op jit(solution)/shard_map/ppermute | solution.py:32
  13.0 0.0 copy-done.1
  13.0 0.4 %shard_map.59 = (f32[64,128]{1,0:T(8,128)S(1)}, f32[64,128]{1,0:T(8,128)S(1)}, f32[64,128]{1,0:T(8,128)S(1)}) custom-call(f32[64,128]{1,0:T(8,128)S(1)} %get-tuple-element.23.after_ref.refs_0_, bf16[16,512]{1,0:T(8,128)(2,1)S(1)} %copy-done.1, bf16[528,128]{1,0:T(8,128)(2,1)S(1)} %collective-permute-done.3.refs_0_, ...), custom_call_target="tpu_custom_call" | custom-call | flops 550000000 | bytes 1845000 | tf_op jit(solution)/shard_map/pallas_call | solution.py:328
  13.4 0.0 collective-permute-done.5.refs_6_
  13.4 0.5 %collective-permute-done.6.refs_7_ = bf16[64,256]{1,0:T(8,128)(2,1)S(1)} collective-permute-done((bf16[64,256]{1,0:T(8,128)(2,1)S(1)}, bf16[64,256]{1,0:T(8,128)(2,1)S(1)}, u32[]{:S(2)}, u32[]{:S(2)}) %collective-permute-start.6) | collective-permute-done | bytes 32800 | tf_op jit(solution)/shard_map/ppermute | solution.py:32
  13.9 0.6 %collective-permute-done.7.refs_8_ = bf16[64,256]{1,0:T(8,128)(2,1)S(1)} collective-permute-done((bf16[64,256]{1,0:T(8,128)(2,1)S(1)}, bf16[64,256]{1,0:T(8,128)(2,1)S(1)}, u32[]{:S(2)}, u32[]{:S(2)}) %collective-permute-start.7) | collective-permute-done | bytes 32800 | tf_op jit(solution)/shard_map/ppermute | solution.py:32
  14.5 0.2 shard_map.60.attended_ref
  14.7 0.0 slice-done
  14.7 0.0 slice-done.1
  14.7 0.4 %shard_map.62 = bf16[16,2048]{1,0:T(8,128)(2,1)S(1)} custom-call(bf16[16,512]{1,0:T(8,128)(2,1)S(1)} %shard_map.60.attended_ref, bf16[512,8192]{1,0:T(8,128)(2,1)S(1)} %bitcast.1), custom_call_target="tpu_custom_call" | custom-call | flops 33554432 | bytes 2097152 | tf_op jit(solution)/shard_map/pallas_call | solution.py:212
  15.1 1.6 %collective-permute-start.8 = (bf16[16,2048]{1,0:T(8,128)(2,1)S(1)}, bf16[16,2048]{1,0:T(8,128)(2,1)S(1)}, u32[]{:S(2)}, u32[]{:S(2)}) collective-permute-start(bf16[16,2048]{1,0:T(8,128)(2,1)S(1)} %shard_map.62), channel_id=1, source_target_pairs={{0,1},{1,0},{2,3},{3,2},{4,5},{5,4},{6,7},{7,6},{8,9},{9,8},{10,11... | collective-permute-start | bytes 196616 | tf_op jit(solution)/shard_map/ppermute | solution.py:37
  16.7 0.6 %shard_map.63 = bf16[16,4096]{1,0:T(8,128)(2,1)S(1)} custom-call(bf16[16,512]{1,0:T(8,128)(2,1)S(1)} %shard_map.60.attended_ref, bf16[512,8192]{1,0:T(8,128)(2,1)S(1)} %bitcast.1), custom_call_target="tpu_custom_call" | custom-call | flops 67108864 | bytes 4194304 | tf_op jit(solution)/shard_map/pallas_call | solution.py:212
  17.3 0.5 %collective-permute-start.11 = (bf16[16,4096]{1,0:T(8,128)(2,1)S(1)}, bf16[16,4096]{1,0:T(8,128)(2,1)S(1)}, u32[]{:S(2)}, u32[]{:S(2)}) collective-permute-start(bf16[16,4096]{1,0:T(8,128)(2,1)S(1)} %shard_map.63), channel_id=1, source_target_pairs={{0,1},{1,0},{2,3},{3,2},{4,5},{5,4},{6,7},{7,6},{8,9},{9,8},{10,11... | collective-permute-start | bytes 393224 | tf_op jit(solution)/shard_map/ppermute | solution.py:37
  17.8 0.4 %shard_map.61 = bf16[16,2048]{1,0:T(8,128)(2,1)S(1)} custom-call(bf16[16,512]{1,0:T(8,128)(2,1)S(1)} %shard_map.60.attended_ref, bf16[512,8192]{1,0:T(8,128)(2,1)S(1)} %bitcast.1), custom_call_target="tpu_custom_call" | custom-call | flops 33554432 | bytes 2097152 | tf_op jit(solution)/shard_map/pallas_call | solution.py:212
  18.2 1.2 %collective-permute-done.8 = bf16[16,2048]{1,0:T(8,128)(2,1)S(1)} collective-permute-done((bf16[16,2048]{1,0:T(8,128)(2,1)S(1)}, bf16[16,2048]{1,0:T(8,128)(2,1)S(1)}, u32[]{:S(2)}, u32[]{:S(2)}) %collective-permute-start.8) | collective-permute-done | bytes 65568 | tf_op jit(solution)/shard_map/ppermute | solution.py:37
  19.4 2.7 %collective-permute-start.9 = (bf16[16,2048]{1,0:T(8,128)(2,1)S(1)}, bf16[16,2048]{1,0:T(8,128)(2,1)S(1)}, u32[]{:S(2)}, u32[]{:S(2)}) collective-permute-start(bf16[16,2048]{1,0:T(8,128)(2,1)S(1)} %add_convert_fusion.2), channel_id=1, source_target_pairs={{0,2},{1,3},{2,0},{3,1},{4,6},{5,7},{6,4},{7,5},{8,10},{9,11},{10,... | collective-permute-start | bytes 196616 | tf_op jit(solution)/shard_map/ppermute | solution.py:37
  22.1 1.0 %collective-permute-done.11 = bf16[16,4096]{1,0:T(8,128)(2,1)S(1)} collective-permute-done((bf16[16,4096]{1,0:T(8,128)(2,1)S(1)}, bf16[16,4096]{1,0:T(8,128)(2,1)S(1)}, u32[]{:S(2)}, u32[]{:S(2)}) %collective-permute-start.11) | collective-permute-done | bytes 131104 | tf_op jit(solution)/shard_map/ppermute | solution.py:37
  23.1 2.6 %collective-permute-start.12 = (bf16[16,4096]{1,0:T(8,128)(2,1)S(1)}, bf16[16,4096]{1,0:T(8,128)(2,1)S(1)}, u32[]{:S(2)}, u32[]{:S(2)}) collective-permute-start(bf16[16,4096]{1,0:T(8,128)(2,1)S(1)} %add_convert_fusion.refs_2_), channel_id=1, source_target_pairs={{0,3},{1,2},{2,1},{3,0},{4,7},{5,6},{6,5},{7,4},{8,11},{9,10},{10,... | collective-permute-start | bytes 393224 | tf_op jit(solution)/shard_map/ppermute | solution.py:37
  25.7 0.0 collective-permute-done.9
  25.7 2.5 %collective-permute-start.10 = (bf16[16,2048]{1,0:T(8,128)(2,1)S(1)}, bf16[16,2048]{1,0:T(8,128)(2,1)S(1)}, u32[]{:S(2)}, u32[]{:S(2)}) collective-permute-start(bf16[16,2048]{1,0:T(8,128)(2,1)S(1)} %add_convert_fusion.1.refs_0_), channel_id=1, source_target_pairs={{0,1},{1,0},{2,3},{3,2},{4,5},{5,4},{6,7},{7,6},{8,9},{9,8},{10,11... | collective-permute-start | bytes 196616 | tf_op jit(solution)/shard_map/ppermute | solution.py:37
  28.2 2.4 %collective-permute-done.10.refs_1_ = bf16[16,2048]{1,0:T(8,128)(2,1)S(1)} collective-permute-done((bf16[16,2048]{1,0:T(8,128)(2,1)S(1)}, bf16[16,2048]{1,0:T(8,128)(2,1)S(1)}, u32[]{:S(2)}, u32[]{:S(2)}) %collective-permute-start.10) | collective-permute-done | bytes 65568 | tf_op jit(solution)/shard_map/ppermute | solution.py:37
  30.7 0.0 collective-permute-done.12.refs_3_
  30.7 0.7 %shard_map.64 = bf16[16,8192]{1,0:T(8,128)(2,1)} custom-call(bf16[16,2048]{1,0:T(8,128)(2,1)S(1)} %add_convert_fusion.1.refs_0_, bf16[16,2048]{1,0:T(8,128)(2,1)S(1)} %collective-permute-done.10.refs_1_, bf16[16,4096]{1,0:T(8,128)(2,1)S(1)} %add_convert_fusion.refs_2_, bf16[16,4096]{1,0:T(8,128)(2,1)S(1)} %collective-permute-done.12.refs_3_), custom_call_target="tpu_custom_call" | custom-call | tf_op jit(solution)/shard_map/pallas_call | solution.py:265
  (5 shorter events, 0.1 us)
Async XLA Ops:
  0.0 4.5 %copy-start.2 = (s32[6]{0:T(128)S(1)}, s32[6]{0:T(128)}, u32[]{:S(2)}) copy-start(s32[6]{0:T(128)} %offset_ref.1) | copy-start | bytes 76
  0.0 4.5 %copy-start = (bf16[6,2,2,128,128]{4,3,2,1,0:T(8,128)(2,1)S(1)}, bf16[6,2,2,128,128]{4,3,2,1,0:T(8,128)(2,1)}, u32[]{:S(2)}) copy-start(bf16[6,2,2,128,128]{4,3,2,1,0:T(8,128)(2,1)} %pool_ref.1) | copy-start | bytes 2359300
  0.0 6.9 %collective-permute-start.2 = (bf16[16,512]{1,0:T(8,128)(2,1)}, bf16[16,512]{1,0:T(8,128)(2,1)S(1)}, u32[]{:S(2)}, u32[]{:S(2)}) collective-permute-start(bf16[16,512]{1,0:T(8,128)(2,1)} %query_ref.1), channel_id=1, source_target_pairs={{0,16},{4,20},{8,24},{12,28},{16,0},{20,4},{24,8},{28,12},{1,17},{... | collective-permute-start | bytes 49160 | tf_op jit(solution)/shard_map/ppermute | solution.py:32
  3.0 4.0 %collective-permute-start.1 = (bf16[16,512]{1,0:T(8,128)(2,1)}, bf16[16,512]{1,0:T(8,128)(2,1)S(1)}, u32[]{:S(2)}, u32[]{:S(2)}) collective-permute-start(bf16[16,512]{1,0:T(8,128)(2,1)} %query_ref.1), channel_id=1, source_target_pairs={{0,24},{4,28},{8,0},{12,4},{16,8},{20,12},{24,16},{28,20},{1,25},{... | collective-permute-start | bytes 49160 | tf_op jit(solution)/shard_map/ppermute | solution.py:32
  4.4 2.5 %collective-permute-start = (bf16[16,512]{1,0:T(8,128)(2,1)}, bf16[16,512]{1,0:T(8,128)(2,1)S(1)}, u32[]{:S(2)}, u32[]{:S(2)}) collective-permute-start(bf16[16,512]{1,0:T(8,128)(2,1)} %query_ref.1), channel_id=1, source_target_pairs={{0,28},{4,0},{8,4},{12,8},{16,12},{20,16},{24,20},{28,24},{1,29},{... | collective-permute-start | bytes 49160 | tf_op jit(solution)/shard_map/ppermute | solution.py:32
  5.1 7.0 %collective-permute-start.3 = (bf16[528,128]{1,0:T(8,128)(2,1)S(1)}, bf16[528,128]{1,0:T(8,128)(2,1)S(1)}, u32[]{:S(2)}, u32[]{:S(2)}) collective-permute-start(bf16[528,128]{1,0:T(8,128)(2,1)S(1)} %get-tuple-element.26), channel_id=1, source_target_pairs={{0,12},{4,16},{8,20},{12,24},{16,28},{20,0},{24,4},{28,8},{1,13},{... | collective-permute-start | bytes 405512 | tf_op jit(solution)/shard_map/ppermute | solution.py:32
  5.9 7.1 %collective-permute-start.4 = (bf16[528,128]{1,0:T(8,128)(2,1)S(1)}, bf16[528,128]{1,0:T(8,128)(2,1)S(1)}, u32[]{:S(2)}, u32[]{:S(2)}) collective-permute-start(bf16[528,128]{1,0:T(8,128)(2,1)S(1)} %get-tuple-element.27), channel_id=1, source_target_pairs={{0,20},{4,24},{8,28},{12,0},{16,4},{20,8},{24,12},{28,16},{1,21},{... | collective-permute-start | bytes 405512 | tf_op jit(solution)/shard_map/ppermute | solution.py:32
  7.4 6.0 %collective-permute-start.5 = (bf16[64,256]{1,0:T(8,128)(2,1)S(1)}, bf16[64,256]{1,0:T(8,128)(2,1)S(1)}, u32[]{:S(2)}, u32[]{:S(2)}) collective-permute-start(bf16[64,256]{1,0:T(8,128)(2,1)S(1)} %get-tuple-element.31), channel_id=1, source_target_pairs={{0,4},{4,8},{8,12},{12,16},{16,20},{20,24},{24,28},{28,0},{1,5},{5... | collective-permute-start | bytes 98312 | tf_op jit(solution)/shard_map/ppermute | solution.py:32
  8.8 5.1 %collective-permute-start.6 = (bf16[64,256]{1,0:T(8,128)(2,1)S(1)}, bf16[64,256]{1,0:T(8,128)(2,1)S(1)}, u32[]{:S(2)}, u32[]{:S(2)}) collective-permute-start(bf16[64,256]{1,0:T(8,128)(2,1)S(1)} %get-tuple-element.32), channel_id=1, source_target_pairs={{0,8},{4,12},{8,16},{12,20},{16,24},{20,28},{24,0},{28,4},{1,9},{5... | collective-permute-start | bytes 98312 | tf_op jit(solution)/shard_map/ppermute | solution.py:32
  10.0 4.7 %slice-start = ((s8[8388608]{0:T(1024)(128)(4,1)}), s8[4194304]{0:T(1024)(128)(4,1)S(1)}, s32[]{:S(2)}) async-start(s8[8388608]{0:T(1024)(128)(4,1)} %bitcast), calls=%async_computation | async-start | bytes 8388608
  10.0 3.0 %copy-start.1 = (bf16[16,512]{1,0:T(8,128)(2,1)S(1)}, bf16[16,512]{1,0:T(8,128)(2,1)}, u32[]{:S(2)}) copy-start(bf16[16,512]{1,0:T(8,128)(2,1)} %query_ref.1) | copy-start | bytes 49156
  10.0 4.7 %slice-start.1 = ((s8[8388608]{0:T(1024)(128)(4,1)}), s8[4194304]{0:T(1024)(128)(4,1)S(1)}, s32[]{:S(2)}) async-start(s8[8388608]{0:T(1024)(128)(4,1)} %bitcast), calls=%async_computation.1 | async-start | bytes 8388608
  10.0 4.5 %collective-permute-start.7 = (bf16[64,256]{1,0:T(8,128)(2,1)S(1)}, bf16[64,256]{1,0:T(8,128)(2,1)S(1)}, u32[]{:S(2)}, u32[]{:S(2)}) collective-permute-start(bf16[64,256]{1,0:T(8,128)(2,1)S(1)} %get-tuple-element.22.after_ref), channel_id=1, source_target_pairs={{0,16},{4,20},{8,24},{12,28},{16,0},{20,4},{24,8},{28,12},{1,17},{... | collective-permute-start | bytes 98312 | tf_op jit(solution)/shard_map/ppermute | solution.py:32
  15.1 4.3 %collective-permute-start.8 = (bf16[16,2048]{1,0:T(8,128)(2,1)S(1)}, bf16[16,2048]{1,0:T(8,128)(2,1)S(1)}, u32[]{:S(2)}, u32[]{:S(2)}) collective-permute-start(bf16[16,2048]{1,0:T(8,128)(2,1)S(1)} %shard_map.62), channel_id=1, source_target_pairs={{0,1},{1,0},{2,3},{3,2},{4,5},{5,4},{6,7},{7,6},{8,9},{9,8},{10,11... | collective-permute-start | bytes 196616 | tf_op jit(solution)/shard_map/ppermute | solution.py:37
  17.3 5.7 %collective-permute-start.11 = (bf16[16,4096]{1,0:T(8,128)(2,1)S(1)}, bf16[16,4096]{1,0:T(8,128)(2,1)S(1)}, u32[]{:S(2)}, u32[]{:S(2)}) collective-permute-start(bf16[16,4096]{1,0:T(8,128)(2,1)S(1)} %shard_map.63), channel_id=1, source_target_pairs={{0,1},{1,0},{2,3},{3,2},{4,5},{5,4},{6,7},{7,6},{8,9},{9,8},{10,11... | collective-permute-start | bytes 393224 | tf_op jit(solution)/shard_map/ppermute | solution.py:37
  19.4 6.3 %collective-permute-start.9 = (bf16[16,2048]{1,0:T(8,128)(2,1)S(1)}, bf16[16,2048]{1,0:T(8,128)(2,1)S(1)}, u32[]{:S(2)}, u32[]{:S(2)}) collective-permute-start(bf16[16,2048]{1,0:T(8,128)(2,1)S(1)} %add_convert_fusion.2), channel_id=1, source_target_pairs={{0,2},{1,3},{2,0},{3,1},{4,6},{5,7},{6,4},{7,5},{8,10},{9,11},{10,... | collective-permute-start | bytes 196616 | tf_op jit(solution)/shard_map/ppermute | solution.py:37
  23.1 7.6 %collective-permute-start.12 = (bf16[16,4096]{1,0:T(8,128)(2,1)S(1)}, bf16[16,4096]{1,0:T(8,128)(2,1)S(1)}, u32[]{:S(2)}, u32[]{:S(2)}) collective-permute-start(bf16[16,4096]{1,0:T(8,128)(2,1)S(1)} %add_convert_fusion.refs_2_), channel_id=1, source_target_pairs={{0,3},{1,2},{2,1},{3,0},{4,7},{5,6},{6,5},{7,4},{8,11},{9,10},{10,... | collective-permute-start | bytes 393224 | tf_op jit(solution)/shard_map/ppermute | solution.py:37
  25.7 5.0 %collective-permute-start.10 = (bf16[16,2048]{1,0:T(8,128)(2,1)S(1)}, bf16[16,2048]{1,0:T(8,128)(2,1)S(1)}, u32[]{:S(2)}, u32[]{:S(2)}) collective-permute-start(bf16[16,2048]{1,0:T(8,128)(2,1)S(1)} %add_convert_fusion.1.refs_0_), channel_id=1, source_target_pairs={{0,1},{1,0},{2,3},{3,2},{4,5},{5,4},{6,7},{7,6},{8,9},{9,8},{10,11... | collective-permute-start | bytes 196616 | tf_op jit(solution)/shard_map/ppermute | solution.py:37

commit v7 on v6

--- a/solution.py
+++ b/solution.py
@@ -10,10 +10,11 @@
 GQA = 8
 SPREAD = 6
 CAPACITY = 2
-PARTS = (('split', 2, 4), ('near', 3, 4))
+PARTS = (("split", 2, 4), ("near", 3, 4))
 ASKED = (1, 2, 4)
 SENT = (3, 5)
 FLAG_ROWS = 8
+STAT_ROWS = 16
 NEG = -(2.0**100)
 
 VMEM_SPEC = pl.BlockSpec(memory_space=pltpu.VMEM)
@@ -122,6 +123,19 @@
     total_ref[...] = jnp.broadcast_to(total, total_ref.shape)
 
 
+def diagonal(rows, lanes):
+    shape = (rows, lanes)
+    return lax.broadcasted_iota(jnp.int32, shape, 0) == lax.broadcasted_iota(jnp.int32, shape, 1)
+
+
+def along_lanes(column, lanes):
+    return jnp.sum(jnp.where(diagonal(column.shape[0], lanes), column, 0.0), axis=0, keepdims=True)
+
+
+def along_rows(row, rows):
+    return jnp.sum(jnp.where(diagonal(rows, row.shape[1]), row, 0.0), axis=1, keepdims=True)
+
+
 def lag_kernel(key_ref, value_ref, bias_ref, *refs):
     query_refs, out_refs = refs[: len(ASKED)], refs[len(ASKED) :]
     lags = range(1, 1 + len(ASKED))
@@ -136,12 +150,12 @@
         for w, lag in zip(weights, lags)
     ]
     totals = [jnp.sum(w, axis=1, keepdims=True).astype(jnp.bfloat16) for w in weights]
-    half = (rows[0].shape[0], head_dim // 2)
+    length = rows[0].shape[0]
+    at = lax.broadcasted_iota(jnp.int32, (STAT_ROWS, head_dim), 0)
     for out_ref, acc, peak, total in zip(out_refs, accs, peaks, totals):
-        out_ref[:, :head_dim] = acc.astype(jnp.bfloat16)
-        out_ref[:, head_dim:] = jnp.concatenate(
-            [jnp.broadcast_to(peak, half), jnp.broadcast_to(total, half)], axis=1
-        )
+        out_ref[:length] = acc.astype(jnp.bfloat16)
+        laid = [along_lanes(x.astype(jnp.float32), head_dim) for x in (peak, total)]
+        out_ref[length:] = jnp.where(at == 0, laid[0], jnp.where(at == 1, laid[1], 0.0)).astype(jnp.bfloat16)
 
 
 def own_kernel(local_heads, key_ref, value_ref, bias_ref, mask_ref, after_ref, query_hbm, suffix_hbm,
@@ -179,15 +193,14 @@
     whole_refs, part_refs, out_ref = refs[:6], refs[6:-1], refs[-1]
     rows, head_dim = whole_refs[0].shape
     samples = out_ref.shape[0]
-    middle = head_dim + head_dim // 2
     accs = [ref[...] for ref in whole_refs[0::3]]
     peaks = [ref[...][:, :1] for ref in whole_refs[1::3]]
     totals = [ref[...][:, :1] for ref in whole_refs[2::3]]
     for ref in part_refs:
         part = ref[...].astype(jnp.float32)
-        accs.append(part[:, :head_dim])
-        peaks.append(part[:, head_dim : head_dim + 1])
-        totals.append(part[:, middle : middle + 1])
+        accs.append(part[:rows])
+        peaks.append(along_rows(part[rows : rows + 1], rows))
+        totals.append(along_rows(part[rows + 1 : rows + 2], rows))
     top = functools.reduce(jnp.maximum, peaks)
     shares = [jnp.exp(peak - top) for peak in peaks]
     total = sum(share * t for share, t in zip(shares, totals))
@@ -305,7 +318,7 @@
     held = [shifted(pack, lag) for pack, lag in zip(packs, SENT)]
     answers = pl.pallas_call(
         lag_kernel,
-        out_shape=(jax.ShapeDtypeStruct((rows, 2 * head_dim), bf16),) * len(ASKED),
+        out_shape=(jax.ShapeDtypeStruct((rows + STAT_ROWS, head_dim), bf16),) * len(ASKED),
         in_specs=[VMEM_SPEC] * (3 + len(ASKED)),
         out_specs=(VMEM_SPEC,) * len(ASKED),
         compiler_params=PARAMS,

time: 31.6 us -> 31.1 us (0.984)
  waiting for transfers between devices: 6.53 us -> 5.88 us
    ppermute x8, waiting for transfers between devices: 1.91 us -> 1.37 us  [shifted(): lax.ppermute(block, 'dp', [(i, (i + distance) % size) for i in range(size)])]
where the time goes in v7:
time: 31.1 us; the launch traced here: 31 us
  starting transfers between devices  19.2 us (62%)
  waiting for transfers between devices  5.88 us (19%)
  Pallas kernels  5.67 us (18%)
    ppermute x5, starting transfers between devices, swapped(): return lax.ppermute(block, 'mp', [(i, i ^ step) for i in range(size)])  9.98 us
    ppermute x8, starting transfers between devices, shifted(): lax.ppermute(block, 'dp', [(i, (i + distance) % size) for i in range(size)])  9.26 us
    ppermute x5, waiting for transfers between devices, swapped(): return lax.ppermute(block, 'mp', [(i, i ^ step) for i in range(size)])  4.52 us
    pallas_call x1, Pallas kernels, local(): pl.pallas_call(functools.partial(own_kernel, local_heads), out_shape=part...  1.74 us
    pallas_call x3, Pallas kernels, project(): pl.pallas_call(functools.partial(project_kernel, half, far, start), out_s...  1.41 us
    ppermute x8, waiting for transfers between devices, shifted(): lax.ppermute(block, 'dp', [(i, (i + distance) % size) for i in range(size)])  1.37 us
    pallas_call x1, Pallas kernels, summed_over_four(): pl.pallas_call(functools.partial(final_kernel, layout), out_shape=jax.Sha...  0.75 us
    pallas_call x1, Pallas kernels, local(): pl.pallas_call(functools.partial(gather_kernel, local_heads), out_shape=(...  0.67 us
  transfers between devices with their start and end apart: 13, of which 6 were waited for; matrix products, arithmetic and copies ran while one was open for 0% of the time, Pallas kernels for 14%

profile of v7, /device:TPU:0, one launch (start us, length us, event | category | flops | bytes accessed | tf_op | source)
XLA Modules:
  0.0 31.0 jit_solution(16940675996977786364)
XLA Ops:
  0.0 0.0 copy-start.2
  0.0 0.0 copy-start
  0.0 3.0 %collective-permute-start.2 = (bf16[16,512]{1,0:T(8,128)(2,1)}, bf16[16,512]{1,0:T(8,128)(2,1)S(1)}, u32[]{:S(2)}, u32[]{:S(2)}) collective-permute-start(bf16[16,512]{1,0:T(8,128)(2,1)} %query_ref.1), channel_id=1, source_target_pairs={{0,16},{4,20},{8,24},{12,28},{16,0},{20,4},{24,8},{28,12},{1,17},{... | collective-permute-start | bytes 49160 | tf_op jit(solution)/shard_map/ppermute | solution.py:33
  3.0 1.4 %collective-permute-start.1 = (bf16[16,512]{1,0:T(8,128)(2,1)}, bf16[16,512]{1,0:T(8,128)(2,1)S(1)}, u32[]{:S(2)}, u32[]{:S(2)}) collective-permute-start(bf16[16,512]{1,0:T(8,128)(2,1)} %query_ref.1), channel_id=1, source_target_pairs={{0,24},{4,28},{8,0},{12,4},{16,8},{20,12},{24,16},{28,20},{1,25},{... | collective-permute-start | bytes 49160 | tf_op jit(solution)/shard_map/ppermute | solution.py:33
  4.4 0.0 collective-permute-start
  4.4 0.0 copy-done.2
  4.5 0.0 copy-done
  4.5 0.7 %shard_map.56 = (bf16[4,256,128]{2,1,0:T(8,128)(2,1)S(1)}, bf16[4,256,128]{2,1,0:T(8,128)(2,1)S(1)}, f32[4,8,256]{2,1,0:T(8,128)S(1)}, bf16[528,128]{1,0:T(8,128)(2,1)S(1)}, bf16[528,128]{1,0:T(8,128)(2,1)S(1)}) custom-call(f32[64,768]{1,0:T(8,128)S(1)} %shard_map.55.after_ref.mask_ref, s32[6]{0:T(128)S(1)} %copy-done.2, bf16[6,2,2,128,128]{4,3,2,1,0:T(8,128)(2,1)S(1)} %copy-done), custom_call_target="tpu_custom_call" | custom-call | flops 8800000000 | bytes 29520000 | tf_op jit(solution)/shard_map/pallas_call | solution.py:309
  5.1 0.8 %collective-permute-start.3 = (bf16[528,128]{1,0:T(8,128)(2,1)S(1)}, bf16[528,128]{1,0:T(8,128)(2,1)S(1)}, u32[]{:S(2)}, u32[]{:S(2)}) collective-permute-start(bf16[528,128]{1,0:T(8,128)(2,1)S(1)} %get-tuple-element.26), channel_id=1, source_target_pairs={{0,12},{4,16},{8,20},{12,24},{16,28},{20,0},{24,4},{28,8},{1,13},{... | collective-permute-start | bytes 405512 | tf_op jit(solution)/shard_map/ppermute | solution.py:33
  5.9 1.0 %collective-permute-start.4 = (bf16[528,128]{1,0:T(8,128)(2,1)S(1)}, bf16[528,128]{1,0:T(8,128)(2,1)S(1)}, u32[]{:S(2)}, u32[]{:S(2)}) collective-permute-start(bf16[528,128]{1,0:T(8,128)(2,1)S(1)} %get-tuple-element.27), channel_id=1, source_target_pairs={{0,20},{4,24},{8,28},{12,0},{16,4},{20,8},{24,12},{28,16},{1,21},{... | collective-permute-start | bytes 405512 | tf_op jit(solution)/shard_map/ppermute | solution.py:33
  6.9 0.0 collective-permute-done.2.refs_2_
  6.9 0.0 collective-permute-done.1.refs_1_
  6.9 0.0 collective-permute-done.refs_0_
  7.0 0.4 %shard_map.57 = (bf16[80,128]{1,0:T(8,128)(2,1)S(1)}, bf16[80,128]{1,0:T(8,128)(2,1)S(1)}, bf16[80,128]{1,0:T(8,128)(2,1)S(1)}) custom-call(bf16[4,256,128]{2,1,0:T(8,128)(2,1)S(1)} %get-tuple-element.19.key_ref, bf16[4,256,128]{2,1,0:T(8,128)(2,1)S(1)} %get-tuple-element.20.value_ref, f32[4,8,256]{2,1,0:T(8,128)S(1)} %get-tuple-element.21.bias_ref, ...), custom_call_target="tpu_custom_call" | custom-call | flops 440000000 | bytes 1476000 | tf_op jit(solution)/shard_map/pallas_call | solution.py:319
  7.4 1.5 %collective-permute-start.5 = (bf16[80,128]{1,0:T(8,128)(2,1)S(1)}, bf16[80,128]{1,0:T(8,128)(2,1)S(1)}, u32[]{:S(2)}, u32[]{:S(2)}) collective-permute-start(bf16[80,128]{1,0:T(8,128)(2,1)S(1)} %get-tuple-element.31), channel_id=1, source_target_pairs={{0,4},{4,8},{8,12},{12,16},{16,20},{20,24},{24,28},{28,0},{1,5},{5... | collective-permute-start | bytes 61448 | tf_op jit(solution)/shard_map/ppermute | solution.py:33
  8.8 1.1 %collective-permute-start.6 = (bf16[80,128]{1,0:T(8,128)(2,1)S(1)}, bf16[80,128]{1,0:T(8,128)(2,1)S(1)}, u32[]{:S(2)}, u32[]{:S(2)}) collective-permute-start(bf16[80,128]{1,0:T(8,128)(2,1)S(1)} %get-tuple-element.32), channel_id=1, source_target_pairs={{0,8},{4,12},{8,16},{12,20},{16,24},{20,28},{24,0},{28,4},{1,9},{5... | collective-permute-start | bytes 61448 | tf_op jit(solution)/shard_map/ppermute | solution.py:33
  10.0 0.0 slice-start
  10.0 0.0 copy-start.1
  10.0 0.0 slice-start.1
  10.0 0.5 %collective-permute-start.7 = (bf16[80,128]{1,0:T(8,128)(2,1)S(1)}, bf16[80,128]{1,0:T(8,128)(2,1)S(1)}, u32[]{:S(2)}, u32[]{:S(2)}) collective-permute-start(bf16[80,128]{1,0:T(8,128)(2,1)S(1)} %get-tuple-element.22.after_ref), channel_id=1, source_target_pairs={{0,16},{4,20},{8,24},{12,28},{16,0},{20,4},{24,8},{28,12},{1,17},{... | collective-permute-start | bytes 61448 | tf_op jit(solution)/shard_map/ppermute | solution.py:33
  10.4 1.7 %shard_map.58 = (f32[64,128]{1,0:T(8,128)S(1)}, f32[64,128]{1,0:T(8,128)S(1)}, f32[64,128]{1,0:T(8,128)S(1)}) custom-call(bf16[4,256,128]{2,1,0:T(8,128)(2,1)S(1)} %get-tuple-element.19.key_ref, bf16[4,256,128]{2,1,0:T(8,128)(2,1)S(1)} %get-tuple-element.20.value_ref, f32[4,8,256]{2,1,0:T(8,128)S(1)} %get-tuple-element.21.bias_ref, ...), custom_call_target="tpu_custom_call" | custom-call | flops 1760000000 | bytes 5904000 | tf_op jit(solution)/shard_map/pallas_call | solution.py:328
  12.2 0.0 collective-permute-done.3.refs_0_
  12.2 0.1 collective-permute-done.4.refs_1_
  12.3 0.0 copy-done.1
  12.3 0.4 %shard_map.59 = (f32[64,128]{1,0:T(8,128)S(1)}, f32[64,128]{1,0:T(8,128)S(1)}, f32[64,128]{1,0:T(8,128)S(1)}) custom-call(f32[64,128]{1,0:T(8,128)S(1)} %get-tuple-element.23.after_ref.refs_0_, bf16[16,512]{1,0:T(8,128)(2,1)S(1)} %copy-done.1, bf16[528,128]{1,0:T(8,128)(2,1)S(1)} %collective-permute-done.3.refs_0_, ...), custom_call_target="tpu_custom_call" | custom-call | flops 550000000 | bytes 1845000 | tf_op jit(solution)/shard_map/pallas_call | solution.py:341
  12.7 0.0 collective-permute-done.5.refs_6_
  12.7 0.9 %collective-permute-done.6.refs_7_ = bf16[80,128]{1,0:T(8,128)(2,1)S(1)} collective-permute-done((bf16[80,128]{1,0:T(8,128)(2,1)S(1)}, bf16[80,128]{1,0:T(8,128)(2,1)S(1)}, u32[]{:S(2)}, u32[]{:S(2)}) %collective-permute-start.6) | collective-permute-done | bytes 20512 | tf_op jit(solution)/shard_map/ppermute | solution.py:33
  13.5 0.4 %collective-permute-done.7.refs_8_ = bf16[80,128]{1,0:T(8,128)(2,1)S(1)} collective-permute-done((bf16[80,128]{1,0:T(8,128)(2,1)S(1)}, bf16[80,128]{1,0:T(8,128)(2,1)S(1)}, u32[]{:S(2)}, u32[]{:S(2)}) %collective-permute-start.7) | collective-permute-done | bytes 20512 | tf_op jit(solution)/shard_map/ppermute | solution.py:33
  14.0 0.3 shard_map.60.attended_ref
  14.2 0.0 slice-done
  14.2 0.0 slice-done.1
  14.3 0.4 %shard_map.62 = bf16[16,2048]{1,0:T(8,128)(2,1)S(1)} custom-call(bf16[16,512]{1,0:T(8,128)(2,1)S(1)} %shard_map.60.attended_ref, bf16[512,8192]{1,0:T(8,128)(2,1)S(1)} %bitcast.1), custom_call_target="tpu_custom_call" | custom-call | flops 33554432 | bytes 2097152 | tf_op jit(solution)/shard_map/pallas_call | solution.py:225
  14.6 1.6 %collective-permute-start.8 = (bf16[16,2048]{1,0:T(8,128)(2,1)S(1)}, bf16[16,2048]{1,0:T(8,128)(2,1)S(1)}, u32[]{:S(2)}, u32[]{:S(2)}) collective-permute-start(bf16[16,2048]{1,0:T(8,128)(2,1)S(1)} %shard_map.62), channel_id=1, source_target_pairs={{0,1},{1,0},{2,3},{3,2},{4,5},{5,4},{6,7},{7,6},{8,9},{9,8},{10,11... | collective-permute-start | bytes 196616 | tf_op jit(solution)/shard_map/ppermute | solution.py:38
  16.2 0.6 %shard_map.63 = bf16[16,4096]{1,0:T(8,128)(2,1)S(1)} custom-call(bf16[16,512]{1,0:T(8,128)(2,1)S(1)} %shard_map.60.attended_ref, bf16[512,8192]{1,0:T(8,128)(2,1)S(1)} %bitcast.1), custom_call_target="tpu_custom_call" | custom-call | flops 67108864 | bytes 4194304 | tf_op jit(solution)/shard_map/pallas_call | solution.py:225
  16.9 0.5 %collective-permute-start.11 = (bf16[16,4096]{1,0:T(8,128)(2,1)S(1)}, bf16[16,4096]{1,0:T(8,128)(2,1)S(1)}, u32[]{:S(2)}, u32[]{:S(2)}) collective-permute-start(bf16[16,4096]{1,0:T(8,128)(2,1)S(1)} %shard_map.63), channel_id=1, source_target_pairs={{0,1},{1,0},{2,3},{3,2},{4,5},{5,4},{6,7},{7,6},{8,9},{9,8},{10,11... | collective-permute-start | bytes 393224 | tf_op jit(solution)/shard_map/ppermute | solution.py:38
  17.4 0.4 %shard_map.61 = bf16[16,2048]{1,0:T(8,128)(2,1)S(1)} custom-call(bf16[16,512]{1,0:T(8,128)(2,1)S(1)} %shard_map.60.attended_ref, bf16[512,8192]{1,0:T(8,128)(2,1)S(1)} %bitcast.1), custom_call_target="tpu_custom_call" | custom-call | flops 33554432 | bytes 2097152 | tf_op jit(solution)/shard_map/pallas_call | solution.py:225
  17.7 1.3 %collective-permute-done.8 = bf16[16,2048]{1,0:T(8,128)(2,1)S(1)} collective-permute-done((bf16[16,2048]{1,0:T(8,128)(2,1)S(1)}, bf16[16,2048]{1,0:T(8,128)(2,1)S(1)}, u32[]{:S(2)}, u32[]{:S(2)}) %collective-permute-start.8) | collective-permute-done | bytes 65568 | tf_op jit(solution)/shard_map/ppermute | solution.py:38
  19.0 2.7 %collective-permute-start.9 = (bf16[16,2048]{1,0:T(8,128)(2,1)S(1)}, bf16[16,2048]{1,0:T(8,128)(2,1)S(1)}, u32[]{:S(2)}, u32[]{:S(2)}) collective-permute-start(bf16[16,2048]{1,0:T(8,128)(2,1)S(1)} %add_convert_fusion.2), channel_id=1, source_target_pairs={{0,2},{1,3},{2,0},{3,1},{4,6},{5,7},{6,4},{7,5},{8,10},{9,11},{10,... | collective-permute-start | bytes 196616 | tf_op jit(solution)/shard_map/ppermute | solution.py:38
  21.7 0.9 %collective-permute-done.11 = bf16[16,4096]{1,0:T(8,128)(2,1)S(1)} collective-permute-done((bf16[16,4096]{1,0:T(8,128)(2,1)S(1)}, bf16[16,4096]{1,0:T(8,128)(2,1)S(1)}, u32[]{:S(2)}, u32[]{:S(2)}) %collective-permute-start.11) | collective-permute-done | bytes 131104 | tf_op jit(solution)/shard_map/ppermute | solution.py:38
  22.6 2.5 %collective-permute-start.12 = (bf16[16,4096]{1,0:T(8,128)(2,1)S(1)}, bf16[16,4096]{1,0:T(8,128)(2,1)S(1)}, u32[]{:S(2)}, u32[]{:S(2)}) collective-permute-start(bf16[16,4096]{1,0:T(8,128)(2,1)S(1)} %add_convert_fusion.refs_2_), channel_id=1, source_target_pairs={{0,3},{1,2},{2,1},{3,0},{4,7},{5,6},{6,5},{7,4},{8,11},{9,10},{10,... | collective-permute-start | bytes 393224 | tf_op jit(solution)/shard_map/ppermute | solution.py:38
  25.1 0.0 collective-permute-done.9
  25.2 2.7 %collective-permute-start.10 = (bf16[16,2048]{1,0:T(8,128)(2,1)S(1)}, bf16[16,2048]{1,0:T(8,128)(2,1)S(1)}, u32[]{:S(2)}, u32[]{:S(2)}) collective-permute-start(bf16[16,2048]{1,0:T(8,128)(2,1)S(1)} %add_convert_fusion.1.refs_0_), channel_id=1, source_target_pairs={{0,1},{1,0},{2,3},{3,2},{4,5},{5,4},{6,7},{7,6},{8,9},{9,8},{10,11... | collective-permute-start | bytes 196616 | tf_op jit(solution)/shard_map/ppermute | solution.py:38
  27.9 2.3 %collective-permute-done.10.refs_1_ = bf16[16,2048]{1,0:T(8,128)(2,1)S(1)} collective-permute-done((bf16[16,2048]{1,0:T(8,128)(2,1)S(1)}, bf16[16,2048]{1,0:T(8,128)(2,1)S(1)}, u32[]{:S(2)}, u32[]{:S(2)}) %collective-permute-start.10) | collective-permute-done | bytes 65568 | tf_op jit(solution)/shard_map/ppermute | solution.py:38
  30.2 0.0 collective-permute-done.12.refs_3_
  30.2 0.7 %shard_map.64 = bf16[16,8192]{1,0:T(8,128)(2,1)} custom-call(bf16[16,2048]{1,0:T(8,128)(2,1)S(1)} %add_convert_fusion.1.refs_0_, bf16[16,2048]{1,0:T(8,128)(2,1)S(1)} %collective-permute-done.10.refs_1_, bf16[16,4096]{1,0:T(8,128)(2,1)S(1)} %add_convert_fusion.refs_2_, bf16[16,4096]{1,0:T(8,128)(2,1)S(1)} %collective-permute-done.12.refs_3_), custom_call_target="tpu_custom_call" | custom-call | tf_op jit(solution)/shard_map/pallas_call | solution.py:278
  (5 shorter events, 0.1 us)
Async XLA Ops:
  0.0 4.5 %copy-start.2 = (s32[6]{0:T(128)S(1)}, s32[6]{0:T(128)}, u32[]{:S(2)}) copy-start(s32[6]{0:T(128)} %offset_ref.1) | copy-start | bytes 76
  0.0 4.5 %copy-start = (bf16[6,2,2,128,128]{4,3,2,1,0:T(8,128)(2,1)S(1)}, bf16[6,2,2,128,128]{4,3,2,1,0:T(8,128)(2,1)}, u32[]{:S(2)}) copy-start(bf16[6,2,2,128,128]{4,3,2,1,0:T(8,128)(2,1)} %pool_ref.1) | copy-start | bytes 2359300
  0.0 6.9 %collective-permute-start.2 = (bf16[16,512]{1,0:T(8,128)(2,1)}, bf16[16,512]{1,0:T(8,128)(2,1)S(1)}, u32[]{:S(2)}, u32[]{:S(2)}) collective-permute-start(bf16[16,512]{1,0:T(8,128)(2,1)} %query_ref.1), channel_id=1, source_target_pairs={{0,16},{4,20},{8,24},{12,28},{16,0},{20,4},{24,8},{28,12},{1,17},{... | collective-permute-start | bytes 49160 | tf_op jit(solution)/shard_map/ppermute | solution.py:33
  3.0 4.0 %collective-permute-start.1 = (bf16[16,512]{1,0:T(8,128)(2,1)}, bf16[16,512]{1,0:T(8,128)(2,1)S(1)}, u32[]{:S(2)}, u32[]{:S(2)}) collective-permute-start(bf16[16,512]{1,0:T(8,128)(2,1)} %query_ref.1), channel_id=1, source_target_pairs={{0,24},{4,28},{8,0},{12,4},{16,8},{20,12},{24,16},{28,20},{1,25},{... | collective-permute-start | bytes 49160 | tf_op jit(solution)/shard_map/ppermute | solution.py:33
  4.4 2.5 %collective-permute-start = (bf16[16,512]{1,0:T(8,128)(2,1)}, bf16[16,512]{1,0:T(8,128)(2,1)S(1)}, u32[]{:S(2)}, u32[]{:S(2)}) collective-permute-start(bf16[16,512]{1,0:T(8,128)(2,1)} %query_ref.1), channel_id=1, source_target_pairs={{0,28},{4,0},{8,4},{12,8},{16,12},{20,16},{24,20},{28,24},{1,29},{... | collective-permute-start | bytes 49160 | tf_op jit(solution)/shard_map/ppermute | solution.py:33
  5.1 7.0 %collective-permute-start.3 = (bf16[528,128]{1,0:T(8,128)(2,1)S(1)}, bf16[528,128]{1,0:T(8,128)(2,1)S(1)}, u32[]{:S(2)}, u32[]{:S(2)}) collective-permute-start(bf16[528,128]{1,0:T(8,128)(2,1)S(1)} %get-tuple-element.26), channel_id=1, source_target_pairs={{0,12},{4,16},{8,20},{12,24},{16,28},{20,0},{24,4},{28,8},{1,13},{... | collective-permute-start | bytes 405512 | tf_op jit(solution)/shard_map/ppermute | solution.py:33
  5.9 6.4 %collective-permute-start.4 = (bf16[528,128]{1,0:T(8,128)(2,1)S(1)}, bf16[528,128]{1,0:T(8,128)(2,1)S(1)}, u32[]{:S(2)}, u32[]{:S(2)}) collective-permute-start(bf16[528,128]{1,0:T(8,128)(2,1)S(1)} %get-tuple-element.27), channel_id=1, source_target_pairs={{0,20},{4,24},{8,28},{12,0},{16,4},{20,8},{24,12},{28,16},{1,21},{... | collective-permute-start | bytes 405512 | tf_op jit(solution)/shard_map/ppermute | solution.py:33
  7.4 5.3 %collective-permute-start.5 = (bf16[80,128]{1,0:T(8,128)(2,1)S(1)}, bf16[80,128]{1,0:T(8,128)(2,1)S(1)}, u32[]{:S(2)}, u32[]{:S(2)}) collective-permute-start(bf16[80,128]{1,0:T(8,128)(2,1)S(1)} %get-tuple-element.31), channel_id=1, source_target_pairs={{0,4},{4,8},{8,12},{12,16},{16,20},{20,24},{24,28},{28,0},{1,5},{5... | collective-permute-start | bytes 61448 | tf_op jit(solution)/shard_map/ppermute | solution.py:33
  8.8 4.7 %collective-permute-start.6 = (bf16[80,128]{1,0:T(8,128)(2,1)S(1)}, bf16[80,128]{1,0:T(8,128)(2,1)S(1)}, u32[]{:S(2)}, u32[]{:S(2)}) collective-permute-start(bf16[80,128]{1,0:T(8,128)(2,1)S(1)} %get-tuple-element.32), channel_id=1, source_target_pairs={{0,8},{4,12},{8,16},{12,20},{16,24},{20,28},{24,0},{28,4},{1,9},{5... | collective-permute-start | bytes 61448 | tf_op jit(solution)/shard_map/ppermute | solution.py:33
  10.0 4.3 %slice-start = ((s8[8388608]{0:T(1024)(128)(4,1)}), s8[4194304]{0:T(1024)(128)(4,1)S(1)}, s32[]{:S(2)}) async-start(s8[8388608]{0:T(1024)(128)(4,1)} %bitcast), calls=%async_computation | async-start | bytes 8388608
  10.0 2.3 %copy-start.1 = (bf16[16,512]{1,0:T(8,128)(2,1)S(1)}, bf16[16,512]{1,0:T(8,128)(2,1)}, u32[]{:S(2)}) copy-start(bf16[16,512]{1,0:T(8,128)(2,1)} %query_ref.1) | copy-start | bytes 49156
  10.0 4.3 %slice-start.1 = ((s8[8388608]{0:T(1024)(128)(4,1)}), s8[4194304]{0:T(1024)(128)(4,1)S(1)}, s32[]{:S(2)}) async-start(s8[8388608]{0:T(1024)(128)(4,1)} %bitcast), calls=%async_computation.1 | async-start | bytes 8388608
  10.0 4.0 %collective-permute-start.7 = (bf16[80,128]{1,0:T(8,128)(2,1)S(1)}, bf16[80,128]{1,0:T(8,128)(2,1)S(1)}, u32[]{:S(2)}, u32[]{:S(2)}) collective-permute-start(bf16[80,128]{1,0:T(8,128)(2,1)S(1)} %get-tuple-element.22.after_ref), channel_id=1, source_target_pairs={{0,16},{4,20},{8,24},{12,28},{16,0},{20,4},{24,8},{28,12},{1,17},{... | collective-permute-start | bytes 61448 | tf_op jit(solution)/shard_map/ppermute | solution.py:33
  14.6 4.3 %collective-permute-start.8 = (bf16[16,2048]{1,0:T(8,128)(2,1)S(1)}, bf16[16,2048]{1,0:T(8,128)(2,1)S(1)}, u32[]{:S(2)}, u32[]{:S(2)}) collective-permute-start(bf16[16,2048]{1,0:T(8,128)(2,1)S(1)} %shard_map.62), channel_id=1, source_target_pairs={{0,1},{1,0},{2,3},{3,2},{4,5},{5,4},{6,7},{7,6},{8,9},{9,8},{10,11... | collective-permute-start | bytes 196616 | tf_op jit(solution)/shard_map/ppermute | solution.py:38
  16.9 5.7 %collective-permute-start.11 = (bf16[16,4096]{1,0:T(8,128)(2,1)S(1)}, bf16[16,4096]{1,0:T(8,128)(2,1)S(1)}, u32[]{:S(2)}, u32[]{:S(2)}) collective-permute-start(bf16[16,4096]{1,0:T(8,128)(2,1)S(1)} %shard_map.63), channel_id=1, source_target_pairs={{0,1},{1,0},{2,3},{3,2},{4,5},{5,4},{6,7},{7,6},{8,9},{9,8},{10,11... | collective-permute-start | bytes 393224 | tf_op jit(solution)/shard_map/ppermute | solution.py:38
  19.0 6.1 %collective-permute-start.9 = (bf16[16,2048]{1,0:T(8,128)(2,1)S(1)}, bf16[16,2048]{1,0:T(8,128)(2,1)S(1)}, u32[]{:S(2)}, u32[]{:S(2)}) collective-permute-start(bf16[16,2048]{1,0:T(8,128)(2,1)S(1)} %add_convert_fusion.2), channel_id=1, source_target_pairs={{0,2},{1,3},{2,0},{3,1},{4,6},{5,7},{6,4},{7,5},{8,10},{9,11},{10,... | collective-permute-start | bytes 196616 | tf_op jit(solution)/shard_map/ppermute | solution.py:38
  22.6 7.6 %collective-permute-start.12 = (bf16[16,4096]{1,0:T(8,128)(2,1)S(1)}, bf16[16,4096]{1,0:T(8,128)(2,1)S(1)}, u32[]{:S(2)}, u32[]{:S(2)}) collective-permute-start(bf16[16,4096]{1,0:T(8,128)(2,1)S(1)} %add_convert_fusion.refs_2_), channel_id=1, source_target_pairs={{0,3},{1,2},{2,1},{3,0},{4,7},{5,6},{6,5},{7,4},{8,11},{9,10},{10,... | collective-permute-start | bytes 393224 | tf_op jit(solution)/shard_map/ppermute | solution.py:38
  25.2 5.1 %collective-permute-start.10 = (bf16[16,2048]{1,0:T(8,128)(2,1)S(1)}, bf16[16,2048]{1,0:T(8,128)(2,1)S(1)}, u32[]{:S(2)}, u32[]{:S(2)}) collective-permute-start(bf16[16,2048]{1,0:T(8,128)(2,1)S(1)} %add_convert_fusion.1.refs_0_), channel_id=1, source_target_pairs={{0,1},{1,0},{2,3},{3,2},{4,5},{5,4},{6,7},{7,6},{8,9},{9,8},{10,11... | collective-permute-start | bytes 196616 | tf_op jit(solution)/shard_map/ppermute | solution.py:38

commit v8 on v7

--- a/solution.py
+++ b/solution.py
@@ -189,8 +189,12 @@
     total_ref[...] = jnp.broadcast_to(total, total_ref.shape)
 
 
-def merge_kernel(*refs):
-    whole_refs, part_refs, out_ref = refs[:6], refs[6:-1], refs[-1]
+def merge_kernel(first, *refs):
+    if first is not None:
+        *refs, weight_ref, out_ref, sent_ref = refs
+    else:
+        *refs, out_ref = refs
+    whole_refs, part_refs = refs[:6], refs[6:]
     rows, head_dim = whole_refs[0].shape
     samples = out_ref.shape[0]
     accs = [ref[...] for ref in whole_refs[0::3]]
@@ -206,9 +210,17 @@
     total = sum(share * t for share, t in zip(shares, totals))
     acc = sum(share * a for share, a in zip(shares, accs))
     attended = (acc / total).astype(jnp.bfloat16)
-    out_ref[...] = jnp.concatenate(
+    attended = jnp.concatenate(
         [attended[h * samples : (h + 1) * samples] for h in range(rows // samples)], axis=1
     )
+    out_ref[...] = attended
+    if first is not None:
+        width = sent_ref.shape[1]
+        sent_ref[...] = jnp.dot(
+            attended,
+            weight_ref[:, pl.ds(first_column(*first, width), width)],
+            preferred_element_type=jnp.float32,
+        ).astype(jnp.bfloat16)
 
 
 def project_kernel(half, far, start, attended_ref, weight_ref, out_ref):
@@ -250,7 +262,7 @@
         at += 2
 
 
-def summed_over_four(attended, weight):
+def summed_over_four(attended, sent, weight):
     columns = weight.shape[1]
     layout, start = [], 0
     for kind, far, eighths in PARTS:
@@ -260,7 +272,7 @@
     got = {}
     for kind, far, start, width in layout:
         if kind == "split":
-            got[start] = swapped(project(attended, weight, 0, far, start, width // 2), 1)
+            got[start] = swapped(sent, 1)
         else:
             first[start] = project(attended, weight, None, far, start, width)
             got[start] = swapped(first[start], 1 if kind == "near" else far)
@@ -346,16 +358,21 @@
         compiler_params=PARAMS,
         cost_estimate=lasting(0.5),
     )(own[0], queries, *held)
-    attended = pl.pallas_call(
-        merge_kernel,
-        out_shape=jax.ShapeDtypeStruct(queries.shape, bf16),
-        in_specs=[VMEM_SPEC] * (6 + len(ASKED)),
-        out_specs=VMEM_SPEC,
+    four = lax.axis_size("mp") == 4
+    (_, far, eighths), columns = PARTS[0], out_weight.shape[1]
+    shapes = [jax.ShapeDtypeStruct(queries.shape, bf16)]
+    if four:
+        shapes.append(jax.ShapeDtypeStruct((samples, columns * eighths // 16), bf16))
+    attended, *sent = pl.pallas_call(
+        functools.partial(merge_kernel, (0, far, 0) if four else None),
+        out_shape=tuple(shapes),
+        in_specs=[VMEM_SPEC] * (6 + len(ASKED) + four),
+        out_specs=(VMEM_SPEC,) * len(shapes),
         compiler_params=PARAMS,
         cost_estimate=lasting(0.2),
-    )(*own, *others, *parts)
-    if lax.axis_size("mp") == 4:
-        return summed_over_four(attended, out_weight)
+    )(*own, *others, *parts, *([out_weight] if four else []))
+    if four:
+        return summed_over_four(attended, sent[0], out_weight)
     return summed_over_any(attended, out_weight)
 
 

time: 31.1 us -> 31.1 us (level)
  waiting for transfers between devices: 5.88 us -> 6.58 us
  starting transfers between devices: 19.2 us -> 18.6 us
    ppermute x5, waiting for transfers between devices: 4.52 us -> 5.21 us  [swapped(): return lax.ppermute(block, 'mp', [(i, i ^ step) for i in range(size)])]
    ppermute x5, starting transfers between devices: 9.98 us -> 9.32 us  [swapped(): return lax.ppermute(block, 'mp', [(i, i ^ step) for i in range(size)])]
    pallas_call x3 -> x2, Pallas kernels: 1.41 us -> 1.02 us  [project(): pl.pallas_call(functools.partial(project_kernel, half, far, start), out_s...]
where the time goes in v8:
time: 31.1 us; the launch traced here: 30.9 us
  starting transfers between devices  18.6 us (60%)
  waiting for transfers between devices  6.58 us (21%)
  Pallas kernels  5.58 us (18%)
    ppermute x5, starting transfers between devices, swapped(): return lax.ppermute(block, 'mp', [(i, i ^ step) for i in range(size)])  9.32 us
    ppermute x8, starting transfers between devices, shifted(): lax.ppermute(block, 'dp', [(i, (i + distance) % size) for i in range(size)])  9.26 us
    ppermute x5, waiting for transfers between devices, swapped(): return lax.ppermute(block, 'mp', [(i, i ^ step) for i in range(size)])  5.21 us
    pallas_call x1, Pallas kernels, local(): pl.pallas_call(functools.partial(own_kernel, local_heads), out_shape=part...  1.74 us
    ppermute x8, waiting for transfers between devices, shifted(): lax.ppermute(block, 'dp', [(i, (i + distance) % size) for i in range(size)])  1.37 us
    pallas_call x2, Pallas kernels, project(): pl.pallas_call(functools.partial(project_kernel, half, far, start), out_s...  1.02 us
    pallas_call x1, Pallas kernels, summed_over_four(): pl.pallas_call(functools.partial(final_kernel, layout), out_shape=jax.Sha...  0.75 us
    pallas_call x1, Pallas kernels, local(): pl.pallas_call(functools.partial(gather_kernel, local_heads), out_shape=(...  0.67 us
  transfers between devices with their start and end apart: 13, of which 6 were waited for; matrix products, arithmetic and copies ran while one was open for 0% of the time, Pallas kernels for 14%

profile of v8, /device:TPU:0, one launch (start us, length us, event | category | flops | bytes accessed | tf_op | source)
XLA Modules:
  0.0 30.9 jit_solution(11160850422987682838)
XLA Ops:
  0.0 0.0 copy-start.2
  0.0 0.0 copy-start
  0.0 3.0 %collective-permute-start.2 = (bf16[16,512]{1,0:T(8,128)(2,1)}, bf16[16,512]{1,0:T(8,128)(2,1)S(1)}, u32[]{:S(2)}, u32[]{:S(2)}) collective-permute-start(bf16[16,512]{1,0:T(8,128)(2,1)} %query_ref.1), channel_id=1, source_target_pairs={{0,16},{4,20},{8,24},{12,28},{16,0},{20,4},{24,8},{28,12},{1,17},{... | collective-permute-start | bytes 49160 | tf_op jit(solution)/shard_map/ppermute | solution.py:33
  3.0 1.4 %collective-permute-start.1 = (bf16[16,512]{1,0:T(8,128)(2,1)}, bf16[16,512]{1,0:T(8,128)(2,1)S(1)}, u32[]{:S(2)}, u32[]{:S(2)}) collective-permute-start(bf16[16,512]{1,0:T(8,128)(2,1)} %query_ref.1), channel_id=1, source_target_pairs={{0,24},{4,28},{8,0},{12,4},{16,8},{20,12},{24,16},{28,20},{1,25},{... | collective-permute-start | bytes 49160 | tf_op jit(solution)/shard_map/ppermute | solution.py:33
  4.4 0.0 collective-permute-start
  4.4 0.0 copy-done.2
  4.5 0.0 copy-done
  4.5 0.7 %shard_map.56 = (bf16[4,256,128]{2,1,0:T(8,128)(2,1)S(1)}, bf16[4,256,128]{2,1,0:T(8,128)(2,1)S(1)}, f32[4,8,256]{2,1,0:T(8,128)S(1)}, bf16[528,128]{1,0:T(8,128)(2,1)S(1)}, bf16[528,128]{1,0:T(8,128)(2,1)S(1)}) custom-call(f32[64,768]{1,0:T(8,128)S(1)} %shard_map.55.after_ref.mask_ref, s32[6]{0:T(128)S(1)} %copy-done.2, bf16[6,2,2,128,128]{4,3,2,1,0:T(8,128)(2,1)S(1)} %copy-done), custom_call_target="tpu_custom_call" | custom-call | flops 8800000000 | bytes 29520000 | tf_op jit(solution)/shard_map/pallas_call | solution.py:321
  5.1 0.8 %collective-permute-start.3 = (bf16[528,128]{1,0:T(8,128)(2,1)S(1)}, bf16[528,128]{1,0:T(8,128)(2,1)S(1)}, u32[]{:S(2)}, u32[]{:S(2)}) collective-permute-start(bf16[528,128]{1,0:T(8,128)(2,1)S(1)} %get-tuple-element.28), channel_id=1, source_target_pairs={{0,12},{4,16},{8,20},{12,24},{16,28},{20,0},{24,4},{28,8},{1,13},{... | collective-permute-start | bytes 405512 | tf_op jit(solution)/shard_map/ppermute | solution.py:33
  5.9 1.0 %collective-permute-start.4 = (bf16[528,128]{1,0:T(8,128)(2,1)S(1)}, bf16[528,128]{1,0:T(8,128)(2,1)S(1)}, u32[]{:S(2)}, u32[]{:S(2)}) collective-permute-start(bf16[528,128]{1,0:T(8,128)(2,1)S(1)} %get-tuple-element.29), channel_id=1, source_target_pairs={{0,20},{4,24},{8,28},{12,0},{16,4},{20,8},{24,12},{28,16},{1,21},{... | collective-permute-start | bytes 405512 | tf_op jit(solution)/shard_map/ppermute | solution.py:33
  6.9 0.0 collective-permute-done.2.refs_2_
  6.9 0.0 collective-permute-done.1.refs_1_
  6.9 0.0 collective-permute-done.refs_0_
  7.0 0.4 %shard_map.57 = (bf16[80,128]{1,0:T(8,128)(2,1)S(1)}, bf16[80,128]{1,0:T(8,128)(2,1)S(1)}, bf16[80,128]{1,0:T(8,128)(2,1)S(1)}) custom-call(bf16[4,256,128]{2,1,0:T(8,128)(2,1)S(1)} %get-tuple-element.21.key_ref, bf16[4,256,128]{2,1,0:T(8,128)(2,1)S(1)} %get-tuple-element.22.value_ref, f32[4,8,256]{2,1,0:T(8,128)S(1)} %get-tuple-element.23.bias_ref, ...), custom_call_target="tpu_custom_call" | custom-call | flops 440000000 | bytes 1476000 | tf_op jit(solution)/shard_map/pallas_call | solution.py:331
  7.4 1.5 %collective-permute-start.5 = (bf16[80,128]{1,0:T(8,128)(2,1)S(1)}, bf16[80,128]{1,0:T(8,128)(2,1)S(1)}, u32[]{:S(2)}, u32[]{:S(2)}) collective-permute-start(bf16[80,128]{1,0:T(8,128)(2,1)S(1)} %get-tuple-element.33), channel_id=1, source_target_pairs={{0,4},{4,8},{8,12},{12,16},{16,20},{20,24},{24,28},{28,0},{1,5},{5... | collective-permute-start | bytes 61448 | tf_op jit(solution)/shard_map/ppermute | solution.py:33
  8.8 1.1 %collective-permute-start.6 = (bf16[80,128]{1,0:T(8,128)(2,1)S(1)}, bf16[80,128]{1,0:T(8,128)(2,1)S(1)}, u32[]{:S(2)}, u32[]{:S(2)}) collective-permute-start(bf16[80,128]{1,0:T(8,128)(2,1)S(1)} %get-tuple-element.34), channel_id=1, source_target_pairs={{0,8},{4,12},{8,16},{12,20},{16,24},{20,28},{24,0},{28,4},{1,9},{5... | collective-permute-start | bytes 61448 | tf_op jit(solution)/shard_map/ppermute | solution.py:33
  10.0 0.0 slice-start
  10.0 0.0 copy-start.1
  10.0 0.0 slice-start.1
  10.0 0.5 %collective-permute-start.7 = (bf16[80,128]{1,0:T(8,128)(2,1)S(1)}, bf16[80,128]{1,0:T(8,128)(2,1)S(1)}, u32[]{:S(2)}, u32[]{:S(2)}) collective-permute-start(bf16[80,128]{1,0:T(8,128)(2,1)S(1)} %get-tuple-element.24.after_ref), channel_id=1, source_target_pairs={{0,16},{4,20},{8,24},{12,28},{16,0},{20,4},{24,8},{28,12},{1,17},{... | collective-permute-start | bytes 61448 | tf_op jit(solution)/shard_map/ppermute | solution.py:33
  10.4 1.7 %shard_map.58 = (f32[64,128]{1,0:T(8,128)S(1)}, f32[64,128]{1,0:T(8,128)S(1)}, f32[64,128]{1,0:T(8,128)S(1)}) custom-call(bf16[4,256,128]{2,1,0:T(8,128)(2,1)S(1)} %get-tuple-element.21.key_ref, bf16[4,256,128]{2,1,0:T(8,128)(2,1)S(1)} %get-tuple-element.22.value_ref, f32[4,8,256]{2,1,0:T(8,128)S(1)} %get-tuple-element.23.bias_ref, ...), custom_call_target="tpu_custom_call" | custom-call | flops 1760000000 | bytes 5904000 | tf_op jit(solution)/shard_map/pallas_call | solution.py:340
  12.2 0.0 collective-permute-done.3.refs_0_
  12.2 0.1 collective-permute-done.4.refs_1_
  12.3 0.0 copy-done.1
  12.3 0.4 %shard_map.59 = (f32[64,128]{1,0:T(8,128)S(1)}, f32[64,128]{1,0:T(8,128)S(1)}, f32[64,128]{1,0:T(8,128)S(1)}) custom-call(f32[64,128]{1,0:T(8,128)S(1)} %get-tuple-element.25.after_ref.refs_0_, bf16[16,512]{1,0:T(8,128)(2,1)S(1)} %copy-done.1, bf16[528,128]{1,0:T(8,128)(2,1)S(1)} %collective-permute-done.3.refs_0_, ...), custom_call_target="tpu_custom_call" | custom-call | flops 550000000 | bytes 1845000 | tf_op jit(solution)/shard_map/pallas_call | solution.py:353
  12.7 0.0 collective-permute-done.5.refs_6_
  12.7 0.9 %collective-permute-done.6.refs_7_ = bf16[80,128]{1,0:T(8,128)(2,1)S(1)} collective-permute-done((bf16[80,128]{1,0:T(8,128)(2,1)S(1)}, bf16[80,128]{1,0:T(8,128)(2,1)S(1)}, u32[]{:S(2)}, u32[]{:S(2)}) %collective-permute-start.6) | collective-permute-done | bytes 20512 | tf_op jit(solution)/shard_map/ppermute | solution.py:33
  13.5 0.4 %collective-permute-done.7.refs_8_ = bf16[80,128]{1,0:T(8,128)(2,1)S(1)} collective-permute-done((bf16[80,128]{1,0:T(8,128)(2,1)S(1)}, bf16[80,128]{1,0:T(8,128)(2,1)S(1)}, u32[]{:S(2)}, u32[]{:S(2)}) %collective-permute-start.7) | collective-permute-done | bytes 20512 | tf_op jit(solution)/shard_map/ppermute | solution.py:33
  14.0 0.0 slice-done
  14.0 0.0 slice-done.1
  14.0 0.6 %shard_map.60 = (bf16[16,512]{1,0:T(8,128)(2,1)S(1)}, bf16[16,2048]{1,0:T(8,128)(2,1)S(1)}) custom-call(f32[64,128]{1,0:T(8,128)S(1)} %get-tuple-element.25.after_ref.refs_0_, f32[64,128]{1,0:T(8,128)S(1)} %get-tuple-element.26.refs_1_, f32[64,128]{1,0:T(8,128)S(1)} %get-tuple-element.27.refs_2_, f32[64,128]{1,0:T(8,128)S(1)} %get-tuple-element.30.refs_3_, ...), custom_call_target="tpu_custom_call" | custom-call | flops 220000000 | bytes 738000 | tf_op jit(solution)/shard_map/pallas_call | solution.py:366
  14.5 1.6 %collective-permute-start.8 = (bf16[16,2048]{1,0:T(8,128)(2,1)S(1)}, bf16[16,2048]{1,0:T(8,128)(2,1)S(1)}, u32[]{:S(2)}, u32[]{:S(2)}) collective-permute-start(bf16[16,2048]{1,0:T(8,128)(2,1)S(1)} %get-tuple-element.36), channel_id=1, source_target_pairs={{0,1},{1,0},{2,3},{3,2},{4,5},{5,4},{6,7},{7,6},{8,9},{9,8},{10,11... | collective-permute-start | bytes 196616 | tf_op jit(solution)/shard_map/ppermute | solution.py:38
  16.1 0.6 %shard_map.62 = bf16[16,4096]{1,0:T(8,128)(2,1)S(1)} custom-call(bf16[16,512]{1,0:T(8,128)(2,1)S(1)} %get-tuple-element.35.attended_ref, bf16[512,8192]{1,0:T(8,128)(2,1)S(1)} %bitcast.1), custom_call_target="tpu_custom_call" | custom-call | flops 67108864 | bytes 4194304 | tf_op jit(solution)/shard_map/pallas_call | solution.py:237
  16.8 0.5 %collective-permute-start.11 = (bf16[16,4096]{1,0:T(8,128)(2,1)S(1)}, bf16[16,4096]{1,0:T(8,128)(2,1)S(1)}, u32[]{:S(2)}, u32[]{:S(2)}) collective-permute-start(bf16[16,4096]{1,0:T(8,128)(2,1)S(1)} %shard_map.62), channel_id=1, source_target_pairs={{0,1},{1,0},{2,3},{3,2},{4,5},{5,4},{6,7},{7,6},{8,9},{9,8},{10,11... | collective-permute-start | bytes 393224 | tf_op jit(solution)/shard_map/ppermute | solution.py:38
  17.2 0.4 %shard_map.61 = bf16[16,2048]{1,0:T(8,128)(2,1)S(1)} custom-call(bf16[16,512]{1,0:T(8,128)(2,1)S(1)} %get-tuple-element.35.attended_ref, bf16[512,8192]{1,0:T(8,128)(2,1)S(1)} %bitcast.1), custom_call_target="tpu_custom_call" | custom-call | flops 33554432 | bytes 2097152 | tf_op jit(solution)/shard_map/pallas_call | solution.py:237
  17.6 1.2 %collective-permute-done.8 = bf16[16,2048]{1,0:T(8,128)(2,1)S(1)} collective-permute-done((bf16[16,2048]{1,0:T(8,128)(2,1)S(1)}, bf16[16,2048]{1,0:T(8,128)(2,1)S(1)}, u32[]{:S(2)}, u32[]{:S(2)}) %collective-permute-start.8) | collective-permute-done | bytes 65568 | tf_op jit(solution)/shard_map/ppermute | solution.py:38
  18.8 2.7 %collective-permute-start.9 = (bf16[16,2048]{1,0:T(8,128)(2,1)S(1)}, bf16[16,2048]{1,0:T(8,128)(2,1)S(1)}, u32[]{:S(2)}, u32[]{:S(2)}) collective-permute-start(bf16[16,2048]{1,0:T(8,128)(2,1)S(1)} %add_convert_fusion.2), channel_id=1, source_target_pairs={{0,2},{1,3},{2,0},{3,1},{4,6},{5,7},{6,4},{7,5},{8,10},{9,11},{10,... | collective-permute-start | bytes 196616 | tf_op jit(solution)/shard_map/ppermute | solution.py:38
  21.5 1.0 %collective-permute-done.11 = bf16[16,4096]{1,0:T(8,128)(2,1)S(1)} collective-permute-done((bf16[16,4096]{1,0:T(8,128)(2,1)S(1)}, bf16[16,4096]{1,0:T(8,128)(2,1)S(1)}, u32[]{:S(2)}, u32[]{:S(2)}) %collective-permute-start.11) | collective-permute-done | bytes 131104 | tf_op jit(solution)/shard_map/ppermute | solution.py:38
  22.5 2.7 %collective-permute-start.12 = (bf16[16,4096]{1,0:T(8,128)(2,1)S(1)}, bf16[16,4096]{1,0:T(8,128)(2,1)S(1)}, u32[]{:S(2)}, u32[]{:S(2)}) collective-permute-start(bf16[16,4096]{1,0:T(8,128)(2,1)S(1)} %add_convert_fusion.refs_2_), channel_id=1, source_target_pairs={{0,3},{1,2},{2,1},{3,0},{4,7},{5,6},{6,5},{7,4},{8,11},{9,10},{10,... | collective-permute-start | bytes 393224 | tf_op jit(solution)/shard_map/ppermute | solution.py:38
  25.2 0.0 collective-permute-done.9
  25.2 1.9 %collective-permute-start.10 = (bf16[16,2048]{1,0:T(8,128)(2,1)S(1)}, bf16[16,2048]{1,0:T(8,128)(2,1)S(1)}, u32[]{:S(2)}, u32[]{:S(2)}) collective-permute-start(bf16[16,2048]{1,0:T(8,128)(2,1)S(1)} %add_convert_fusion.1.refs_0_), channel_id=1, source_target_pairs={{0,1},{1,0},{2,3},{3,2},{4,5},{5,4},{6,7},{7,6},{8,9},{9,8},{10,11... | collective-permute-start | bytes 196616 | tf_op jit(solution)/shard_map/ppermute | solution.py:38
  27.2 3.0 %collective-permute-done.10.refs_1_ = bf16[16,2048]{1,0:T(8,128)(2,1)S(1)} collective-permute-done((bf16[16,2048]{1,0:T(8,128)(2,1)S(1)}, bf16[16,2048]{1,0:T(8,128)(2,1)S(1)}, u32[]{:S(2)}, u32[]{:S(2)}) %collective-permute-start.10) | collective-permute-done | bytes 65568 | tf_op jit(solution)/shard_map/ppermute | solution.py:38
  30.2 0.0 collective-permute-done.12.refs_3_
  30.2 0.7 %shard_map.63 = bf16[16,8192]{1,0:T(8,128)(2,1)} custom-call(bf16[16,2048]{1,0:T(8,128)(2,1)S(1)} %add_convert_fusion.1.refs_0_, bf16[16,2048]{1,0:T(8,128)(2,1)S(1)} %collective-permute-done.10.refs_1_, bf16[16,4096]{1,0:T(8,128)(2,1)S(1)} %add_convert_fusion.refs_2_, bf16[16,4096]{1,0:T(8,128)(2,1)S(1)} %collective-permute-done.12.refs_3_), custom_call_target="tpu_custom_call" | custom-call | tf_op jit(solution)/shard_map/pallas_call | solution.py:290
  (5 shorter events, 0.1 us)
Async XLA Ops:
  0.0 4.5 %copy-start.2 = (s32[6]{0:T(128)S(1)}, s32[6]{0:T(128)}, u32[]{:S(2)}) copy-start(s32[6]{0:T(128)} %offset_ref.1) | copy-start | bytes 76
  0.0 4.5 %copy-start = (bf16[6,2,2,128,128]{4,3,2,1,0:T(8,128)(2,1)S(1)}, bf16[6,2,2,128,128]{4,3,2,1,0:T(8,128)(2,1)}, u32[]{:S(2)}) copy-start(bf16[6,2,2,128,128]{4,3,2,1,0:T(8,128)(2,1)} %pool_ref.1) | copy-start | bytes 2359300
  0.0 6.9 %collective-permute-start.2 = (bf16[16,512]{1,0:T(8,128)(2,1)}, bf16[16,512]{1,0:T(8,128)(2,1)S(1)}, u32[]{:S(2)}, u32[]{:S(2)}) collective-permute-start(bf16[16,512]{1,0:T(8,128)(2,1)} %query_ref.1), channel_id=1, source_target_pairs={{0,16},{4,20},{8,24},{12,28},{16,0},{20,4},{24,8},{28,12},{1,17},{... | collective-permute-start | bytes 49160 | tf_op jit(solution)/shard_map/ppermute | solution.py:33
  3.0 4.0 %collective-permute-start.1 = (bf16[16,512]{1,0:T(8,128)(2,1)}, bf16[16,512]{1,0:T(8,128)(2,1)S(1)}, u32[]{:S(2)}, u32[]{:S(2)}) collective-permute-start(bf16[16,512]{1,0:T(8,128)(2,1)} %query_ref.1), channel_id=1, source_target_pairs={{0,24},{4,28},{8,0},{12,4},{16,8},{20,12},{24,16},{28,20},{1,25},{... | collective-permute-start | bytes 49160 | tf_op jit(solution)/shard_map/ppermute | solution.py:33
  4.4 2.5 %collective-permute-start = (bf16[16,512]{1,0:T(8,128)(2,1)}, bf16[16,512]{1,0:T(8,128)(2,1)S(1)}, u32[]{:S(2)}, u32[]{:S(2)}) collective-permute-start(bf16[16,512]{1,0:T(8,128)(2,1)} %query_ref.1), channel_id=1, source_target_pairs={{0,28},{4,0},{8,4},{12,8},{16,12},{20,16},{24,20},{28,24},{1,29},{... | collective-permute-start | bytes 49160 | tf_op jit(solution)/shard_map/ppermute | solution.py:33
  5.1 7.0 %collective-permute-start.3 = (bf16[528,128]{1,0:T(8,128)(2,1)S(1)}, bf16[528,128]{1,0:T(8,128)(2,1)S(1)}, u32[]{:S(2)}, u32[]{:S(2)}) collective-permute-start(bf16[528,128]{1,0:T(8,128)(2,1)S(1)} %get-tuple-element.28), channel_id=1, source_target_pairs={{0,12},{4,16},{8,20},{12,24},{16,28},{20,0},{24,4},{28,8},{1,13},{... | collective-permute-start | bytes 405512 | tf_op jit(solution)/shard_map/ppermute | solution.py:33
  5.9 6.4 %collective-permute-start.4 = (bf16[528,128]{1,0:T(8,128)(2,1)S(1)}, bf16[528,128]{1,0:T(8,128)(2,1)S(1)}, u32[]{:S(2)}, u32[]{:S(2)}) collective-permute-start(bf16[528,128]{1,0:T(8,128)(2,1)S(1)} %get-tuple-element.29), channel_id=1, source_target_pairs={{0,20},{4,24},{8,28},{12,0},{16,4},{20,8},{24,12},{28,16},{1,21},{... | collective-permute-start | bytes 405512 | tf_op jit(solution)/shard_map/ppermute | solution.py:33
  7.4 5.3 %collective-permute-start.5 = (bf16[80,128]{1,0:T(8,128)(2,1)S(1)}, bf16[80,128]{1,0:T(8,128)(2,1)S(1)}, u32[]{:S(2)}, u32[]{:S(2)}) collective-permute-start(bf16[80,128]{1,0:T(8,128)(2,1)S(1)} %get-tuple-element.33), channel_id=1, source_target_pairs={{0,4},{4,8},{8,12},{12,16},{16,20},{20,24},{24,28},{28,0},{1,5},{5... | collective-permute-start | bytes 61448 | tf_op jit(solution)/shard_map/ppermute | solution.py:33
  8.8 4.7 %collective-permute-start.6 = (bf16[80,128]{1,0:T(8,128)(2,1)S(1)}, bf16[80,128]{1,0:T(8,128)(2,1)S(1)}, u32[]{:S(2)}, u32[]{:S(2)}) collective-permute-start(bf16[80,128]{1,0:T(8,128)(2,1)S(1)} %get-tuple-element.34), channel_id=1, source_target_pairs={{0,8},{4,12},{8,16},{12,20},{16,24},{20,28},{24,0},{28,4},{1,9},{5... | collective-permute-start | bytes 61448 | tf_op jit(solution)/shard_map/ppermute | solution.py:33
  10.0 4.0 %slice-start = ((s8[8388608]{0:T(1024)(128)(4,1)}), s8[4194304]{0:T(1024)(128)(4,1)S(1)}, s32[]{:S(2)}) async-start(s8[8388608]{0:T(1024)(128)(4,1)} %bitcast), calls=%async_computation | async-start | bytes 8388608
  10.0 2.3 %copy-start.1 = (bf16[16,512]{1,0:T(8,128)(2,1)S(1)}, bf16[16,512]{1,0:T(8,128)(2,1)}, u32[]{:S(2)}) copy-start(bf16[16,512]{1,0:T(8,128)(2,1)} %query_ref.1) | copy-start | bytes 49156
  10.0 4.0 %slice-start.1 = ((s8[8388608]{0:T(1024)(128)(4,1)}), s8[4194304]{0:T(1024)(128)(4,1)S(1)}, s32[]{:S(2)}) async-start(s8[8388608]{0:T(1024)(128)(4,1)} %bitcast), calls=%async_computation.1 | async-start | bytes 8388608
  10.0 4.0 %collective-permute-start.7 = (bf16[80,128]{1,0:T(8,128)(2,1)S(1)}, bf16[80,128]{1,0:T(8,128)(2,1)S(1)}, u32[]{:S(2)}, u32[]{:S(2)}) collective-permute-start(bf16[80,128]{1,0:T(8,128)(2,1)S(1)} %get-tuple-element.24.after_ref), channel_id=1, source_target_pairs={{0,16},{4,20},{8,24},{12,28},{16,0},{20,4},{24,8},{28,12},{1,17},{... | collective-permute-start | bytes 61448 | tf_op jit(solution)/shard_map/ppermute | solution.py:33
  14.5 4.3 %collective-permute-start.8 = (bf16[16,2048]{1,0:T(8,128)(2,1)S(1)}, bf16[16,2048]{1,0:T(8,128)(2,1)S(1)}, u32[]{:S(2)}, u32[]{:S(2)}) collective-permute-start(bf16[16,2048]{1,0:T(8,128)(2,1)S(1)} %get-tuple-element.36), channel_id=1, source_target_pairs={{0,1},{1,0},{2,3},{3,2},{4,5},{5,4},{6,7},{7,6},{8,9},{9,8},{10,11... | collective-permute-start | bytes 196616 | tf_op jit(solution)/shard_map/ppermute | solution.py:38
  16.8 5.7 %collective-permute-start.11 = (bf16[16,4096]{1,0:T(8,128)(2,1)S(1)}, bf16[16,4096]{1,0:T(8,128)(2,1)S(1)}, u32[]{:S(2)}, u32[]{:S(2)}) collective-permute-start(bf16[16,4096]{1,0:T(8,128)(2,1)S(1)} %shard_map.62), channel_id=1, source_target_pairs={{0,1},{1,0},{2,3},{3,2},{4,5},{5,4},{6,7},{7,6},{8,9},{9,8},{10,11... | collective-permute-start | bytes 393224 | tf_op jit(solution)/shard_map/ppermute | solution.py:38
  18.8 6.4 %collective-permute-start.9 = (bf16[16,2048]{1,0:T(8,128)(2,1)S(1)}, bf16[16,2048]{1,0:T(8,128)(2,1)S(1)}, u32[]{:S(2)}, u32[]{:S(2)}) collective-permute-start(bf16[16,2048]{1,0:T(8,128)(2,1)S(1)} %add_convert_fusion.2), channel_id=1, source_target_pairs={{0,2},{1,3},{2,0},{3,1},{4,6},{5,7},{6,4},{7,5},{8,10},{9,11},{10,... | collective-permute-start | bytes 196616 | tf_op jit(solution)/shard_map/ppermute | solution.py:38
  22.5 7.6 %collective-permute-start.12 = (bf16[16,4096]{1,0:T(8,128)(2,1)S(1)}, bf16[16,4096]{1,0:T(8,128)(2,1)S(1)}, u32[]{:S(2)}, u32[]{:S(2)}) collective-permute-start(bf16[16,4096]{1,0:T(8,128)(2,1)S(1)} %add_convert_fusion.refs_2_), channel_id=1, source_target_pairs={{0,3},{1,2},{2,1},{3,0},{4,7},{5,6},{6,5},{7,4},{8,11},{9,10},{10,... | collective-permute-start | bytes 393224 | tf_op jit(solution)/shard_map/ppermute | solution.py:38
  25.2 4.9 %collective-permute-start.10 = (bf16[16,2048]{1,0:T(8,128)(2,1)S(1)}, bf16[16,2048]{1,0:T(8,128)(2,1)S(1)}, u32[]{:S(2)}, u32[]{:S(2)}) collective-permute-start(bf16[16,2048]{1,0:T(8,128)(2,1)S(1)} %add_convert_fusion.1.refs_0_), channel_id=1, source_target_pairs={{0,1},{1,0},{2,3},{3,2},{4,5},{5,4},{6,7},{7,6},{8,9},{9,8},{10,11... | collective-permute-start | bytes 196616 | tf_op jit(solution)/shard_map/ppermute | solution.py:38

commit v9 on v8

--- a/solution.py
+++ b/solution.py
@@ -203,8 +203,9 @@
     for ref in part_refs:
         part = ref[...].astype(jnp.float32)
         accs.append(part[:rows])
-        peaks.append(along_rows(part[rows : rows + 1], rows))
-        totals.append(along_rows(part[rows + 1 : rows + 2], rows))
+        stats = jnp.transpose(part[rows:])
+        peaks.append(stats[:rows, 0:1])
+        totals.append(stats[:rows, 1:2])
     top = functools.reduce(jnp.maximum, peaks)
     shares = [jnp.exp(peak - top) for peak in peaks]
     total = sum(share * t for share, t in zip(shares, totals))

time: 31.1 us -> 31.1 us (level)
  no operation moved by 1% of the time
where the time goes in v9:
time: 31.1 us; the launch traced here: 30.9 us
  starting transfers between devices  18.6 us (60%)
  waiting for transfers between devices  6.58 us (21%)
  Pallas kernels  5.59 us (18%)
    ppermute x5, starting transfers between devices, swapped(): return lax.ppermute(block, 'mp', [(i, i ^ step) for i in range(size)])  9.32 us
    ppermute x8, starting transfers between devices, shifted(): lax.ppermute(block, 'dp', [(i, (i + distance) % size) for i in range(size)])  9.26 us
    ppermute x5, waiting for transfers between devices, swapped(): return lax.ppermute(block, 'mp', [(i, i ^ step) for i in range(size)])  5.21 us
    pallas_call x1, Pallas kernels, local(): pl.pallas_call(functools.partial(own_kernel, local_heads), out_shape=part...  1.74 us
    ppermute x8, waiting for transfers between devices, shifted(): lax.ppermute(block, 'dp', [(i, (i + distance) % size) for i in range(size)])  1.37 us
    pallas_call x2, Pallas kernels, project(): pl.pallas_call(functools.partial(project_kernel, half, far, start), out_s...  1.02 us
    pallas_call x1, Pallas kernels, summed_over_four(): pl.pallas_call(functools.partial(final_kernel, layout), out_shape=jax.Sha...  0.75 us
    pallas_call x1, Pallas kernels, local(): pl.pallas_call(functools.partial(gather_kernel, local_heads), out_shape=(...  0.67 us
  transfers between devices with their start and end apart: 13, of which 6 were waited for; matrix products, arithmetic and copies ran while one was open for 0% of the time, Pallas kernels for 14%

profile of v9, /device:TPU:0, one launch (start us, length us, event | category | flops | bytes accessed | tf_op | source)
XLA Modules:
  0.0 30.9 jit_solution(684870753934360484)
XLA Ops:
  0.0 0.0 copy-start.2
  0.0 0.0 copy-start
  0.0 3.0 %collective-permute-start.2 = (bf16[16,512]{1,0:T(8,128)(2,1)}, bf16[16,512]{1,0:T(8,128)(2,1)S(1)}, u32[]{:S(2)}, u32[]{:S(2)}) collective-permute-start(bf16[16,512]{1,0:T(8,128)(2,1)} %query_ref.1), channel_id=1, source_target_pairs={{0,16},{4,20},{8,24},{12,28},{16,0},{20,4},{24,8},{28,12},{1,17},{... | collective-permute-start | bytes 49160 | tf_op jit(solution)/shard_map/ppermute | solution.py:33
  3.0 1.4 %collective-permute-start.1 = (bf16[16,512]{1,0:T(8,128)(2,1)}, bf16[16,512]{1,0:T(8,128)(2,1)S(1)}, u32[]{:S(2)}, u32[]{:S(2)}) collective-permute-start(bf16[16,512]{1,0:T(8,128)(2,1)} %query_ref.1), channel_id=1, source_target_pairs={{0,24},{4,28},{8,0},{12,4},{16,8},{20,12},{24,16},{28,20},{1,25},{... | collective-permute-start | bytes 49160 | tf_op jit(solution)/shard_map/ppermute | solution.py:33
  4.4 0.0 collective-permute-start
  4.4 0.0 copy-done.2
  4.5 0.0 copy-done
  4.5 0.7 %shard_map.56 = (bf16[4,256,128]{2,1,0:T(8,128)(2,1)S(1)}, bf16[4,256,128]{2,1,0:T(8,128)(2,1)S(1)}, f32[4,8,256]{2,1,0:T(8,128)S(1)}, bf16[528,128]{1,0:T(8,128)(2,1)S(1)}, bf16[528,128]{1,0:T(8,128)(2,1)S(1)}) custom-call(f32[64,768]{1,0:T(8,128)S(1)} %shard_map.55.after_ref.mask_ref, s32[6]{0:T(128)S(1)} %copy-done.2, bf16[6,2,2,128,128]{4,3,2,1,0:T(8,128)(2,1)S(1)} %copy-done), custom_call_target="tpu_custom_call" | custom-call | flops 8800000000 | bytes 29520000 | tf_op jit(solution)/shard_map/pallas_call | solution.py:322
  5.1 0.8 %collective-permute-start.3 = (bf16[528,128]{1,0:T(8,128)(2,1)S(1)}, bf16[528,128]{1,0:T(8,128)(2,1)S(1)}, u32[]{:S(2)}, u32[]{:S(2)}) collective-permute-start(bf16[528,128]{1,0:T(8,128)(2,1)S(1)} %get-tuple-element.28), channel_id=1, source_target_pairs={{0,12},{4,16},{8,20},{12,24},{16,28},{20,0},{24,4},{28,8},{1,13},{... | collective-permute-start | bytes 405512 | tf_op jit(solution)/shard_map/ppermute | solution.py:33
  5.9 1.0 %collective-permute-start.4 = (bf16[528,128]{1,0:T(8,128)(2,1)S(1)}, bf16[528,128]{1,0:T(8,128)(2,1)S(1)}, u32[]{:S(2)}, u32[]{:S(2)}) collective-permute-start(bf16[528,128]{1,0:T(8,128)(2,1)S(1)} %get-tuple-element.29), channel_id=1, source_target_pairs={{0,20},{4,24},{8,28},{12,0},{16,4},{20,8},{24,12},{28,16},{1,21},{... | collective-permute-start | bytes 405512 | tf_op jit(solution)/shard_map/ppermute | solution.py:33
  6.9 0.0 collective-permute-done.2.refs_2_
  6.9 0.0 collective-permute-done.1.refs_1_
  6.9 0.0 collective-permute-done.refs_0_
  7.0 0.4 %shard_map.57 = (bf16[80,128]{1,0:T(8,128)(2,1)S(1)}, bf16[80,128]{1,0:T(8,128)(2,1)S(1)}, bf16[80,128]{1,0:T(8,128)(2,1)S(1)}) custom-call(bf16[4,256,128]{2,1,0:T(8,128)(2,1)S(1)} %get-tuple-element.21.key_ref, bf16[4,256,128]{2,1,0:T(8,128)(2,1)S(1)} %get-tuple-element.22.value_ref, f32[4,8,256]{2,1,0:T(8,128)S(1)} %get-tuple-element.23.bias_ref, ...), custom_call_target="tpu_custom_call" | custom-call | flops 440000000 | bytes 1476000 | tf_op jit(solution)/shard_map/pallas_call | solution.py:332
  7.4 1.5 %collective-permute-start.5 = (bf16[80,128]{1,0:T(8,128)(2,1)S(1)}, bf16[80,128]{1,0:T(8,128)(2,1)S(1)}, u32[]{:S(2)}, u32[]{:S(2)}) collective-permute-start(bf16[80,128]{1,0:T(8,128)(2,1)S(1)} %get-tuple-element.33), channel_id=1, source_target_pairs={{0,4},{4,8},{8,12},{12,16},{16,20},{20,24},{24,28},{28,0},{1,5},{5... | collective-permute-start | bytes 61448 | tf_op jit(solution)/shard_map/ppermute | solution.py:33
  8.8 1.1 %collective-permute-start.6 = (bf16[80,128]{1,0:T(8,128)(2,1)S(1)}, bf16[80,128]{1,0:T(8,128)(2,1)S(1)}, u32[]{:S(2)}, u32[]{:S(2)}) collective-permute-start(bf16[80,128]{1,0:T(8,128)(2,1)S(1)} %get-tuple-element.34), channel_id=1, source_target_pairs={{0,8},{4,12},{8,16},{12,20},{16,24},{20,28},{24,0},{28,4},{1,9},{5... | collective-permute-start | bytes 61448 | tf_op jit(solution)/shard_map/ppermute | solution.py:33
  10.0 0.0 slice-start
  10.0 0.0 copy-start.1
  10.0 0.0 slice-start.1
  10.0 0.5 %collective-permute-start.7 = (bf16[80,128]{1,0:T(8,128)(2,1)S(1)}, bf16[80,128]{1,0:T(8,128)(2,1)S(1)}, u32[]{:S(2)}, u32[]{:S(2)}) collective-permute-start(bf16[80,128]{1,0:T(8,128)(2,1)S(1)} %get-tuple-element.24.after_ref), channel_id=1, source_target_pairs={{0,16},{4,20},{8,24},{12,28},{16,0},{20,4},{24,8},{28,12},{1,17},{... | collective-permute-start | bytes 61448 | tf_op jit(solution)/shard_map/ppermute | solution.py:33
  10.4 1.7 %shard_map.58 = (f32[64,128]{1,0:T(8,128)S(1)}, f32[64,128]{1,0:T(8,128)S(1)}, f32[64,128]{1,0:T(8,128)S(1)}) custom-call(bf16[4,256,128]{2,1,0:T(8,128)(2,1)S(1)} %get-tuple-element.21.key_ref, bf16[4,256,128]{2,1,0:T(8,128)(2,1)S(1)} %get-tuple-element.22.value_ref, f32[4,8,256]{2,1,0:T(8,128)S(1)} %get-tuple-element.23.bias_ref, ...), custom_call_target="tpu_custom_call" | custom-call | flops 1760000000 | bytes 5904000 | tf_op jit(solution)/shard_map/pallas_call | solution.py:341
  12.2 0.0 collective-permute-done.3.refs_0_
  12.2 0.1 collective-permute-done.4.refs_1_
  12.3 0.0 copy-done.1
  12.3 0.4 %shard_map.59 = (f32[64,128]{1,0:T(8,128)S(1)}, f32[64,128]{1,0:T(8,128)S(1)}, f32[64,128]{1,0:T(8,128)S(1)}) custom-call(f32[64,128]{1,0:T(8,128)S(1)} %get-tuple-element.25.after_ref.refs_0_, bf16[16,512]{1,0:T(8,128)(2,1)S(1)} %copy-done.1, bf16[528,128]{1,0:T(8,128)(2,1)S(1)} %collective-permute-done.3.refs_0_, ...), custom_call_target="tpu_custom_call" | custom-call | flops 550000000 | bytes 1845000 | tf_op jit(solution)/shard_map/pallas_call | solution.py:354
  12.7 0.0 collective-permute-done.5.refs_6_
  12.7 0.9 %collective-permute-done.6.refs_7_ = bf16[80,128]{1,0:T(8,128)(2,1)S(1)} collective-permute-done((bf16[80,128]{1,0:T(8,128)(2,1)S(1)}, bf16[80,128]{1,0:T(8,128)(2,1)S(1)}, u32[]{:S(2)}, u32[]{:S(2)}) %collective-permute-start.6) | collective-permute-done | bytes 20512 | tf_op jit(solution)/shard_map/ppermute | solution.py:33
  13.5 0.4 %collective-permute-done.7.refs_8_ = bf16[80,128]{1,0:T(8,128)(2,1)S(1)} collective-permute-done((bf16[80,128]{1,0:T(8,128)(2,1)S(1)}, bf16[80,128]{1,0:T(8,128)(2,1)S(1)}, u32[]{:S(2)}, u32[]{:S(2)}) %collective-permute-start.7) | collective-permute-done | bytes 20512 | tf_op jit(solution)/shard_map/ppermute | solution.py:33
  14.0 0.0 slice-done
  14.0 0.0 slice-done.1
  14.0 0.6 %shard_map.60 = (bf16[16,512]{1,0:T(8,128)(2,1)S(1)}, bf16[16,2048]{1,0:T(8,128)(2,1)S(1)}) custom-call(f32[64,128]{1,0:T(8,128)S(1)} %get-tuple-element.25.after_ref.refs_0_, f32[64,128]{1,0:T(8,128)S(1)} %get-tuple-element.26.refs_1_, f32[64,128]{1,0:T(8,128)S(1)} %get-tuple-element.27.refs_2_, f32[64,128]{1,0:T(8,128)S(1)} %get-tuple-element.30.refs_3_, ...), custom_call_target="tpu_custom_call" | custom-call | flops 220000000 | bytes 738000 | tf_op jit(solution)/shard_map/pallas_call | solution.py:367
  14.5 1.6 %collective-permute-start.8 = (bf16[16,2048]{1,0:T(8,128)(2,1)S(1)}, bf16[16,2048]{1,0:T(8,128)(2,1)S(1)}, u32[]{:S(2)}, u32[]{:S(2)}) collective-permute-start(bf16[16,2048]{1,0:T(8,128)(2,1)S(1)} %get-tuple-element.36), channel_id=1, source_target_pairs={{0,1},{1,0},{2,3},{3,2},{4,5},{5,4},{6,7},{7,6},{8,9},{9,8},{10,11... | collective-permute-start | bytes 196616 | tf_op jit(solution)/shard_map/ppermute | solution.py:38
  16.1 0.6 %shard_map.62 = bf16[16,4096]{1,0:T(8,128)(2,1)S(1)} custom-call(bf16[16,512]{1,0:T(8,128)(2,1)S(1)} %get-tuple-element.35.attended_ref, bf16[512,8192]{1,0:T(8,128)(2,1)S(1)} %bitcast.1), custom_call_target="tpu_custom_call" | custom-call | flops 67108864 | bytes 4194304 | tf_op jit(solution)/shard_map/pallas_call | solution.py:238
  16.8 0.5 %collective-permute-start.11 = (bf16[16,4096]{1,0:T(8,128)(2,1)S(1)}, bf16[16,4096]{1,0:T(8,128)(2,1)S(1)}, u32[]{:S(2)}, u32[]{:S(2)}) collective-permute-start(bf16[16,4096]{1,0:T(8,128)(2,1)S(1)} %shard_map.62), channel_id=1, source_target_pairs={{0,1},{1,0},{2,3},{3,2},{4,5},{5,4},{6,7},{7,6},{8,9},{9,8},{10,11... | collective-permute-start | bytes 393224 | tf_op jit(solution)/shard_map/ppermute | solution.py:38
  17.2 0.4 %shard_map.61 = bf16[16,2048]{1,0:T(8,128)(2,1)S(1)} custom-call(bf16[16,512]{1,0:T(8,128)(2,1)S(1)} %get-tuple-element.35.attended_ref, bf16[512,8192]{1,0:T(8,128)(2,1)S(1)} %bitcast.1), custom_call_target="tpu_custom_call" | custom-call | flops 33554432 | bytes 2097152 | tf_op jit(solution)/shard_map/pallas_call | solution.py:238
  17.6 1.2 %collective-permute-done.8 = bf16[16,2048]{1,0:T(8,128)(2,1)S(1)} collective-permute-done((bf16[16,2048]{1,0:T(8,128)(2,1)S(1)}, bf16[16,2048]{1,0:T(8,128)(2,1)S(1)}, u32[]{:S(2)}, u32[]{:S(2)}) %collective-permute-start.8) | collective-permute-done | bytes 65568 | tf_op jit(solution)/shard_map/ppermute | solution.py:38
  18.8 2.7 %collective-permute-start.9 = (bf16[16,2048]{1,0:T(8,128)(2,1)S(1)}, bf16[16,2048]{1,0:T(8,128)(2,1)S(1)}, u32[]{:S(2)}, u32[]{:S(2)}) collective-permute-start(bf16[16,2048]{1,0:T(8,128)(2,1)S(1)} %add_convert_fusion.2), channel_id=1, source_target_pairs={{0,2},{1,3},{2,0},{3,1},{4,6},{5,7},{6,4},{7,5},{8,10},{9,11},{10,... | collective-permute-start | bytes 196616 | tf_op jit(solution)/shard_map/ppermute | solution.py:38
  21.5 1.0 %collective-permute-done.11 = bf16[16,4096]{1,0:T(8,128)(2,1)S(1)} collective-permute-done((bf16[16,4096]{1,0:T(8,128)(2,1)S(1)}, bf16[16,4096]{1,0:T(8,128)(2,1)S(1)}, u32[]{:S(2)}, u32[]{:S(2)}) %collective-permute-start.11) | collective-permute-done | bytes 131104 | tf_op jit(solution)/shard_map/ppermute | solution.py:38
  22.6 2.7 %collective-permute-start.12 = (bf16[16,4096]{1,0:T(8,128)(2,1)S(1)}, bf16[16,4096]{1,0:T(8,128)(2,1)S(1)}, u32[]{:S(2)}, u32[]{:S(2)}) collective-permute-start(bf16[16,4096]{1,0:T(8,128)(2,1)S(1)} %add_convert_fusion.refs_2_), channel_id=1, source_target_pairs={{0,3},{1,2},{2,1},{3,0},{4,7},{5,6},{6,5},{7,4},{8,11},{9,10},{10,... | collective-permute-start | bytes 393224 | tf_op jit(solution)/shard_map/ppermute | solution.py:38
  25.2 0.0 collective-permute-done.9
  25.3 1.9 %collective-permute-start.10 = (bf16[16,2048]{1,0:T(8,128)(2,1)S(1)}, bf16[16,2048]{1,0:T(8,128)(2,1)S(1)}, u32[]{:S(2)}, u32[]{:S(2)}) collective-permute-start(bf16[16,2048]{1,0:T(8,128)(2,1)S(1)} %add_convert_fusion.1.refs_0_), channel_id=1, source_target_pairs={{0,1},{1,0},{2,3},{3,2},{4,5},{5,4},{6,7},{7,6},{8,9},{9,8},{10,11... | collective-permute-start | bytes 196616 | tf_op jit(solution)/shard_map/ppermute | solution.py:38
  27.2 3.0 %collective-permute-done.10.refs_1_ = bf16[16,2048]{1,0:T(8,128)(2,1)S(1)} collective-permute-done((bf16[16,2048]{1,0:T(8,128)(2,1)S(1)}, bf16[16,2048]{1,0:T(8,128)(2,1)S(1)}, u32[]{:S(2)}, u32[]{:S(2)}) %collective-permute-start.10) | collective-permute-done | bytes 65568 | tf_op jit(solution)/shard_map/ppermute | solution.py:38
  30.2 0.0 collective-permute-done.12.refs_3_
  30.2 0.7 %shard_map.63 = bf16[16,8192]{1,0:T(8,128)(2,1)} custom-call(bf16[16,2048]{1,0:T(8,128)(2,1)S(1)} %add_convert_fusion.1.refs_0_, bf16[16,2048]{1,0:T(8,128)(2,1)S(1)} %collective-permute-done.10.refs_1_, bf16[16,4096]{1,0:T(8,128)(2,1)S(1)} %add_convert_fusion.refs_2_, bf16[16,4096]{1,0:T(8,128)(2,1)S(1)} %collective-permute-done.12.refs_3_), custom_call_target="tpu_custom_call" | custom-call | tf_op jit(solution)/shard_map/pallas_call | solution.py:291
  (5 shorter events, 0.1 us)
Async XLA Ops:
  0.0 4.5 %copy-start.2 = (s32[6]{0:T(128)S(1)}, s32[6]{0:T(128)}, u32[]{:S(2)}) copy-start(s32[6]{0:T(128)} %offset_ref.1) | copy-start | bytes 76
  0.0 4.5 %copy-start = (bf16[6,2,2,128,128]{4,3,2,1,0:T(8,128)(2,1)S(1)}, bf16[6,2,2,128,128]{4,3,2,1,0:T(8,128)(2,1)}, u32[]{:S(2)}) copy-start(bf16[6,2,2,128,128]{4,3,2,1,0:T(8,128)(2,1)} %pool_ref.1) | copy-start | bytes 2359300
  0.0 6.9 %collective-permute-start.2 = (bf16[16,512]{1,0:T(8,128)(2,1)}, bf16[16,512]{1,0:T(8,128)(2,1)S(1)}, u32[]{:S(2)}, u32[]{:S(2)}) collective-permute-start(bf16[16,512]{1,0:T(8,128)(2,1)} %query_ref.1), channel_id=1, source_target_pairs={{0,16},{4,20},{8,24},{12,28},{16,0},{20,4},{24,8},{28,12},{1,17},{... | collective-permute-start | bytes 49160 | tf_op jit(solution)/shard_map/ppermute | solution.py:33
  3.0 4.0 %collective-permute-start.1 = (bf16[16,512]{1,0:T(8,128)(2,1)}, bf16[16,512]{1,0:T(8,128)(2,1)S(1)}, u32[]{:S(2)}, u32[]{:S(2)}) collective-permute-start(bf16[16,512]{1,0:T(8,128)(2,1)} %query_ref.1), channel_id=1, source_target_pairs={{0,24},{4,28},{8,0},{12,4},{16,8},{20,12},{24,16},{28,20},{1,25},{... | collective-permute-start | bytes 49160 | tf_op jit(solution)/shard_map/ppermute | solution.py:33
  4.4 2.5 %collective-permute-start = (bf16[16,512]{1,0:T(8,128)(2,1)}, bf16[16,512]{1,0:T(8,128)(2,1)S(1)}, u32[]{:S(2)}, u32[]{:S(2)}) collective-permute-start(bf16[16,512]{1,0:T(8,128)(2,1)} %query_ref.1), channel_id=1, source_target_pairs={{0,28},{4,0},{8,4},{12,8},{16,12},{20,16},{24,20},{28,24},{1,29},{... | collective-permute-start | bytes 49160 | tf_op jit(solution)/shard_map/ppermute | solution.py:33
  5.1 7.0 %collective-permute-start.3 = (bf16[528,128]{1,0:T(8,128)(2,1)S(1)}, bf16[528,128]{1,0:T(8,128)(2,1)S(1)}, u32[]{:S(2)}, u32[]{:S(2)}) collective-permute-start(bf16[528,128]{1,0:T(8,128)(2,1)S(1)} %get-tuple-element.28), channel_id=1, source_target_pairs={{0,12},{4,16},{8,20},{12,24},{16,28},{20,0},{24,4},{28,8},{1,13},{... | collective-permute-start | bytes 405512 | tf_op jit(solution)/shard_map/ppermute | solution.py:33
  5.9 6.4 %collective-permute-start.4 = (bf16[528,128]{1,0:T(8,128)(2,1)S(1)}, bf16[528,128]{1,0:T(8,128)(2,1)S(1)}, u32[]{:S(2)}, u32[]{:S(2)}) collective-permute-start(bf16[528,128]{1,0:T(8,128)(2,1)S(1)} %get-tuple-element.29), channel_id=1, source_target_pairs={{0,20},{4,24},{8,28},{12,0},{16,4},{20,8},{24,12},{28,16},{1,21},{... | collective-permute-start | bytes 405512 | tf_op jit(solution)/shard_map/ppermute | solution.py:33
  7.4 5.3 %collective-permute-start.5 = (bf16[80,128]{1,0:T(8,128)(2,1)S(1)}, bf16[80,128]{1,0:T(8,128)(2,1)S(1)}, u32[]{:S(2)}, u32[]{:S(2)}) collective-permute-start(bf16[80,128]{1,0:T(8,128)(2,1)S(1)} %get-tuple-element.33), channel_id=1, source_target_pairs={{0,4},{4,8},{8,12},{12,16},{16,20},{20,24},{24,28},{28,0},{1,5},{5... | collective-permute-start | bytes 61448 | tf_op jit(solution)/shard_map/ppermute | solution.py:33
  8.8 4.7 %collective-permute-start.6 = (bf16[80,128]{1,0:T(8,128)(2,1)S(1)}, bf16[80,128]{1,0:T(8,128)(2,1)S(1)}, u32[]{:S(2)}, u32[]{:S(2)}) collective-permute-start(bf16[80,128]{1,0:T(8,128)(2,1)S(1)} %get-tuple-element.34), channel_id=1, source_target_pairs={{0,8},{4,12},{8,16},{12,20},{16,24},{20,28},{24,0},{28,4},{1,9},{5... | collective-permute-start | bytes 61448 | tf_op jit(solution)/shard_map/ppermute | solution.py:33
  10.0 4.0 %slice-start = ((s8[8388608]{0:T(1024)(128)(4,1)}), s8[4194304]{0:T(1024)(128)(4,1)S(1)}, s32[]{:S(2)}) async-start(s8[8388608]{0:T(1024)(128)(4,1)} %bitcast), calls=%async_computation | async-start | bytes 8388608
  10.0 2.3 %copy-start.1 = (bf16[16,512]{1,0:T(8,128)(2,1)S(1)}, bf16[16,512]{1,0:T(8,128)(2,1)}, u32[]{:S(2)}) copy-start(bf16[16,512]{1,0:T(8,128)(2,1)} %query_ref.1) | copy-start | bytes 49156
  10.0 4.0 %slice-start.1 = ((s8[8388608]{0:T(1024)(128)(4,1)}), s8[4194304]{0:T(1024)(128)(4,1)S(1)}, s32[]{:S(2)}) async-start(s8[8388608]{0:T(1024)(128)(4,1)} %bitcast), calls=%async_computation.1 | async-start | bytes 8388608
  10.0 4.0 %collective-permute-start.7 = (bf16[80,128]{1,0:T(8,128)(2,1)S(1)}, bf16[80,128]{1,0:T(8,128)(2,1)S(1)}, u32[]{:S(2)}, u32[]{:S(2)}) collective-permute-start(bf16[80,128]{1,0:T(8,128)(2,1)S(1)} %get-tuple-element.24.after_ref), channel_id=1, source_target_pairs={{0,16},{4,20},{8,24},{12,28},{16,0},{20,4},{24,8},{28,12},{1,17},{... | collective-permute-start | bytes 61448 | tf_op jit(solution)/shard_map/ppermute | solution.py:33
  14.5 4.3 %collective-permute-start.8 = (bf16[16,2048]{1,0:T(8,128)(2,1)S(1)}, bf16[16,2048]{1,0:T(8,128)(2,1)S(1)}, u32[]{:S(2)}, u32[]{:S(2)}) collective-permute-start(bf16[16,2048]{1,0:T(8,128)(2,1)S(1)} %get-tuple-element.36), channel_id=1, source_target_pairs={{0,1},{1,0},{2,3},{3,2},{4,5},{5,4},{6,7},{7,6},{8,9},{9,8},{10,11... | collective-permute-start | bytes 196616 | tf_op jit(solution)/shard_map/ppermute | solution.py:38
  16.8 5.7 %collective-permute-start.11 = (bf16[16,4096]{1,0:T(8,128)(2,1)S(1)}, bf16[16,4096]{1,0:T(8,128)(2,1)S(1)}, u32[]{:S(2)}, u32[]{:S(2)}) collective-permute-start(bf16[16,4096]{1,0:T(8,128)(2,1)S(1)} %shard_map.62), channel_id=1, source_target_pairs={{0,1},{1,0},{2,3},{3,2},{4,5},{5,4},{6,7},{7,6},{8,9},{9,8},{10,11... | collective-permute-start | bytes 393224 | tf_op jit(solution)/shard_map/ppermute | solution.py:38
  18.8 6.4 %collective-permute-start.9 = (bf16[16,2048]{1,0:T(8,128)(2,1)S(1)}, bf16[16,2048]{1,0:T(8,128)(2,1)S(1)}, u32[]{:S(2)}, u32[]{:S(2)}) collective-permute-start(bf16[16,2048]{1,0:T(8,128)(2,1)S(1)} %add_convert_fusion.2), channel_id=1, source_target_pairs={{0,2},{1,3},{2,0},{3,1},{4,6},{5,7},{6,4},{7,5},{8,10},{9,11},{10,... | collective-permute-start | bytes 196616 | tf_op jit(solution)/shard_map/ppermute | solution.py:38
  22.6 7.6 %collective-permute-start.12 = (bf16[16,4096]{1,0:T(8,128)(2,1)S(1)}, bf16[16,4096]{1,0:T(8,128)(2,1)S(1)}, u32[]{:S(2)}, u32[]{:S(2)}) collective-permute-start(bf16[16,4096]{1,0:T(8,128)(2,1)S(1)} %add_convert_fusion.refs_2_), channel_id=1, source_target_pairs={{0,3},{1,2},{2,1},{3,0},{4,7},{5,6},{6,5},{7,4},{8,11},{9,10},{10,... | collective-permute-start | bytes 393224 | tf_op jit(solution)/shard_map/ppermute | solution.py:38
  25.3 4.9 %collective-permute-start.10 = (bf16[16,2048]{1,0:T(8,128)(2,1)S(1)}, bf16[16,2048]{1,0:T(8,128)(2,1)S(1)}, u32[]{:S(2)}, u32[]{:S(2)}) collective-permute-start(bf16[16,2048]{1,0:T(8,128)(2,1)S(1)} %add_convert_fusion.1.refs_0_), channel_id=1, source_target_pairs={{0,1},{1,0},{2,3},{3,2},{4,5},{5,4},{6,7},{7,6},{8,9},{9,8},{10,11... | collective-permute-start | bytes 196616 | tf_op jit(solution)/shard_map/ppermute | solution.py:38

commit v10 on v8

--- a/solution.py
+++ b/solution.py
@@ -251,15 +251,31 @@
 
 
 def final_kernel(layout, *refs):
-    out_ref = refs[-1]
+    *part_refs, out_hbm, sum_ref, sems = refs
+    copies = []
+
+    def send(ref, start):
+        copies.append(
+            pltpu.make_async_copy(ref, out_hbm.at[:, pl.ds(start, ref.shape[1])], sems.at[len(copies)])
+        )
+        copies[-1].start()
+
     at = 0
     for kind, far, start, width in layout:
         if kind == "split":
             for half in (1, 0):
-                out_ref[:, pl.ds(first_column(half, far, start, width // 2), width // 2)] = refs[at + 1 - half][...]
-        else:
-            out_ref[:, start : start + width] = add(refs[at][...], refs[at + 1][...])
+                send(part_refs[at + 1 - half], first_column(half, far, start, width // 2))
         at += 2
+    at = place = 0
+    for kind, far, start, width in layout:
+        if kind != "split":
+            piece = sum_ref.at[:, place : place + width]
+            piece[...] = add(part_refs[at][...], part_refs[at + 1][...])
+            send(piece, start)
+            place += width
+        at += 2
+    for copy in copies:
+        copy.wait()
 
 
 def summed_over_four(attended, sent, weight):
@@ -291,7 +307,11 @@
         functools.partial(final_kernel, layout),
         out_shape=jax.ShapeDtypeStruct((attended.shape[0], columns), jnp.bfloat16),
         in_specs=[VMEM_SPEC] * len(operands),
-        out_specs=VMEM_SPEC,
+        out_specs=HBM_SPEC,
+        scratch_shapes=[
+            pltpu.VMEM((attended.shape[0], sum(w for kind, _, _, w in layout if kind != "split")), jnp.bfloat16),
+            pltpu.SemaphoreType.DMA((2 * len(layout),)),
+        ],
         compiler_params=PARAMS,
     )(*operands)
 

time: 31.1 us -> 31.1 us (level)
  no operation moved by 1% of the time
where the time goes in v10:
time: 31.1 us; the launch traced here: 30.9 us
  starting transfers between devices  18.6 us (60%)
  waiting for transfers between devices  6.58 us (21%)
  Pallas kernels  5.58 us (18%)
    ppermute x5, starting transfers between devices, swapped(): return lax.ppermute(block, 'mp', [(i, i ^ step) for i in range(size)])  9.32 us
    ppermute x8, starting transfers between devices, shifted(): lax.ppermute(block, 'dp', [(i, (i + distance) % size) for i in range(size)])  9.26 us
    ppermute x5, waiting for transfers between devices, swapped(): return lax.ppermute(block, 'mp', [(i, i ^ step) for i in range(size)])  5.21 us
    pallas_call x1, Pallas kernels, local(): pl.pallas_call(functools.partial(own_kernel, local_heads), out_shape=part...  1.74 us
    ppermute x8, waiting for transfers between devices, shifted(): lax.ppermute(block, 'dp', [(i, (i + distance) % size) for i in range(size)])  1.37 us
    pallas_call x2, Pallas kernels, project(): pl.pallas_call(functools.partial(project_kernel, half, far, start), out_s...  1.02 us
    pallas_call x1, Pallas kernels, summed_over_four(): pl.pallas_call(functools.partial(final_kernel, layout), out_shape=jax.Sha...  0.75 us
    pallas_call x1, Pallas kernels, local(): pl.pallas_call(functools.partial(gather_kernel, local_heads), out_shape=(...  0.67 us
  transfers between devices with their start and end apart: 13, of which 6 were waited for; matrix products, arithmetic and copies ran while one was open for 0% of the time, Pallas kernels for 14%

profile of v10, /device:TPU:0, one launch (start us, length us, event | category | flops | bytes accessed | tf_op | source)
XLA Modules:
  0.0 30.9 jit_solution(13523360230533608907)
XLA Ops:
  0.0 0.0 copy-start.2
  0.0 0.0 copy-start
  0.0 3.0 %collective-permute-start.2 = (bf16[16,512]{1,0:T(8,128)(2,1)}, bf16[16,512]{1,0:T(8,128)(2,1)S(1)}, u32[]{:S(2)}, u32[]{:S(2)}) collective-permute-start(bf16[16,512]{1,0:T(8,128)(2,1)} %query_ref.1), channel_id=1, source_target_pairs={{0,16},{4,20},{8,24},{12,28},{16,0},{20,4},{24,8},{28,12},{1,17},{... | collective-permute-start | bytes 49160 | tf_op jit(solution)/shard_map/ppermute | solution.py:33
  3.0 1.4 %collective-permute-start.1 = (bf16[16,512]{1,0:T(8,128)(2,1)}, bf16[16,512]{1,0:T(8,128)(2,1)S(1)}, u32[]{:S(2)}, u32[]{:S(2)}) collective-permute-start(bf16[16,512]{1,0:T(8,128)(2,1)} %query_ref.1), channel_id=1, source_target_pairs={{0,24},{4,28},{8,0},{12,4},{16,8},{20,12},{24,16},{28,20},{1,25},{... | collective-permute-start | bytes 49160 | tf_op jit(solution)/shard_map/ppermute | solution.py:33
  4.4 0.0 collective-permute-start
  4.4 0.0 copy-done.2
  4.5 0.0 copy-done
  4.5 0.7 %shard_map.56 = (bf16[4,256,128]{2,1,0:T(8,128)(2,1)S(1)}, bf16[4,256,128]{2,1,0:T(8,128)(2,1)S(1)}, f32[4,8,256]{2,1,0:T(8,128)S(1)}, bf16[528,128]{1,0:T(8,128)(2,1)S(1)}, bf16[528,128]{1,0:T(8,128)(2,1)S(1)}) custom-call(f32[64,768]{1,0:T(8,128)S(1)} %shard_map.55.after_ref.mask_ref, s32[6]{0:T(128)S(1)} %copy-done.2, bf16[6,2,2,128,128]{4,3,2,1,0:T(8,128)(2,1)S(1)} %copy-done), custom_call_target="tpu_custom_call" | custom-call | flops 8800000000 | bytes 29520000 | tf_op jit(solution)/shard_map/pallas_call | solution.py:341
  5.1 0.8 %collective-permute-start.3 = (bf16[528,128]{1,0:T(8,128)(2,1)S(1)}, bf16[528,128]{1,0:T(8,128)(2,1)S(1)}, u32[]{:S(2)}, u32[]{:S(2)}) collective-permute-start(bf16[528,128]{1,0:T(8,128)(2,1)S(1)} %get-tuple-element.28), channel_id=1, source_target_pairs={{0,12},{4,16},{8,20},{12,24},{16,28},{20,0},{24,4},{28,8},{1,13},{... | collective-permute-start | bytes 405512 | tf_op jit(solution)/shard_map/ppermute | solution.py:33
  5.9 1.0 %collective-permute-start.4 = (bf16[528,128]{1,0:T(8,128)(2,1)S(1)}, bf16[528,128]{1,0:T(8,128)(2,1)S(1)}, u32[]{:S(2)}, u32[]{:S(2)}) collective-permute-start(bf16[528,128]{1,0:T(8,128)(2,1)S(1)} %get-tuple-element.29), channel_id=1, source_target_pairs={{0,20},{4,24},{8,28},{12,0},{16,4},{20,8},{24,12},{28,16},{1,21},{... | collective-permute-start | bytes 405512 | tf_op jit(solution)/shard_map/ppermute | solution.py:33
  6.9 0.0 collective-permute-done.2.refs_2_
  6.9 0.0 collective-permute-done.1.refs_1_
  6.9 0.0 collective-permute-done.refs_0_
  7.0 0.4 %shard_map.57 = (bf16[80,128]{1,0:T(8,128)(2,1)S(1)}, bf16[80,128]{1,0:T(8,128)(2,1)S(1)}, bf16[80,128]{1,0:T(8,128)(2,1)S(1)}) custom-call(bf16[4,256,128]{2,1,0:T(8,128)(2,1)S(1)} %get-tuple-element.21.key_ref, bf16[4,256,128]{2,1,0:T(8,128)(2,1)S(1)} %get-tuple-element.22.value_ref, f32[4,8,256]{2,1,0:T(8,128)S(1)} %get-tuple-element.23.bias_ref, ...), custom_call_target="tpu_custom_call" | custom-call | flops 440000000 | bytes 1476000 | tf_op jit(solution)/shard_map/pallas_call | solution.py:351
  7.4 1.5 %collective-permute-start.5 = (bf16[80,128]{1,0:T(8,128)(2,1)S(1)}, bf16[80,128]{1,0:T(8,128)(2,1)S(1)}, u32[]{:S(2)}, u32[]{:S(2)}) collective-permute-start(bf16[80,128]{1,0:T(8,128)(2,1)S(1)} %get-tuple-element.33), channel_id=1, source_target_pairs={{0,4},{4,8},{8,12},{12,16},{16,20},{20,24},{24,28},{28,0},{1,5},{5... | collective-permute-start | bytes 61448 | tf_op jit(solution)/shard_map/ppermute | solution.py:33
  8.8 1.1 %collective-permute-start.6 = (bf16[80,128]{1,0:T(8,128)(2,1)S(1)}, bf16[80,128]{1,0:T(8,128)(2,1)S(1)}, u32[]{:S(2)}, u32[]{:S(2)}) collective-permute-start(bf16[80,128]{1,0:T(8,128)(2,1)S(1)} %get-tuple-element.34), channel_id=1, source_target_pairs={{0,8},{4,12},{8,16},{12,20},{16,24},{20,28},{24,0},{28,4},{1,9},{5... | collective-permute-start | bytes 61448 | tf_op jit(solution)/shard_map/ppermute | solution.py:33
  10.0 0.0 slice-start
  10.0 0.0 copy-start.1
  10.0 0.0 slice-start.1
  10.0 0.5 %collective-permute-start.7 = (bf16[80,128]{1,0:T(8,128)(2,1)S(1)}, bf16[80,128]{1,0:T(8,128)(2,1)S(1)}, u32[]{:S(2)}, u32[]{:S(2)}) collective-permute-start(bf16[80,128]{1,0:T(8,128)(2,1)S(1)} %get-tuple-element.24.after_ref), channel_id=1, source_target_pairs={{0,16},{4,20},{8,24},{12,28},{16,0},{20,4},{24,8},{28,12},{1,17},{... | collective-permute-start | bytes 61448 | tf_op jit(solution)/shard_map/ppermute | solution.py:33
  10.4 1.7 %shard_map.58 = (f32[64,128]{1,0:T(8,128)S(1)}, f32[64,128]{1,0:T(8,128)S(1)}, f32[64,128]{1,0:T(8,128)S(1)}) custom-call(bf16[4,256,128]{2,1,0:T(8,128)(2,1)S(1)} %get-tuple-element.21.key_ref, bf16[4,256,128]{2,1,0:T(8,128)(2,1)S(1)} %get-tuple-element.22.value_ref, f32[4,8,256]{2,1,0:T(8,128)S(1)} %get-tuple-element.23.bias_ref, ...), custom_call_target="tpu_custom_call" | custom-call | flops 1760000000 | bytes 5904000 | tf_op jit(solution)/shard_map/pallas_call | solution.py:360
  12.2 0.0 collective-permute-done.3.refs_0_
  12.2 0.1 collective-permute-done.4.refs_1_
  12.3 0.0 copy-done.1
  12.3 0.4 %shard_map.59 = (f32[64,128]{1,0:T(8,128)S(1)}, f32[64,128]{1,0:T(8,128)S(1)}, f32[64,128]{1,0:T(8,128)S(1)}) custom-call(f32[64,128]{1,0:T(8,128)S(1)} %get-tuple-element.25.after_ref.refs_0_, bf16[16,512]{1,0:T(8,128)(2,1)S(1)} %copy-done.1, bf16[528,128]{1,0:T(8,128)(2,1)S(1)} %collective-permute-done.3.refs_0_, ...), custom_call_target="tpu_custom_call" | custom-call | flops 550000000 | bytes 1845000 | tf_op jit(solution)/shard_map/pallas_call | solution.py:373
  12.7 0.0 collective-permute-done.5.refs_6_
  12.7 0.9 %collective-permute-done.6.refs_7_ = bf16[80,128]{1,0:T(8,128)(2,1)S(1)} collective-permute-done((bf16[80,128]{1,0:T(8,128)(2,1)S(1)}, bf16[80,128]{1,0:T(8,128)(2,1)S(1)}, u32[]{:S(2)}, u32[]{:S(2)}) %collective-permute-start.6) | collective-permute-done | bytes 20512 | tf_op jit(solution)/shard_map/ppermute | solution.py:33
  13.5 0.4 %collective-permute-done.7.refs_8_ = bf16[80,128]{1,0:T(8,128)(2,1)S(1)} collective-permute-done((bf16[80,128]{1,0:T(8,128)(2,1)S(1)}, bf16[80,128]{1,0:T(8,128)(2,1)S(1)}, u32[]{:S(2)}, u32[]{:S(2)}) %collective-permute-start.7) | collective-permute-done | bytes 20512 | tf_op jit(solution)/shard_map/ppermute | solution.py:33
  14.0 0.0 slice-done
  14.0 0.0 slice-done.1
  14.0 0.6 %shard_map.60 = (bf16[16,512]{1,0:T(8,128)(2,1)S(1)}, bf16[16,2048]{1,0:T(8,128)(2,1)S(1)}) custom-call(f32[64,128]{1,0:T(8,128)S(1)} %get-tuple-element.25.after_ref.refs_0_, f32[64,128]{1,0:T(8,128)S(1)} %get-tuple-element.26.refs_1_, f32[64,128]{1,0:T(8,128)S(1)} %get-tuple-element.27.refs_2_, f32[64,128]{1,0:T(8,128)S(1)} %get-tuple-element.30.refs_3_, ...), custom_call_target="tpu_custom_call" | custom-call | flops 220000000 | bytes 738000 | tf_op jit(solution)/shard_map/pallas_call | solution.py:386
  14.5 1.6 %collective-permute-start.8 = (bf16[16,2048]{1,0:T(8,128)(2,1)S(1)}, bf16[16,2048]{1,0:T(8,128)(2,1)S(1)}, u32[]{:S(2)}, u32[]{:S(2)}) collective-permute-start(bf16[16,2048]{1,0:T(8,128)(2,1)S(1)} %get-tuple-element.36), channel_id=1, source_target_pairs={{0,1},{1,0},{2,3},{3,2},{4,5},{5,4},{6,7},{7,6},{8,9},{9,8},{10,11... | collective-permute-start | bytes 196616 | tf_op jit(solution)/shard_map/ppermute | solution.py:38
  16.1 0.6 %shard_map.62 = bf16[16,4096]{1,0:T(8,128)(2,1)S(1)} custom-call(bf16[16,512]{1,0:T(8,128)(2,1)S(1)} %get-tuple-element.35.attended_ref, bf16[512,8192]{1,0:T(8,128)(2,1)S(1)} %bitcast.1), custom_call_target="tpu_custom_call" | custom-call | flops 67108864 | bytes 4194304 | tf_op jit(solution)/shard_map/pallas_call | solution.py:237
  16.8 0.5 %collective-permute-start.11 = (bf16[16,4096]{1,0:T(8,128)(2,1)S(1)}, bf16[16,4096]{1,0:T(8,128)(2,1)S(1)}, u32[]{:S(2)}, u32[]{:S(2)}) collective-permute-start(bf16[16,4096]{1,0:T(8,128)(2,1)S(1)} %shard_map.62), channel_id=1, source_target_pairs={{0,1},{1,0},{2,3},{3,2},{4,5},{5,4},{6,7},{7,6},{8,9},{9,8},{10,11... | collective-permute-start | bytes 393224 | tf_op jit(solution)/shard_map/ppermute | solution.py:38
  17.2 0.4 %shard_map.61 = bf16[16,2048]{1,0:T(8,128)(2,1)S(1)} custom-call(bf16[16,512]{1,0:T(8,128)(2,1)S(1)} %get-tuple-element.35.attended_ref, bf16[512,8192]{1,0:T(8,128)(2,1)S(1)} %bitcast.1), custom_call_target="tpu_custom_call" | custom-call | flops 33554432 | bytes 2097152 | tf_op jit(solution)/shard_map/pallas_call | solution.py:237
  17.6 1.2 %collective-permute-done.8 = bf16[16,2048]{1,0:T(8,128)(2,1)S(1)} collective-permute-done((bf16[16,2048]{1,0:T(8,128)(2,1)S(1)}, bf16[16,2048]{1,0:T(8,128)(2,1)S(1)}, u32[]{:S(2)}, u32[]{:S(2)}) %collective-permute-start.8) | collective-permute-done | bytes 65568 | tf_op jit(solution)/shard_map/ppermute | solution.py:38
  18.8 2.7 %collective-permute-start.9 = (bf16[16,2048]{1,0:T(8,128)(2,1)S(1)}, bf16[16,2048]{1,0:T(8,128)(2,1)S(1)}, u32[]{:S(2)}, u32[]{:S(2)}) collective-permute-start(bf16[16,2048]{1,0:T(8,128)(2,1)S(1)} %add_convert_fusion.2), channel_id=1, source_target_pairs={{0,2},{1,3},{2,0},{3,1},{4,6},{5,7},{6,4},{7,5},{8,10},{9,11},{10,... | collective-permute-start | bytes 196616 | tf_op jit(solution)/shard_map/ppermute | solution.py:38
  21.5 1.0 %collective-permute-done.11 = bf16[16,4096]{1,0:T(8,128)(2,1)S(1)} collective-permute-done((bf16[16,4096]{1,0:T(8,128)(2,1)S(1)}, bf16[16,4096]{1,0:T(8,128)(2,1)S(1)}, u32[]{:S(2)}, u32[]{:S(2)}) %collective-permute-start.11) | collective-permute-done | bytes 131104 | tf_op jit(solution)/shard_map/ppermute | solution.py:38
  22.5 2.7 %collective-permute-start.12 = (bf16[16,4096]{1,0:T(8,128)(2,1)S(1)}, bf16[16,4096]{1,0:T(8,128)(2,1)S(1)}, u32[]{:S(2)}, u32[]{:S(2)}) collective-permute-start(bf16[16,4096]{1,0:T(8,128)(2,1)S(1)} %add_convert_fusion.refs_2_), channel_id=1, source_target_pairs={{0,3},{1,2},{2,1},{3,0},{4,7},{5,6},{6,5},{7,4},{8,11},{9,10},{10,... | collective-permute-start | bytes 393224 | tf_op jit(solution)/shard_map/ppermute | solution.py:38
  25.2 0.0 collective-permute-done.9
  25.2 1.9 %collective-permute-start.10 = (bf16[16,2048]{1,0:T(8,128)(2,1)S(1)}, bf16[16,2048]{1,0:T(8,128)(2,1)S(1)}, u32[]{:S(2)}, u32[]{:S(2)}) collective-permute-start(bf16[16,2048]{1,0:T(8,128)(2,1)S(1)} %add_convert_fusion.1.refs_0_), channel_id=1, source_target_pairs={{0,1},{1,0},{2,3},{3,2},{4,5},{5,4},{6,7},{7,6},{8,9},{9,8},{10,11... | collective-permute-start | bytes 196616 | tf_op jit(solution)/shard_map/ppermute | solution.py:38
  27.2 3.0 %collective-permute-done.10.refs_1_ = bf16[16,2048]{1,0:T(8,128)(2,1)S(1)} collective-permute-done((bf16[16,2048]{1,0:T(8,128)(2,1)S(1)}, bf16[16,2048]{1,0:T(8,128)(2,1)S(1)}, u32[]{:S(2)}, u32[]{:S(2)}) %collective-permute-start.10) | collective-permute-done | bytes 65568 | tf_op jit(solution)/shard_map/ppermute | solution.py:38
  30.2 0.0 collective-permute-done.12.refs_3_
  30.2 0.7 %shard_map.63 = bf16[16,8192]{1,0:T(8,128)(2,1)} custom-call(bf16[16,2048]{1,0:T(8,128)(2,1)S(1)} %add_convert_fusion.1.refs_0_, bf16[16,2048]{1,0:T(8,128)(2,1)S(1)} %collective-permute-done.10.refs_1_, bf16[16,4096]{1,0:T(8,128)(2,1)S(1)} %add_convert_fusion.refs_2_, bf16[16,4096]{1,0:T(8,128)(2,1)S(1)} %collective-permute-done.12.refs_3_), custom_call_target="tpu_custom_call" | custom-call | tf_op jit(solution)/shard_map/pallas_call | solution.py:306
  (5 shorter events, 0.1 us)
Async XLA Ops:
  0.0 4.5 %copy-start.2 = (s32[6]{0:T(128)S(1)}, s32[6]{0:T(128)}, u32[]{:S(2)}) copy-start(s32[6]{0:T(128)} %offset_ref.1) | copy-start | bytes 76
  0.0 4.5 %copy-start = (bf16[6,2,2,128,128]{4,3,2,1,0:T(8,128)(2,1)S(1)}, bf16[6,2,2,128,128]{4,3,2,1,0:T(8,128)(2,1)}, u32[]{:S(2)}) copy-start(bf16[6,2,2,128,128]{4,3,2,1,0:T(8,128)(2,1)} %pool_ref.1) | copy-start | bytes 2359300
  0.0 6.9 %collective-permute-start.2 = (bf16[16,512]{1,0:T(8,128)(2,1)}, bf16[16,512]{1,0:T(8,128)(2,1)S(1)}, u32[]{:S(2)}, u32[]{:S(2)}) collective-permute-start(bf16[16,512]{1,0:T(8,128)(2,1)} %query_ref.1), channel_id=1, source_target_pairs={{0,16},{4,20},{8,24},{12,28},{16,0},{20,4},{24,8},{28,12},{1,17},{... | collective-permute-start | bytes 49160 | tf_op jit(solution)/shard_map/ppermute | solution.py:33
  3.0 4.0 %collective-permute-start.1 = (bf16[16,512]{1,0:T(8,128)(2,1)}, bf16[16,512]{1,0:T(8,128)(2,1)S(1)}, u32[]{:S(2)}, u32[]{:S(2)}) collective-permute-start(bf16[16,512]{1,0:T(8,128)(2,1)} %query_ref.1), channel_id=1, source_target_pairs={{0,24},{4,28},{8,0},{12,4},{16,8},{20,12},{24,16},{28,20},{1,25},{... | collective-permute-start | bytes 49160 | tf_op jit(solution)/shard_map/ppermute | solution.py:33
  4.4 2.5 %collective-permute-start = (bf16[16,512]{1,0:T(8,128)(2,1)}, bf16[16,512]{1,0:T(8,128)(2,1)S(1)}, u32[]{:S(2)}, u32[]{:S(2)}) collective-permute-start(bf16[16,512]{1,0:T(8,128)(2,1)} %query_ref.1), channel_id=1, source_target_pairs={{0,28},{4,0},{8,4},{12,8},{16,12},{20,16},{24,20},{28,24},{1,29},{... | collective-permute-start | bytes 49160 | tf_op jit(solution)/shard_map/ppermute | solution.py:33
  5.1 7.0 %collective-permute-start.3 = (bf16[528,128]{1,0:T(8,128)(2,1)S(1)}, bf16[528,128]{1,0:T(8,128)(2,1)S(1)}, u32[]{:S(2)}, u32[]{:S(2)}) collective-permute-start(bf16[528,128]{1,0:T(8,128)(2,1)S(1)} %get-tuple-element.28), channel_id=1, source_target_pairs={{0,12},{4,16},{8,20},{12,24},{16,28},{20,0},{24,4},{28,8},{1,13},{... | collective-permute-start | bytes 405512 | tf_op jit(solution)/shard_map/ppermute | solution.py:33
  5.9 6.4 %collective-permute-start.4 = (bf16[528,128]{1,0:T(8,128)(2,1)S(1)}, bf16[528,128]{1,0:T(8,128)(2,1)S(1)}, u32[]{:S(2)}, u32[]{:S(2)}) collective-permute-start(bf16[528,128]{1,0:T(8,128)(2,1)S(1)} %get-tuple-element.29), channel_id=1, source_target_pairs={{0,20},{4,24},{8,28},{12,0},{16,4},{20,8},{24,12},{28,16},{1,21},{... | collective-permute-start | bytes 405512 | tf_op jit(solution)/shard_map/ppermute | solution.py:33
  7.4 5.3 %collective-permute-start.5 = (bf16[80,128]{1,0:T(8,128)(2,1)S(1)}, bf16[80,128]{1,0:T(8,128)(2,1)S(1)}, u32[]{:S(2)}, u32[]{:S(2)}) collective-permute-start(bf16[80,128]{1,0:T(8,128)(2,1)S(1)} %get-tuple-element.33), channel_id=1, source_target_pairs={{0,4},{4,8},{8,12},{12,16},{16,20},{20,24},{24,28},{28,0},{1,5},{5... | collective-permute-start | bytes 61448 | tf_op jit(solution)/shard_map/ppermute | solution.py:33
  8.8 4.7 %collective-permute-start.6 = (bf16[80,128]{1,0:T(8,128)(2,1)S(1)}, bf16[80,128]{1,0:T(8,128)(2,1)S(1)}, u32[]{:S(2)}, u32[]{:S(2)}) collective-permute-start(bf16[80,128]{1,0:T(8,128)(2,1)S(1)} %get-tuple-element.34), channel_id=1, source_target_pairs={{0,8},{4,12},{8,16},{12,20},{16,24},{20,28},{24,0},{28,4},{1,9},{5... | collective-permute-start | bytes 61448 | tf_op jit(solution)/shard_map/ppermute | solution.py:33
  10.0 4.0 %slice-start = ((s8[8388608]{0:T(1024)(128)(4,1)}), s8[4194304]{0:T(1024)(128)(4,1)S(1)}, s32[]{:S(2)}) async-start(s8[8388608]{0:T(1024)(128)(4,1)} %bitcast), calls=%async_computation | async-start | bytes 8388608
  10.0 2.3 %copy-start.1 = (bf16[16,512]{1,0:T(8,128)(2,1)S(1)}, bf16[16,512]{1,0:T(8,128)(2,1)}, u32[]{:S(2)}) copy-start(bf16[16,512]{1,0:T(8,128)(2,1)} %query_ref.1) | copy-start | bytes 49156
  10.0 4.0 %slice-start.1 = ((s8[8388608]{0:T(1024)(128)(4,1)}), s8[4194304]{0:T(1024)(128)(4,1)S(1)}, s32[]{:S(2)}) async-start(s8[8388608]{0:T(1024)(128)(4,1)} %bitcast), calls=%async_computation.1 | async-start | bytes 8388608
  10.0 4.0 %collective-permute-start.7 = (bf16[80,128]{1,0:T(8,128)(2,1)S(1)}, bf16[80,128]{1,0:T(8,128)(2,1)S(1)}, u32[]{:S(2)}, u32[]{:S(2)}) collective-permute-start(bf16[80,128]{1,0:T(8,128)(2,1)S(1)} %get-tuple-element.24.after_ref), channel_id=1, source_target_pairs={{0,16},{4,20},{8,24},{12,28},{16,0},{20,4},{24,8},{28,12},{1,17},{... | collective-permute-start | bytes 61448 | tf_op jit(solution)/shard_map/ppermute | solution.py:33
  14.5 4.3 %collective-permute-start.8 = (bf16[16,2048]{1,0:T(8,128)(2,1)S(1)}, bf16[16,2048]{1,0:T(8,128)(2,1)S(1)}, u32[]{:S(2)}, u32[]{:S(2)}) collective-permute-start(bf16[16,2048]{1,0:T(8,128)(2,1)S(1)} %get-tuple-element.36), channel_id=1, source_target_pairs={{0,1},{1,0},{2,3},{3,2},{4,5},{5,4},{6,7},{7,6},{8,9},{9,8},{10,11... | collective-permute-start | bytes 196616 | tf_op jit(solution)/shard_map/ppermute | solution.py:38
  16.8 5.7 %collective-permute-start.11 = (bf16[16,4096]{1,0:T(8,128)(2,1)S(1)}, bf16[16,4096]{1,0:T(8,128)(2,1)S(1)}, u32[]{:S(2)}, u32[]{:S(2)}) collective-permute-start(bf16[16,4096]{1,0:T(8,128)(2,1)S(1)} %shard_map.62), channel_id=1, source_target_pairs={{0,1},{1,0},{2,3},{3,2},{4,5},{5,4},{6,7},{7,6},{8,9},{9,8},{10,11... | collective-permute-start | bytes 393224 | tf_op jit(solution)/shard_map/ppermute | solution.py:38
  18.8 6.4 %collective-permute-start.9 = (bf16[16,2048]{1,0:T(8,128)(2,1)S(1)}, bf16[16,2048]{1,0:T(8,128)(2,1)S(1)}, u32[]{:S(2)}, u32[]{:S(2)}) collective-permute-start(bf16[16,2048]{1,0:T(8,128)(2,1)S(1)} %add_convert_fusion.2), channel_id=1, source_target_pairs={{0,2},{1,3},{2,0},{3,1},{4,6},{5,7},{6,4},{7,5},{8,10},{9,11},{10,... | collective-permute-start | bytes 196616 | tf_op jit(solution)/shard_map/ppermute | solution.py:38
  22.5 7.6 %collective-permute-start.12 = (bf16[16,4096]{1,0:T(8,128)(2,1)S(1)}, bf16[16,4096]{1,0:T(8,128)(2,1)S(1)}, u32[]{:S(2)}, u32[]{:S(2)}) collective-permute-start(bf16[16,4096]{1,0:T(8,128)(2,1)S(1)} %add_convert_fusion.refs_2_), channel_id=1, source_target_pairs={{0,3},{1,2},{2,1},{3,0},{4,7},{5,6},{6,5},{7,4},{8,11},{9,10},{10,... | collective-permute-start | bytes 393224 | tf_op jit(solution)/shard_map/ppermute | solution.py:38
  25.2 4.9 %collective-permute-start.10 = (bf16[16,2048]{1,0:T(8,128)(2,1)S(1)}, bf16[16,2048]{1,0:T(8,128)(2,1)S(1)}, u32[]{:S(2)}, u32[]{:S(2)}) collective-permute-start(bf16[16,2048]{1,0:T(8,128)(2,1)S(1)} %add_convert_fusion.1.refs_0_), channel_id=1, source_target_pairs={{0,1},{1,0},{2,3},{3,2},{4,5},{5,4},{6,7},{7,6},{8,9},{9,8},{10,11... | collective-permute-start | bytes 196616 | tf_op jit(solution)/shard_map/ppermute | solution.py:38
